TPU v7x, 512 devices: a whole 4x8x8 slice. The times are simulated.
512 devices in a mesh: serve: 64 (over y, z), head: 8 (over x, core).
Axes of the slice: x: 4, y: 8, z: 8, core: 2. Of those that a mesh axis runs over, the one named last changes fastest.
Arguments:
- pre_x: bfloat16 [16384, 4096], P(('serve', 'head')), may hold values from -6 to 6
- pre_z: bfloat16 [16384, 4096], P(('serve', 'head')), may hold values from -6 to 6
- pre_b: bfloat16 [16384, 1024], P(('serve', 'head')), may hold values from -0.59765625 to 0.59765625
- pre_c: bfloat16 [16384, 1024], P(('serve', 'head')), may hold values from -0.59765625 to 0.59765625
- pre_dt: bfloat16 [16384, 64], P(('serve', 'head')), may hold values from -3 to 3
- suffix_lengths: int32 [64, 3], P('serve'), may hold values from 1 to 128, 256 in all within a row
- prefix_hits: int32 [192], replicated, may hold values from 0 to 255
- snapshot_slots: int32 [192], replicated, may hold values from 0 to 255, as said below
- cache_states: float32 [256, 64, 64, 128], P('serve', 'head'), may hold values from -6 to 6
- dec_x: bfloat16 [128, 4096], P('serve', 'head'), may hold values from -6 to 6
- dec_z: bfloat16 [128, 4096], P('serve', 'head'), may hold values from -6 to 6
- dec_b: bfloat16 [128, 1024], P('serve', 'head'), may hold values from -0.59765625 to 0.59765625
- dec_c: bfloat16 [128, 1024], P('serve', 'head'), may hold values from -0.59765625 to 0.59765625
- dec_dt: bfloat16 [128, 64], P('serve', 'head'), may hold values from -3 to 3
- dec_states: float32 [128, 64, 64, 128], P('serve', 'head'), may hold values from -6 to 6
- decay_rate: float32 [64], P('head'), may hold values from 0.001 to 0.04
- d_skip: float32 [64], P('head'), may hold values from 0.5 to 2
- norm_weight: float32 [4096], P('head'), may hold values from 0.5 to 1.5
Outputs:
- pre_out: bfloat16 [16384, 4096], P('serve', 'head')
- cache_out: float32 [256, 64, 64, 128], P('serve', 'head')
- dec_out: bfloat16 [128, 4096], P('serve', 'head')
- dec_new: float32 [128, 64, 64, 128], P('serve', 'head')
Inputs may be any that keep to these rules, and one draw needn't show every extreme that they name: `snapshot_slots`: entries are distinct; each holder's block of 4 slots is named by exactly 3 entries. `prefix_hits`: entry r belongs to the (r mod 3)-th suffix of serving device r // 3.
All inputs are finite; a program needn't handle non-finite values.
Results may differ from a plain program's by a relative error of at most 0.0055.
Values may be sent and summed in bfloat16 or wider, within the bound.
No kernel may reach another device: no remote copies, remote signals or barrier semaphores. Data moves between devices by JAX's collectives and lax.ppermute only.
A program may use at most 64 MiB of HBM per device.

v0:
```python
import jax
import jax.numpy as jnp
from jax import lax
from jax.sharding import PartitionSpec as P

HEAD_DIM = 64
STATE = 128


highest = lax.Precision.HIGHEST


def gated_norm(values, gate_in, norm_weight):
    shaped = values.shape
    gated = values * jax.nn.silu(gate_in.astype(jnp.float32).reshape(shaped))
    square_mean = jnp.mean(gated * gated, axis=(2, 3), keepdims=True)
    normed = gated * lax.rsqrt(square_mean + 1e-05) * norm_weight.reshape(shaped[1:])
    return normed.reshape(shaped[0], -1).astype(jnp.bfloat16)


def segment_block(
    inputs, gate_in, b_proj, c_proj, step_raw, lengths, initial, head_rates, skip_gain, norm_weight
):
    length = inputs.shape[0]
    head_count = step_raw.shape[1]
    groups = b_proj.shape[1] // STATE
    per_group = head_count // groups
    seg_ends = jnp.cumsum(lengths)
    starts = seg_ends - lengths
    position = jnp.arange(length, dtype=jnp.int32)
    seg_index = jnp.sum((position[:, None] >= seg_ends[None, :]).astype(jnp.int32), axis=1)
    member = (seg_index[:, None] == jnp.arange(lengths.shape[0], dtype=jnp.int32)[None, :]).astype(
        jnp.float32
    )
    step_size = jax.nn.softplus(step_raw.astype(jnp.float32))
    log_decay = -step_size * head_rates[None, :]
    running = jnp.cumsum(log_decay, axis=0)
    before = running - log_decay
    seg_base = jnp.take(before, starts, axis=0)
    seg_end = jnp.take(running, seg_ends - 1, axis=0)
    tok_base = jnp.take(seg_base, seg_index, axis=0)
    tok_end = jnp.take(seg_end, seg_index, axis=0)
    allowed = (seg_index[:, None] == seg_index[None, :]) & (position[:, None] >= position[None, :])
    running_t = running.T
    decay_mat = jnp.exp(
        jnp.where(allowed[None], running_t[:, :, None] - running_t[:, None, :], -jnp.inf)
    )
    b_half = b_proj.reshape(length, groups, STATE)
    c_half = c_proj.reshape(length, groups, STATE)
    scores = jnp.einsum("tgn,sgn->gts", c_half, b_half, preferred_element_type=jnp.float32)
    weights = (
        decay_mat.reshape(groups, per_group, length, length)
        * scores[:, None]
        * step_size.T.reshape(groups, per_group, 1, length)
    )
    values = inputs.astype(jnp.float32).reshape(length, groups, per_group, HEAD_DIM)
    inner_out = jnp.einsum("gkts,sgkp->tgkp", weights, values, precision=highest)
    b_group = b_half.astype(jnp.float32)
    c_group = c_half.astype(jnp.float32)
    start_states = initial.reshape(-1, groups, per_group, HEAD_DIM, STATE)
    readout = jnp.einsum("tgn,jgkpn->tjgkp", c_group, start_states, precision=highest)
    carried = jnp.einsum("tj,tjgkp->tgkp", member, readout, precision=highest)
    carried = carried * jnp.exp(running - tok_base).reshape(length, groups, per_group, 1)
    outputs = inner_out + carried + skip_gain.reshape(groups, per_group, 1) * values
    result = gated_norm(outputs, gate_in, norm_weight)
    to_end = (jnp.exp(tok_end - running) * step_size).reshape(length, groups, per_group, 1) * values
    spread = member[:, :, None, None, None] * to_end[:, None]
    local_state = jnp.einsum("tjgkp,tgn->jgkpn", spread, b_group, precision=highest)
    kept_part = jnp.exp(seg_end - seg_base).reshape(-1, groups, per_group, 1, 1) * start_states
    finals = (kept_part + local_state).reshape(-1, head_count, HEAD_DIM, STATE)
    return (result, finals)


def decode_block(
    inputs, gate_in, b_proj, c_proj, step_raw, states, head_rates, skip_gain, norm_weight
):
    row_count = inputs.shape[0]
    head_count = step_raw.shape[1]
    groups = b_proj.shape[1] // STATE
    per_group = head_count // groups
    step_size = jax.nn.softplus(step_raw.astype(jnp.float32))
    factor = jnp.exp(-step_size * head_rates[None, :]).reshape(row_count, groups, per_group, 1, 1)
    values = inputs.astype(jnp.float32).reshape(row_count, groups, per_group, HEAD_DIM)
    b_group = b_proj.astype(jnp.float32).reshape(row_count, groups, STATE)
    c_group = c_proj.astype(jnp.float32).reshape(row_count, groups, STATE)
    written = (step_size.reshape(row_count, groups, per_group, 1) * values)[..., None] * b_group[
        :, :, None, None, :
    ]
    updated = factor * states.reshape(row_count, groups, per_group, HEAD_DIM, STATE) + written
    outputs = (
        jnp.einsum("rgkpn,rgn->rgkp", updated, c_group, precision=highest)
        + skip_gain.reshape(groups, per_group, 1) * values
    )
    return (
        gated_norm(outputs, gate_in, norm_weight),
        updated.reshape(row_count, head_count, HEAD_DIM, STATE),
    )


def local(
    pre_x,
    pre_z,
    pre_b,
    pre_c,
    pre_dt,
    suffix_lengths,
    prefix_hits,
    snapshot_slots,
    cache_states,
    dec_x,
    dec_z,
    dec_b,
    dec_c,
    dec_dt,
    dec_states,
    decay_rate,
    d_skip,
    norm_weight,
):
    x_cols, z_cols, b_cols, c_cols, dt_cols = (
        lax.all_to_all(pre_x, "head", split_axis=1, concat_axis=0, tiled=True),
        lax.all_to_all(pre_z, "head", split_axis=1, concat_axis=0, tiled=True),
        lax.all_to_all(pre_b, "head", split_axis=1, concat_axis=0, tiled=True),
        lax.all_to_all(pre_c, "head", split_axis=1, concat_axis=0, tiled=True),
        lax.all_to_all(pre_dt, "head", split_axis=1, concat_axis=0, tiled=True),
    )
    slots_dev = cache_states.shape[0]
    heads_dev = cache_states.shape[1]
    state_rows = cache_states.reshape(slots_dev, heads_dev, HEAD_DIM * STATE)
    pieces = lax.all_to_all(state_rows, "serve", split_axis=2, concat_axis=0, tiled=True)
    wanted = jnp.take(pieces, prefix_hits, axis=0)
    prefix = lax.all_to_all(wanted, "serve", split_axis=0, concat_axis=2, tiled=True)
    initial = prefix.reshape(prefix.shape[0], heads_dev, HEAD_DIM, STATE)
    dec_out, dec_new = decode_block(
        dec_x, dec_z, dec_b, dec_c, dec_dt, dec_states, decay_rate, d_skip, norm_weight
    )
    pre_out, finals = segment_block(
        x_cols,
        z_cols,
        b_cols,
        c_cols,
        dt_cols,
        suffix_lengths[0],
        initial,
        decay_rate,
        d_skip,
        norm_weight,
    )
    snap_pieces = lax.all_to_all(
        finals.reshape(finals.shape[0], heads_dev, HEAD_DIM * STATE).astype(jnp.bfloat16),
        "serve",
        split_axis=2,
        concat_axis=0,
        tiled=True,
    ).astype(jnp.float32)
    renewed = pieces.at[snapshot_slots].set(snap_pieces)
    returned = lax.all_to_all(renewed, "serve", split_axis=0, concat_axis=2, tiled=True)
    cache_out = returned.reshape(cache_states.shape)
    return (pre_out, cache_out, dec_out, dec_new)


def solution(mesh):
    return jax.shard_map(
        local,
        mesh=mesh,
        in_specs=(
            P(("serve", "head"), None),
            P(("serve", "head"), None),
            P(("serve", "head"), None),
            P(("serve", "head"), None),
            P(("serve", "head"), None),
            P("serve", None),
            P(),
            P(),
            P("serve", "head", None, None),
            P("serve", "head"),
            P("serve", "head"),
            P("serve", "head"),
            P("serve", "head"),
            P("serve", "head"),
            P("serve", "head", None, None),
            P("head"),
            P("head"),
            P("head"),
        ),
        out_specs=(
            P("serve", "head"),
            P("serve", "head", None, None),
            P("serve", "head"),
            P("serve", "head", None, None),
        ),
        check_vma=False,
    )
```

profile of v0, /device:TPU:18, one launch (start us, length us, event | category | flops | bytes accessed | tf_op | source)
XLA Modules:
  0.0 306.2 jit_solution(1626870179872891737)
XLA Ops:
  0.6 0.8 copy.120
  1.5 0.7 reshape.490
  2.2 4.8 %all-to-all-start = ((bf16[8,2,128]{2,1,0:T(2,128)(2,1)}), bf16[8,2,128]{2,1,0:T(2,128)(2,1)S(1)}, u32[]{:S(2)}, u32[]{:S(2)}) async-start(bf16[8,2,128]{2,1,0:T(2,128)(2,1)} %reshape.490), calls=%async_computation | async-start | bytes 8192 | tf_op jit(solution)/shard_map/all_to_all | solution.py:125
  7.0 0.8 reduce-window.18
  7.8 0.7 compare_and_fusion.2
  8.6 0.7 compare_and_fusion.3
  9.3 9.8 %copy.126 = f32[4,8,64,128]{1,0,3,2:T(4,128)} copy(f32[4,8,64,128]{3,2,1,0:T(8,128)} %param.30) | data formatting | bytes 2097152 | tf_op args[8]
  19.1 22.0 %reshape.492 = f32[64,1,4096]{2,1,0:T(1,128)} reshape(f32[8192,4,8]{2,1,0:T(4,128)} %bitcast.150) | data formatting | bytes 2097152
  41.1 16.6 %all-to-all-start.4 = ((f32[64,1,4096]{2,1,0:T(1,128)}), f32[64,1,4096]{2,1,0:T(1,128)S(1)}, u32[]{:S(2)}, u32[]{:S(2)}) async-start(f32[64,1,4096]{2,1,0:T(1,128)} %reshape.492), calls=%async_computation.4 | async-start | bytes 2097152 | tf_op jit(solution)/shard_map/all_to_all | solution.py:130
  57.8 0.7 copy.181
  58.8 0.2 multiply_add_fusion
  59.1 0.7 fusion.53
  59.8 0.2 multiply_reduce_fusion.1
  60.0 0.6 copy_bitcast_fusion.2
  60.6 27.8 %all-to-all-done.4 = f32[64,1,4096]{2,1,0:T(1,128)S(1)} async-done(((f32[64,1,4096]{2,1,0:T(1,128)}), f32[64,1,4096]{2,1,0:T(1,128)S(1)}, u32[]{:S(2)}, u32[]{:S(2)}) %all-to-all-start.4) | async-done | bytes 1048608 | tf_op jit(solution)/shard_map/all_to_all | solution.py:130
  88.4 4.8 %all-to-all-start.2 = ((bf16[32,8,128]{2,0,1:T(8,128)(2,1)}), bf16[32,8,128]{2,0,1:T(8,128)(2,1)S(1)}, u32[]{:S(2)}, u32[]{:S(2)}) async-start(bf16[32,8,128]{2,0,1:T(8,128)(2,1)} %copy_bitcast_fusion.2), calls=%async_computation.2 | async-start | bytes 131072 | tf_op jit(solution)/shard_map/all_to_all | solution.py:123
  93.2 0.5 broadcast.258
  93.7 3.3 %reduce.7 = f32[64,4096]{1,0:T(8,128)S(1)} reduce(f32[64,1,4096]{2,1,0:T(1,128)S(1)} %all-to-all-done.4, f32[]{:T(128)} %broadcast.258), dimensions={1}, to_apply=%all_to_all.109.reduce_sub_computation | reduce | bytes 2097156 | tf_op jit(solution)/shard_map/all_to_all | solution.py:130
  97.0 21.2 %reshape.493 = f32[8192,4,8]{2,1,0:T(4,128)} reshape(f32[64,4096]{1,0:T(8,128)S(1)} %reduce.7) | data formatting | bytes 2097152
  118.2 13.0 %copy.155 = f32[4,8,64,128]{3,1,0,2:T(8,128)} copy(f32[4,8,64,128]{1,0,3,2:T(4,128)} %bitcast.149) | data formatting | bytes 2097152 | tf_op jit(solution)/shard_map/all_to_all | solution.py:130
  131.2 1.9 gather_fusion
  133.2 4.8 %all-to-all-start.3 = ((bf16[32,8,512]{2,0,1:T(8,128)(2,1)}), bf16[32,8,512]{2,0,1:T(8,128)(2,1)S(1)}, u32[]{:S(2)}, u32[]{:S(2)}) async-start(bf16[32,8,512]{2,0,1:T(8,128)(2,1)} %bitcast.148), calls=%async_computation.3 | async-start | bytes 524288 | tf_op jit(solution)/shard_map/all_to_all | solution.py:121
  138.0 1.2 broadcast_select_fusion
  139.1 4.9 %all-to-all-done.3 = bf16[32,8,512]{2,0,1:T(8,128)(2,1)S(1)} async-done(((bf16[32,8,512]{2,0,1:T(8,128)(2,1)}), bf16[32,8,512]{2,0,1:T(8,128)(2,1)S(1)}, u32[]{:S(2)}, u32[]{:S(2)}) %all-to-all-start.3) | async-done | bytes 262176 | tf_op jit(solution)/shard_map/all_to_all | solution.py:121
  144.1 6.0 %all-to-all-start.5 = ((f32[192,8,128]{2,1,0:T(8,128)}), f32[192,8,128]{2,1,0:T(8,128)S(1)}, u32[]{:S(2)}, u32[]{:S(2)}) async-start(f32[192,8,128]{2,1,0:T(8,128)} %broadcast_select_fusion), calls=%async_computation.5 | async-start | bytes 1572864 | tf_op jit(solution)/shard_map/all_to_all | solution.py:132
  150.4 0.6 reduce-window.19
  151.5 0.6 gather_fusion.3
  152.1 0.6 gather_fusion.1
  152.7 0.7 gather_fusion.2
  153.5 0.7 gather_fusion.4
  154.3 0.6 fusion.44
  155.0 0.3 reshape.403
  155.3 0.3 convert_multiply_fusion
  155.7 0.4 copy.139
  156.0 18.7 %all-to-all-done.5 = f32[192,8,128]{2,1,0:T(8,128)S(1)} async-done(((f32[192,8,128]{2,1,0:T(8,128)}), f32[192,8,128]{2,1,0:T(8,128)S(1)}, u32[]{:S(2)}, u32[]{:S(2)}) %all-to-all-start.5) | async-done | bytes 786464 | tf_op jit(solution)/shard_map/all_to_all | solution.py:132
  174.7 0.9 fusion.15
  175.6 6.4 %copy.156 = bf16[3,1,8,64,128]{2,0,4,3,1:T(4,128)(2,1)} copy(bf16[3,1,8,64,128]{4,3,2,0,1:T(8,128)(2,1)S(1)} %fusion.15) | data formatting | bytes 786432 | tf_op jit(solution)/shard_map/convert_element_type | solution.py:150
  182.0 13.6 %reshape.494 = bf16[64,2,1536]{2,1,0:T(2,128)(2,1)} reshape(bf16[8192,3,8]{2,1,0:T(4,128)(2,1)} %bitcast.151) | data formatting | bytes 786432
  195.6 5.4 %all-to-all-start.7 = ((bf16[64,2,1536]{2,1,0:T(2,128)(2,1)}), bf16[64,2,1536]{2,1,0:T(2,128)(2,1)S(1)}, u32[]{:S(2)}, u32[]{:S(2)}) async-start(bf16[64,2,1536]{2,1,0:T(2,128)(2,1)} %reshape.494), calls=%async_computation.7 | async-start | bytes 786432 | tf_op jit(solution)/shard_map/all_to_all | solution.py:149
  201.3 0.6 copy_bitcast_fusion.3
  202.0 15.4 %all-to-all-done.7 = bf16[64,2,1536]{2,1,0:T(2,128)(2,1)S(1)} async-done(((bf16[64,2,1536]{2,1,0:T(2,128)(2,1)}), bf16[64,2,1536]{2,1,0:T(2,128)(2,1)S(1)}, u32[]{:S(2)}, u32[]{:S(2)}) %all-to-all-start.7) | async-done | bytes 393248 | tf_op jit(solution)/shard_map/all_to_all | solution.py:149
  217.3 4.7 %all-to-all-start.1 = ((bf16[32,8,128]{2,0,1:T(8,128)(2,1)}), bf16[32,8,128]{2,0,1:T(8,128)(2,1)S(1)}, u32[]{:S(2)}, u32[]{:S(2)}) async-start(bf16[32,8,128]{2,0,1:T(8,128)(2,1)} %copy_bitcast_fusion.3), calls=%async_computation.1 | async-start | bytes 131072 | tf_op jit(solution)/shard_map/all_to_all | solution.py:124
  222.1 0.7 copy.180
  222.8 0.7 convert_element_type.123
  223.5 10.7 %reshape.495 = bf16[8192,3,8]{2,1,0:T(4,128)(2,1)} reshape(bf16[64,2,1536]{2,1,0:T(2,128)(2,1)S(1)} %all-to-all-done.7) | data formatting | bytes 786432
  234.1 9.5 %copy.141 = bf16[3,8,8192]{2,1,0:T(8,128)(2,1)S(1)} copy(bf16[3,8,8192]{1,0,2:T(4,128)(2,1)} %bitcast.152) | data formatting | bytes 786432 | tf_op jit(solution)/shard_map/all_to_all | solution.py:149
  243.7 4.8 %all-to-all-start.6 = ((bf16[32,8,512]{2,0,1:T(8,128)(2,1)}), bf16[32,8,512]{2,0,1:T(8,128)(2,1)S(1)}, u32[]{:S(2)}, u32[]{:S(2)}) async-start(bf16[32,8,512]{2,0,1:T(8,128)(2,1)} %bitcast.147), calls=%async_computation.6 | async-start | bytes 524288 | tf_op jit(solution)/shard_map/all_to_all | solution.py:122
  248.7 0.5 copy.142
  249.2 19.5 %scatter_fusion = f32[256,8,128]{2,1,0:T(8,128)} fusion(f32[256,8,128]{2,1,0:T(8,128)} %bitcast.20, s32[192]{0:T(256)S(1)} %compare_select_fusion.3, f32[192,8,128]{2,1,0:T(8,128)S(1)} %bitcast.157), kind=kCustom, calls=%fused_computation.5 | custom fusion | bytes 2360064 | tf_op jit(solution)/shard_map/scatter | solution.py:156
  268.7 5.2 %all-to-all-start.8 = ((f32[256,8,128]{2,1,0:T(8,128)}), f32[256,8,128]{2,1,0:T(8,128)S(1)}, u32[]{:S(2)}, u32[]{:S(2)}) async-start(f32[256,8,128]{2,1,0:T(8,128)} %scatter_fusion), calls=%async_computation.8 | async-start | bytes 2097152 | tf_op jit(solution)/shard_map/all_to_all | solution.py:157
  273.9 0.7 add_bitcast_fusion.1
  274.6 0.9 fusion.57
  275.4 0.9 bitcast_convert_fusion
  276.3 1.2 reshape.411
  277.6 1.2 copy.132
  278.8 1.0 convert_bitcast_fusion.1
  279.8 0.2 reshape.412
  280.0 0.4 copy.135
  280.4 0.8 fusion.36
  281.2 0.2 fusion.6
  281.6 1.9 multiply_reduce_fusion
  283.7 0.8 copy.143
  284.5 20.0 %all-to-all-done.8 = f32[256,8,128]{2,1,0:T(8,128)S(1)} async-done(((f32[256,8,128]{2,1,0:T(8,128)}), f32[256,8,128]{2,1,0:T(8,128)S(1)}, u32[]{:S(2)}, u32[]{:S(2)}) %all-to-all-start.8) | async-done | bytes 1048608 | tf_op jit(solution)/shard_map/all_to_all | solution.py:157
  304.6 1.6 copy.144
  (92 shorter events, 2.4 us)
Async XLA Ops:
  0.6 59.4 %copy-start = (bf16[32,1024]{1,0:T(8,128)(2,1)S(1)}, bf16[32,1024]{1,0:T(8,128)(2,1)}, u32[]{:S(2)}) copy-start(bf16[32,1024]{1,0:T(8,128)(2,1)} %param.24) | copy-start | bytes 196612
  2.2 39.0 %all-to-all-start = ((bf16[8,2,128]{2,1,0:T(2,128)(2,1)}), bf16[8,2,128]{2,1,0:T(2,128)(2,1)S(1)}, u32[]{:S(2)}, u32[]{:S(2)}) async-start(bf16[8,2,128]{2,1,0:T(2,128)(2,1)} %reshape.490), calls=%async_computation | async-start | bytes 8192 | tf_op jit(solution)/shard_map/all_to_all | solution.py:125
  41.0 16.7 %copy-start.9 = (bf16[32,4096]{1,0:T(8,128)(2,1)S(1)}, bf16[32,4096]{1,0:T(8,128)(2,1)}, u32[]{:S(2)}) copy-start(bf16[32,4096]{1,0:T(8,128)(2,1)} %param.22) | copy-start | bytes 786436
  41.0 17.5 %copy-start.16 = (bf16[2,512]{1,0:T(2,128)(2,1)S(1)}, bf16[2,512]{1,0:T(2,128)(2,1)}, u32[]{:S(2)}) copy-start(bf16[2,512]{1,0:T(2,128)(2,1)} %param.31) | copy-start | bytes 6148
  41.0 17.6 %copy-start.24 = (bf16[2,128]{1,0:T(2,128)(2,1)S(1)}, bf16[2,128]{1,0:T(2,128)(2,1)}, u32[]{:S(2)}) copy-start(bf16[2,128]{1,0:T(2,128)(2,1)} %param.33) | copy-start | bytes 1540
  41.0 17.6 %copy-start.17 = (bf16[2,512]{1,0:T(2,128)(2,1)S(1)}, bf16[2,512]{1,0:T(2,128)(2,1)}, u32[]{:S(2)}) copy-start(bf16[2,512]{1,0:T(2,128)(2,1)} %param.32) | copy-start | bytes 6148
  41.1 17.6 %copy-start.19 = (s32[192]{0:T(256)S(1)}, s32[192]{0:T(256)}, u32[]{:S(2)}) copy-start(s32[192]{0:T(256)} %param.28) | copy-start | bytes 2308
  41.1 17.6 %copy-start.14 = (f32[8]{0:T(128)S(1)}, f32[8]{0:T(128)}, u32[]{:S(2)}) copy-start(f32[8]{0:T(128)} %param.37) | copy-start | bytes 100
  41.1 17.6 %copy-start.23 = (bf16[2,8]{1,0:T(2,128)(2,1)S(1)}, bf16[2,8]{1,0:T(2,128)(2,1)}, u32[]{:S(2)}) copy-start(bf16[2,8]{1,0:T(2,128)(2,1)} %param.35) | copy-start | bytes 100
  41.1 17.7 %copy-start.7 = (f32[2,8,64,128]{3,2,1,0:T(8,128)S(1)}, f32[2,8,64,128]{3,2,1,0:T(8,128)}, u32[]{:S(2)}) copy-start(f32[2,8,64,128]{3,2,1,0:T(8,128)} %param.36) | copy-start | bytes 1572868
  41.1 18.0 %copy-start.15 = (bf16[2,128]{1,0:T(2,128)(2,1)S(1)}, bf16[2,128]{1,0:T(2,128)(2,1)}, u32[]{:S(2)}) copy-start(bf16[2,128]{1,0:T(2,128)(2,1)} %param.34) | copy-start | bytes 1540
  41.1 18.7 %copy-start.21 = (f32[8]{0:T(128)S(1)}, f32[8]{0:T(128)}, u32[]{:S(2)}) copy-start(f32[8]{0:T(128)} %param.38) | copy-start | bytes 100
  41.1 47.3 %all-to-all-start.4 = ((f32[64,1,4096]{2,1,0:T(1,128)}), f32[64,1,4096]{2,1,0:T(1,128)S(1)}, u32[]{:S(2)}, u32[]{:S(2)}) async-start(f32[64,1,4096]{2,1,0:T(1,128)} %reshape.492), calls=%async_computation.4 | async-start | bytes 2097152 | tf_op jit(solution)/shard_map/all_to_all | solution.py:130
  59.1 0.9 copy-start.2
  88.4 44.7 %all-to-all-start.2 = ((bf16[32,8,128]{2,0,1:T(8,128)(2,1)}), bf16[32,8,128]{2,0,1:T(8,128)(2,1)S(1)}, u32[]{:S(2)}, u32[]{:S(2)}) async-start(bf16[32,8,128]{2,0,1:T(8,128)(2,1)} %copy_bitcast_fusion.2), calls=%async_computation.2 | async-start | bytes 131072 | tf_op jit(solution)/shard_map/all_to_all | solution.py:123
  133.2 10.9 %all-to-all-start.3 = ((bf16[32,8,512]{2,0,1:T(8,128)(2,1)}), bf16[32,8,512]{2,0,1:T(8,128)(2,1)S(1)}, u32[]{:S(2)}, u32[]{:S(2)}) async-start(bf16[32,8,512]{2,0,1:T(8,128)(2,1)} %bitcast.148), calls=%async_computation.3 | async-start | bytes 524288 | tf_op jit(solution)/shard_map/all_to_all | solution.py:121
  144.1 30.7 %all-to-all-start.5 = ((f32[192,8,128]{2,1,0:T(8,128)}), f32[192,8,128]{2,1,0:T(8,128)S(1)}, u32[]{:S(2)}, u32[]{:S(2)}) async-start(f32[192,8,128]{2,1,0:T(8,128)} %broadcast_select_fusion), calls=%async_computation.5 | async-start | bytes 1572864 | tf_op jit(solution)/shard_map/all_to_all | solution.py:132
  155.3 20.3 %copy-start.3 = (bf16[256,8,64]{2,1,0:T(8,128)(2,1)}, bf16[256,8,64]{2,1,0:T(8,128)(2,1)S(1)}, u32[]{:S(2)}) copy-start(bf16[256,8,64]{2,1,0:T(8,128)(2,1)S(1)} %reshape.403) | copy-start | bytes 786436
  182.0 19.0 %copy-start.18 = (f32[512]{0:T(512)S(1)}, f32[512]{0:T(512)}, u32[]{:S(2)}) copy-start(f32[512]{0:T(512)} %param.39) | copy-start | bytes 6148
  182.0 19.3 %copy-start.11 = (bf16[32,1024]{1,0:T(8,128)(2,1)S(1)}, bf16[32,1024]{1,0:T(8,128)(2,1)}, u32[]{:S(2)}) copy-start(bf16[32,1024]{1,0:T(8,128)(2,1)} %param.25) | copy-start | bytes 196612
  182.0 40.0 %copy-start.20 = (s32[192]{0:T(256)S(1)}, s32[192]{0:T(256)}, u32[]{:S(2)}) copy-start(s32[192]{0:T(256)} %param.29) | copy-start | bytes 2308
  182.0 40.0 %copy-start.10 = (bf16[32,4096]{1,0:T(8,128)(2,1)S(1)}, bf16[32,4096]{1,0:T(8,128)(2,1)}, u32[]{:S(2)}) copy-start(bf16[32,4096]{1,0:T(8,128)(2,1)} %param.23) | copy-start | bytes 786436
  195.6 21.7 %all-to-all-start.7 = ((bf16[64,2,1536]{2,1,0:T(2,128)(2,1)}), bf16[64,2,1536]{2,1,0:T(2,128)(2,1)S(1)}, u32[]{:S(2)}, u32[]{:S(2)}) async-start(bf16[64,2,1536]{2,1,0:T(2,128)(2,1)} %reshape.494), calls=%async_computation.7 | async-start | bytes 786432 | tf_op jit(solution)/shard_map/all_to_all | solution.py:149
  217.3 26.3 %all-to-all-start.1 = ((bf16[32,8,128]{2,0,1:T(8,128)(2,1)}), bf16[32,8,128]{2,0,1:T(8,128)(2,1)S(1)}, u32[]{:S(2)}, u32[]{:S(2)}) async-start(bf16[32,8,128]{2,0,1:T(8,128)(2,1)} %copy_bitcast_fusion.3), calls=%async_computation.1 | async-start | bytes 131072 | tf_op jit(solution)/shard_map/all_to_all | solution.py:124
  243.7 25.0 %all-to-all-start.6 = ((bf16[32,8,512]{2,0,1:T(8,128)(2,1)}), bf16[32,8,512]{2,0,1:T(8,128)(2,1)S(1)}, u32[]{:S(2)}, u32[]{:S(2)}) async-start(bf16[32,8,512]{2,0,1:T(8,128)(2,1)} %bitcast.147), calls=%async_computation.6 | async-start | bytes 524288 | tf_op jit(solution)/shard_map/all_to_all | solution.py:122
  268.7 6.8 %copy-start.5 = (bf16[32,8,512]{2,0,1:T(8,128)(2,1)}, bf16[32,8,512]{2,0,1:T(8,128)(2,1)S(1)}, u32[]{:S(2)}) copy-start(bf16[32,8,512]{2,0,1:T(8,128)(2,1)S(1)} %all-to-all-done.6) | copy-start | bytes 786436
  268.7 35.9 %all-to-all-start.8 = ((f32[256,8,128]{2,1,0:T(8,128)}), f32[256,8,128]{2,1,0:T(8,128)S(1)}, u32[]{:S(2)}, u32[]{:S(2)}) async-start(f32[256,8,128]{2,1,0:T(8,128)} %scatter_fusion), calls=%async_computation.8 | async-start | bytes 2097152 | tf_op jit(solution)/shard_map/all_to_all | solution.py:157
  280.4 1.0 copy-start.4
  280.4 1.2 copy-start.6
  280.4 1.2 copy-start.8
  280.4 1.2 copy-start.12
  280.4 1.2 copy-start.13
  280.4 1.2 copy-start.22
  281.6 24.5 %copy-start.1 = (bf16[32,1024]{1,0:T(8,128)(2,1)S(1)}, bf16[32,1024]{1,0:T(8,128)(2,1)}, u32[]{:S(2)}) copy-start(bf16[32,1024]{1,0:T(8,128)(2,1)} %param.24) | copy-start | bytes 196612
where the time goes:
time: 309 us; the launch traced here: 306 us
  local copies, waits for them, and re-layouts  144 us (47%)
  waiting for transfers between devices  86.8 us (28%)
  starting transfers between devices  57.3 us (19%)
  other arithmetic  12.1 us (4%)
  matrix products  5.16 us (2%)
    unnamed x62, local copies, waits for them, and re-layouts  81.7 us
    all_to_all x1, waiting for transfers between devices, local(): lax.all_to_all(state_rows, 'serve', split_axis=2, concat_axis=0, tiled=True)  27.8 us
    all_to_all x1, waiting for transfers between devices, local(): lax.all_to_all(renewed, 'serve', split_axis=0, concat_axis=2, tiled=True)  20 us
    scatter x1, local copies, waits for them, and re-layouts, local(): renewed = pieces.at[snapshot_slots].set(snap_pieces)  19.5 us
    all_to_all x1, waiting for transfers between devices, local(): lax.all_to_all(wanted, 'serve', split_axis=0, concat_axis=2, tiled=True)  18.7 us
    all_to_all x1, starting transfers between devices, local(): lax.all_to_all(state_rows, 'serve', split_axis=2, concat_axis=0, tiled=True)  16.6 us
    all_to_all x1, waiting for transfers between devices, local(): lax.all_to_all(finals.reshape(finals.shape[0], heads_dev, HEAD_DIM * STAT...  15.4 us
    all_to_all x2, local copies, waits for them, and re-layouts, local(): lax.all_to_all(state_rows, 'serve', split_axis=2, concat_axis=0, tiled=True)  13.5 us
  transfers between devices with their start and end apart: 9, of which 5 were waited for; matrix products, arithmetic and copies ran while one was open for 45% of the time, Pallas kernels for 0%

commit v1 on v0

v1 whole, which is shorter than its diff:
```python
import jax
import jax.numpy as jnp
from jax import lax
from jax.experimental import pallas as pl
from jax.experimental.pallas import tpu as pltpu
from jax.sharding import PartitionSpec as P

HEAD_DIM = 64
STATE = 128
REQS = 3
SLOTS = 4
ROWS = 8

f32 = jnp.float32
bf16 = jnp.bfloat16
highest = lax.Precision.HIGHEST

ANY = pl.BlockSpec(memory_space=pl.ANY)
HBM = pl.BlockSpec(memory_space=pltpu.HBM)
VMEM = pl.BlockSpec(memory_space=pltpu.VMEM)
SMEM = pl.BlockSpec(memory_space=pltpu.SMEM)


def params(mib=12):
    return pltpu.CompilerParams(vmem_limit_bytes=mib * 1024 * 1024)


def cost(flops, moved):
    return pl.CostEstimate(flops=flops, bytes_accessed=moved, transcendentals=0)


def dot(a, b):
    return jnp.dot(a, b, preferred_element_type=f32)


def dot_nt(a, b):
    return lax.dot_general(a, b, (((1,), (1,)), ((), ())), preferred_element_type=f32)


def dot_tn(a, b):
    return lax.dot_general(a, b, (((0,), (0,)), ((), ())), preferred_element_type=f32)


def split(value, parts):
    pieces = []
    for _ in range(parts):
        piece = value.astype(bf16)
        pieces.append(piece)
        value = value - piece.astype(f32)
    return pieces


def exact_left(mask, value, parts=3):
    total = None
    for piece in split(value, parts):
        term = dot(mask, piece)
        total = term if total is None else total + term
    return total


def exact_right(value, mask, parts=3):
    total = None
    for piece in split(value, parts):
        term = dot(piece, mask)
        total = term if total is None else total + term
    return total


def pack_first(x_ref, b_ref, dt_ref, out_ref, steps, held, sems):
    count = out_ref.shape[0]
    heads_dev = dt_ref.shape[1] // count
    width = x_ref.shape[1] // count
    copies = []
    for d in range(count):
        copies.append(
            pltpu.make_async_copy(
                x_ref.at[:, d * width : (d + 1) * width],
                out_ref.at[d, :, 0:width],
                sems.at[0, d],
            )
        )
        copies.append(
            pltpu.make_async_copy(
                b_ref.at[:, d * STATE : (d + 1) * STATE],
                out_ref.at[d, :, width : width + STATE],
                sems.at[1, d],
            )
        )
    early = pltpu.make_async_copy(dt_ref, steps, sems.at[1, count])
    early.start()
    for copy in copies:
        copy.start()
    early.wait()
    raw = steps[...].astype(f32)
    raw = jnp.concatenate([raw, jnp.zeros((raw.shape[0], STATE - raw.shape[1]), f32)], axis=1)
    for d in range(count):
        mine = raw if d == 0 else pltpu.roll(raw, STATE - d * heads_dev, 1)
        held[d] = mine.astype(bf16)
    last = pltpu.make_async_copy(
        held, out_ref.at[:, :, width + STATE : width + 2 * STATE], sems.at[0, count]
    )
    last.start()
    for copy in copies:
        copy.wait()
    last.wait()


def pack_second(me_ref, after_ref, z_ref, c_ref, *refs):
    del after_ref
    out_refs, sems = refs[:-1], refs[-1]
    count = len(out_refs)
    width = z_ref.shape[1] // count
    copies = []
    for k in range(count):
        peer = me_ref[0] ^ k
        z_start = pl.multiple_of(peer * width, STATE)
        c_start = pl.multiple_of(peer * STATE, STATE)
        copies.append(
            pltpu.make_async_copy(
                z_ref.at[:, pl.ds(z_start, width)], out_refs[k].at[:, 0:width], sems.at[0, k]
            )
        )
        copies.append(
            pltpu.make_async_copy(
                c_ref.at[:, pl.ds(c_start, STATE)],
                out_refs[k].at[:, width : width + STATE],
                sems.at[1, k],
            )
        )
    for copy in copies:
        copy.start()
    for copy in copies:
        copy.wait()


def pack_cache(cache_ref, out_ref):
    for s in range(SLOTS):
        out_ref[:, s * STATE : (s + 1) * STATE] = cache_ref[s].astype(bf16)


def segment_of(position, ends):
    return (position >= ends[0]).astype(jnp.int32) + (position >= ends[1]).astype(jnp.int32)


def segment_ends(len_ref):
    first = len_ref[0, 0]
    return first, first + len_ref[0, 1]


def spread_heads(heads, width):
    row = lax.broadcasted_iota(jnp.int32, (heads, width), 0)
    column = lax.broadcasted_iota(jnp.int32, (heads, width), 1)
    return (row == column // (width // heads)).astype(bf16)


def local_state(len_ref, rate_ref, tok_ref, send_ref, out_ref):
    del send_ref
    length = tok_ref.shape[0]
    heads = rate_ref.shape[1]
    width = heads * HEAD_DIM
    ends = segment_ends(len_ref)
    step_size = jax.nn.softplus(tok_ref[:, width + STATE : width + STATE + heads].astype(f32))
    log_decay = -step_size * rate_ref[...]
    row = lax.broadcasted_iota(jnp.int32, (length, length), 0)
    column = lax.broadcasted_iota(jnp.int32, (length, length), 1)
    later = (segment_of(row, ends) == segment_of(column, ends)) & (column > row)
    after = exact_left(later.astype(f32).astype(bf16), log_decay)
    weight = exact_right(jnp.exp(after) * step_size, spread_heads(heads, width), 2)
    scaled = (weight * tok_ref[:, 0:width].astype(f32)).astype(bf16)
    token = lax.broadcasted_iota(jnp.int32, (length, STATE), 0)
    lane = lax.broadcasted_iota(jnp.int32, (length, STATE), 1)
    seg_index = segment_of(token, ends)
    b_half = tok_ref[:, width : width + STATE].astype(f32)
    b_parts = jnp.concatenate(
        [jnp.where(seg_index == j, b_half, 0.0).astype(bf16) for j in range(REQS)], axis=1
    )
    out_ref[:, 0 : REQS * STATE] = dot_tn(scaled, b_parts).astype(bf16)
    member = (seg_index == lane % REQS).astype(f32).astype(bf16)
    total = None
    for piece in split(log_decay, 3):
        term = dot_tn(piece, member)
        total = term if total is None else total + term
    kept = jnp.exp(total)
    high = kept.astype(bf16).astype(f32)
    lane_h = lax.broadcasted_iota(jnp.int32, (heads, STATE), 1)
    parts = jnp.where(lane_h < REQS, high, jnp.where(lane_h < 2 * REQS, kept - high, 0.0))
    row_w = lax.broadcasted_iota(jnp.int32, (width, heads), 0)
    col_w = lax.broadcasted_iota(jnp.int32, (width, heads), 1)
    owner = (row_w // HEAD_DIM == col_w).astype(f32).astype(bf16)
    spread = dot(owner, parts.astype(bf16))
    row_s = lax.broadcasted_iota(jnp.int32, (width, STATE), 0)
    lane_s = lax.broadcasted_iota(jnp.int32, (width, STATE), 1)
    chosen = jnp.where(lane_s == row_s % ROWS, spread, 0.0).astype(bf16)
    out_ref[:, REQS * STATE :] = dot(chosen, jnp.ones((STATE, STATE), bf16)).astype(bf16)


def combine(hit_ref, place_ref, after_ref, recv_ref, out_ref, held):
    del after_ref
    for s in range(recv_ref.shape[0]):
        block = recv_ref[s, :, 0 : SLOTS * STATE].astype(f32)
        for k in range(SLOTS):
            held[s * SLOTS + k] = block[:, k * STATE : (k + 1) * STATE]
    for s in range(recv_ref.shape[0]):
        block = recv_ref[s, :, SLOTS * STATE :].astype(f32)
        kept = block[:, REQS * STATE :]
        for j in range(REQS):
            prefix = held[hit_ref[s * REQS + j]]
            out_ref[s, :, j * STATE : (j + 1) * STATE] = prefix.astype(bf16)
            factor = kept[j : j + 1, :] + kept[REQS + j : REQS + j + 1, :]
            new = factor * prefix + block[:, j * STATE : (j + 1) * STATE]
            place = place_ref[s * REQS + j]
            start = pl.multiple_of((REQS + (place & 3)) * STATE, STATE)
            out_ref[place >> 2, :, pl.ds(start, STATE)] = new.astype(bf16)


def write_cache(missing_ref, cache_ref, recv_ref, out_ref):
    missing = missing_ref[0]
    for s in range(SLOTS):

        @pl.when(missing == s)
        def _():
            out_ref[s] = cache_ref[s]

        if s < REQS:

            @pl.when(missing > s)
            def _():
                out_ref[s] = recv_ref[:, (REQS + s) * STATE : (REQS + s + 1) * STATE].astype(f32)

        if s > 0:

            @pl.when(missing < s)
            def _():
                out_ref[s] = recv_ref[:, (REQS + s - 1) * STATE : (REQS + s) * STATE].astype(f32)


def token_inner(len_ref, me_ref, rate_ref, skip_ref, tok_ref, *refs):
    gate_refs, (base_ref, factor_ref, read_ref, gates, sems) = refs[:-5], refs[-5:]
    length = tok_ref.shape[0]
    heads = rate_ref.shape[1]
    width = heads * HEAD_DIM
    rows = length // len(gate_refs)
    copies = []
    for k in range(len(gate_refs)):
        start = pl.multiple_of((me_ref[0] ^ k) * rows, rows)
        copies.append(
            pltpu.make_async_copy(gate_refs[k], gates.at[pl.ds(start, rows), :], sems.at[k])
        )
    for copy in copies:
        copy.start()
    ends = segment_ends(len_ref)
    step_size = jax.nn.softplus(tok_ref[:, width + STATE : width + STATE + heads].astype(f32))
    log_decay = -step_size * rate_ref[...]
    row = lax.broadcasted_iota(jnp.int32, (length, length), 0)
    column = lax.broadcasted_iota(jnp.int32, (length, length), 1)
    upto = (segment_of(row, ends) == segment_of(column, ends)) & (column <= row)
    running = exact_left(upto.astype(f32).astype(bf16), log_decay)
    spread = spread_heads(heads, width)
    decay = exact_right(jnp.exp(running), spread)
    undo = exact_right(jnp.exp(-running) * step_size, spread, 2)
    values = tok_ref[:, 0:width].astype(f32)
    b_half = tok_ref[:, width : width + STATE]
    for copy in copies:
        copy.wait()
    c_half = gates[:, width : width + STATE]
    c_wide = c_half.astype(f32)
    scores = jnp.where(upto, dot_nt(c_half, b_half), 0.0).astype(bf16)
    token = lax.broadcasted_iota(jnp.int32, (length, STATE), 0)
    seg_index = segment_of(token, ends)
    for j in range(REQS):
        read_ref[:, j * STATE : (j + 1) * STATE] = jnp.where(seg_index == j, c_wide, 0.0).astype(
            bf16
        )
    inner = dot(scores, (undo * values).astype(bf16))
    gate_in = gates[:, 0:width].astype(f32)
    gate = gate_in / (1.0 + jnp.exp(-gate_in))
    base_ref[...] = gate * (decay * inner + exact_right(skip_ref[...], spread) * values)
    factor_ref[...] = gate * decay


def token_outputs(gain_ref, base_ref, factor_ref, read_ref, recv_ref, out_ref):
    carried = dot_nt(read_ref[...], recv_ref[:, 0 : REQS * STATE])
    gated = base_ref[...] + factor_ref[...] * carried
    square_mean = jnp.mean(gated * gated, axis=1, keepdims=True)
    out_ref[...] = (gated * lax.rsqrt(square_mean + 1e-05) * gain_ref[...]).astype(bf16)


def gated_norm(values, gate_in, norm_weight):
    shaped = values.shape
    gated = values * jax.nn.silu(gate_in.astype(jnp.float32).reshape(shaped))
    square_mean = jnp.mean(gated * gated, axis=(2, 3), keepdims=True)
    normed = gated * lax.rsqrt(square_mean + 1e-05) * norm_weight.reshape(shaped[1:])
    return normed.reshape(shaped[0], -1).astype(jnp.bfloat16)


def decode_block(
    inputs, gate_in, b_proj, c_proj, step_raw, states, head_rates, skip_gain, norm_weight
):
    row_count = inputs.shape[0]
    head_count = step_raw.shape[1]
    groups = b_proj.shape[1] // STATE
    per_group = head_count // groups
    step_size = jax.nn.softplus(step_raw.astype(jnp.float32))
    factor = jnp.exp(-step_size * head_rates[None, :]).reshape(row_count, groups, per_group, 1, 1)
    values = inputs.astype(jnp.float32).reshape(row_count, groups, per_group, HEAD_DIM)
    b_group = b_proj.astype(jnp.float32).reshape(row_count, groups, STATE)
    c_group = c_proj.astype(jnp.float32).reshape(row_count, groups, STATE)
    written = (step_size.reshape(row_count, groups, per_group, 1) * values)[..., None] * b_group[
        :, :, None, None, :
    ]
    updated = factor * states.reshape(row_count, groups, per_group, HEAD_DIM, STATE) + written
    outputs = (
        jnp.einsum("rgkpn,rgn->rgkp", updated, c_group, precision=highest)
        + skip_gain.reshape(groups, per_group, 1) * values
    )
    return (
        gated_norm(outputs, gate_in, norm_weight),
        updated.reshape(row_count, head_count, HEAD_DIM, STATE),
    )


def local(
    pre_x,
    pre_z,
    pre_b,
    pre_c,
    pre_dt,
    suffix_lengths,
    prefix_hits,
    snapshot_slots,
    cache_states,
    dec_x,
    dec_z,
    dec_b,
    dec_c,
    dec_dt,
    dec_states,
    decay_rate,
    d_skip,
    norm_weight,
):
    n_head = lax.axis_size("head")
    n_serve = lax.axis_size("serve")
    rows = pre_x.shape[0]
    heads = cache_states.shape[1]
    width = heads * HEAD_DIM
    length = rows * n_head
    tiles = SLOTS + REQS + 1
    shape = jax.ShapeDtypeStruct

    def swap(value, axis):
        return lax.all_to_all(value, axis, split_axis=0, concat_axis=0, tiled=True)

    with jax.named_scope("tokens"):
        first = pl.pallas_call(
            pack_first,
            out_shape=shape((n_head, rows, width + 2 * STATE), bf16),
            in_specs=[HBM] * 3,
            out_specs=HBM,
            scratch_shapes=[
                pltpu.VMEM(pre_dt.shape, bf16),
                pltpu.VMEM((n_head, rows, STATE), bf16),
                pltpu.SemaphoreType.DMA((2, n_head + 1)),
            ],
            compiler_params=params(),
            cost_estimate=cost(0, 800_000),
        )(pre_x, pre_b, pre_dt)
        tokens = swap(first, "head").reshape(length, width + 2 * STATE)
    with jax.named_scope("cache"):
        cache_rows = cache_states.reshape(SLOTS, width, STATE)
        send = pl.pallas_call(
            pack_cache,
            out_shape=shape((width, tiles * STATE), bf16),
            grid=(1,),
            in_specs=[VMEM],
            out_specs=pl.BlockSpec((width, SLOTS * STATE), lambda i: (0, 0)),
            compiler_params=params(),
            cost_estimate=cost(0, 1_600_000),
        )(cache_rows)
    with jax.named_scope("orders"):
        rank = jnp.sum(
            (snapshot_slots[None, :] < snapshot_slots[:, None]).astype(jnp.int32), axis=1
        )
        place = (rank // REQS) * 4 + rank % REQS
        serve_me = lax.axis_index("serve")
        missing = (
            sum(range(SLOTS))
            - jnp.sum(jnp.where(snapshot_slots // SLOTS == serve_me, snapshot_slots % SLOTS, 0))
        ).reshape(1)
        head_me = lax.axis_index("head").astype(jnp.int32).reshape(1)
    rates = decay_rate.reshape(1, heads)
    with jax.named_scope("local"):
        send = pl.pallas_call(
            local_state,
            out_shape=shape((width, tiles * STATE), bf16),
            grid=(1,),
            in_specs=[SMEM, VMEM, VMEM, ANY],
            out_specs=pl.BlockSpec((width, SLOTS * STATE), lambda i: (0, 1)),
            input_output_aliases={3: 0},
            compiler_params=params(),
            cost_estimate=cost(300_000_000, 800_000),
        )(suffix_lengths, rates, tokens, send)
        pieces = swap(send.reshape(n_serve, ROWS, tiles * STATE), "serve")
    with jax.named_scope("gates"):
        mine = pl.pallas_call(
            pack_second,
            out_shape=[shape((rows, width + STATE), bf16)] * n_head,
            in_specs=[SMEM, ANY, HBM, HBM],
            out_specs=[ANY] * n_head,
            scratch_shapes=[pltpu.SemaphoreType.DMA((2, n_head))],
            compiler_params=params(),
            cost_estimate=cost(0, 650_000),
        )(head_me, send, pre_z, pre_c)
        gates = [mine[0]] + [
            lax.ppermute(mine[k], "head", [(i, i ^ k) for i in range(n_head)])
            for k in range(1, n_head)
        ]
    with jax.named_scope("inner"):
        base, factor, read = pl.pallas_call(
            token_inner,
            out_shape=(
                shape((length, width), f32),
                shape((length, width), f32),
                shape((length, REQS * STATE), bf16),
            ),
            in_specs=[SMEM] * 2 + [VMEM] * 3 + [ANY] * n_head,
            out_specs=[VMEM] * 3,
            scratch_shapes=[
                pltpu.VMEM((length, width + STATE), bf16),
                pltpu.SemaphoreType.DMA((n_head,)),
            ],
            compiler_params=params(),
            cost_estimate=cost(400_000_000, 1_500_000),
        )(suffix_lengths, head_me, rates, d_skip.reshape(1, heads), tokens, *gates)
    with jax.named_scope("combine"):
        answer = pl.pallas_call(
            combine,
            out_shape=shape((n_serve, ROWS, 2 * REQS * STATE), bf16),
            in_specs=[SMEM, SMEM, ANY, VMEM],
            out_specs=VMEM,
            scratch_shapes=[pltpu.VMEM((n_serve * SLOTS, ROWS, STATE), f32)],
            compiler_params=params(),
            cost_estimate=cost(0, 4_000_000),
        )(prefix_hits, place, read, pieces)
        got = swap(answer, "serve").reshape(width, 2 * REQS * STATE)
    dec_out, dec_new = decode_block(
        dec_x, dec_z, dec_b, dec_c, dec_dt, dec_states, decay_rate, d_skip, norm_weight
    )
    with jax.named_scope("outputs"):
        pre_out = pl.pallas_call(
            token_outputs,
            out_shape=shape((length, width), bf16),
            in_specs=[VMEM] * 5,
            out_specs=VMEM,
            compiler_params=params(),
            cost_estimate=cost(200_000_000, 1_500_000),
        )(norm_weight.reshape(1, width), base, factor, read, got)
        cache_out = pl.pallas_call(
            write_cache,
            out_shape=shape((SLOTS, width, STATE), f32),
            in_specs=[SMEM, VMEM, VMEM],
            out_specs=VMEM,
            compiler_params=params(),
            cost_estimate=cost(0, 2_500_000),
        )(missing, cache_rows, got).reshape(cache_states.shape)
    return (pre_out, cache_out, dec_out, dec_new)


def solution(mesh):
    return jax.shard_map(
        local,
        mesh=mesh,
        in_specs=(
            P(("serve", "head"), None),
            P(("serve", "head"), None),
            P(("serve", "head"), None),
            P(("serve", "head"), None),
            P(("serve", "head"), None),
            P("serve", None),
            P(),
            P(),
            P("serve", "head", None, None),
            P("serve", "head"),
            P("serve", "head"),
            P("serve", "head"),
            P("serve", "head"),
            P("serve", "head"),
            P("serve", "head", None, None),
            P("head"),
            P("head"),
            P("head"),
        ),
        out_specs=(
            P("serve", "head"),
            P("serve", "head", None, None),
            P("serve", "head"),
            P("serve", "head", None, None),
        ),
        check_vma=False,
    )
```

time: 309 us -> 110 us (0.36)
  the two profiles are of different devices: /device:TPU:18 before, /device:TPU:16 now
where the time goes in v1:
time: 110 us; the launch traced here: 109 us
  starting transfers between devices  54.4 us (49%)
  waiting for transfers between devices  31 us (28%)
  Pallas kernels  11.5 us (10%)
  local copies, waits for them, and re-layouts  7.6 us (7%)
  other arithmetic  2.45 us (2%)
  between operations  1.57 us (1%)
    all_to_all x3, starting transfers between devices, swap(): return lax.all_to_all(value, axis, split_axis=0, concat_axis=0, tiled=True)  33 us
    all_to_all x3, waiting for transfers between devices, swap(): return lax.all_to_all(value, axis, split_axis=0, concat_axis=0, tiled=True)  28.2 us
    ppermute x7, starting transfers between devices, local(): lax.ppermute(mine[k], 'head', [(i, i ^ k) for i in range(n_head)])  21.4 us
    unnamed x40, local copies, waits for them, and re-layouts  6.7 us
    ppermute x7, waiting for transfers between devices, local(): lax.ppermute(mine[k], 'head', [(i, i ^ k) for i in range(n_head)])  2.81 us
    pallas_call x1, Pallas kernels, local(): pl.pallas_call(local_state, out_shape=shape((width, tiles * STATE), bf16)...  2.61 us
    pallas_call x1, Pallas kernels, local(): pl.pallas_call(token_inner, out_shape=(shape((length, width), f32), shape...  2.45 us
  transfers between devices with their start and end apart: 10, of which 5 were waited for; matrix products, arithmetic and copies ran while one was open for 4% of the time, Pallas kernels for 3%

profile of v1, /device:TPU:16, one launch (start us, length us, event | category | flops | bytes accessed | tf_op | source)
XLA Modules:
  0.0 109.3 jit_solution(6881295541051921404)
XLA Ops:
  0.6 0.0 copy-start
  0.6 0.0 copy-start.1
  0.7 0.0 copy-start.5
  0.7 1.0 copy-done.5
  1.7 0.8 copy-done.6
  2.5 0.7 copy-done.8
  3.2 0.9 tokens.1
  4.1 4.3 %all-to-all-start = ((bf16[8,32,768]{2,1,0:T(8,128)(2,1)}), bf16[8,32,768]{2,1,0:T(8,128)(2,1)S(1)}, u32[]{:S(2)}, u32[]{:S(2)}) async-start(bf16[8,32,768]{2,1,0:T(8,128)(2,1)} %tokens.1), calls=%async_computation | async-start | bytes 786432 | tf_op jit(solution)/shard_map/tokens/all_to_all | solution.py:352
  8.5 0.0 copy-done.1
  8.5 0.9 cache.1.send_ref
  9.3 8.1 %all-to-all-done = bf16[8,32,768]{2,1,0:T(8,128)(2,1)S(1)} async-done(((bf16[8,32,768]{2,1,0:T(8,128)(2,1)}), bf16[8,32,768]{2,1,0:T(8,128)(2,1)S(1)}, u32[]{:S(2)}, u32[]{:S(2)}) %all-to-all-start) | async-done | bytes 393248 | tf_op jit(solution)/shard_map/tokens/all_to_all | solution.py:352
  17.4 0.7 copy-done.10
  18.1 0.0 copy-done.12
  18.1 2.6 %local.1.after_ref = bf16[512,1024]{1,0:T(8,128)(2,1)} custom-call(s32[1,3]{1,0:T(1,128)S(1)} %copy-done.12, f32[1,8]{1,0:T(1,128)S(1)} %bitcast.22, bf16[256,768]{1,0:T(8,128)(2,1)S(1)} %bitcast.19, bf16[512,1024]{1,0:T(8,128)(2,1)} %cache.1.send_ref), custom_call_target="tpu_custom_call", output_to_operand_aliasing={{}: (3, {})} | custom-call | flops 300000000 | bytes 800000 | tf_op jit(solution)/shard_map/local/pallas_call | solution.py:393
  20.7 16.6 %all-to-all-start.1 = ((bf16[64,8,1024]{2,1,0:T(8,128)(2,1)}), bf16[64,8,1024]{2,1,0:T(8,128)(2,1)S(1)}, u32[]{:S(2)}, u32[]{:S(2)}) async-start(bf16[64,8,1024]{2,1,0:T(8,128)(2,1)} %bitcast.6), calls=%async_computation.1 | async-start | bytes 2097152 | tf_op jit(solution)/shard_map/local/all_to_all | solution.py:352
  37.3 0.0 copy-done.4
  37.3 0.0 copy-done.7
  37.3 0.3 gates.1
  37.7 0.0 copy-start.15
  37.7 1.9 %collective-permute-start = (bf16[32,640]{1,0:T(8,128)(2,1)S(1)}, bf16[32,640]{1,0:T(8,128)(2,1)S(1)}, u32[]{:S(2)}, u32[]{:S(2)}) collective-permute-start(bf16[32,640]{1,0:T(8,128)(2,1)S(1)} %get-tuple-element.16), channel_id=1, source_target_pairs={{0,1},{1,0},{2,3},{3,2},{4,5},{5,4},{6,7},{7,6},{8,9},{9,8},{10,11... | collective-permute-start | bytes 122888 | tf_op jit(solution)/shard_map/gates/ppermute | solution.py:415
  39.6 2.5 %collective-permute-start.1 = (bf16[32,640]{1,0:T(8,128)(2,1)S(1)}, bf16[32,640]{1,0:T(8,128)(2,1)S(1)}, u32[]{:S(2)}, u32[]{:S(2)}) collective-permute-start(bf16[32,640]{1,0:T(8,128)(2,1)S(1)} %get-tuple-element.17), channel_id=1, source_target_pairs={{0,2},{1,3},{2,0},{3,1},{4,6},{5,7},{6,4},{7,5},{8,10},{9,11},{10,... | collective-permute-start | bytes 122888 | tf_op jit(solution)/shard_map/gates/ppermute | solution.py:415
  42.1 0.0 copy-done.15
  42.1 0.2 convert_reduce_fusion
  42.3 3.2 %collective-permute-start.2 = (bf16[32,640]{1,0:T(8,128)(2,1)S(1)}, bf16[32,640]{1,0:T(8,128)(2,1)S(1)}, u32[]{:S(2)}, u32[]{:S(2)}) collective-permute-start(bf16[32,640]{1,0:T(8,128)(2,1)S(1)} %get-tuple-element.18), channel_id=1, source_target_pairs={{0,3},{1,2},{2,1},{3,0},{4,7},{5,6},{6,5},{7,4},{8,11},{9,10},{10,... | collective-permute-start | bytes 122888 | tf_op jit(solution)/shard_map/gates/ppermute | solution.py:415
  45.5 2.8 %collective-permute-start.3 = (bf16[32,640]{1,0:T(8,128)(2,1)S(1)}, bf16[32,640]{1,0:T(8,128)(2,1)S(1)}, u32[]{:S(2)}, u32[]{:S(2)}) collective-permute-start(bf16[32,640]{1,0:T(8,128)(2,1)S(1)} %get-tuple-element.19), channel_id=1, source_target_pairs={{0,4},{1,5},{2,6},{3,7},{4,0},{5,1},{6,2},{7,3},{8,12},{9,13},{10,... | collective-permute-start | bytes 122888 | tf_op jit(solution)/shard_map/gates/ppermute | solution.py:415
  48.3 4.2 %collective-permute-start.4 = (bf16[32,640]{1,0:T(8,128)(2,1)S(1)}, bf16[32,640]{1,0:T(8,128)(2,1)S(1)}, u32[]{:S(2)}, u32[]{:S(2)}) collective-permute-start(bf16[32,640]{1,0:T(8,128)(2,1)S(1)} %get-tuple-element.20), channel_id=1, source_target_pairs={{0,5},{1,4},{2,7},{3,6},{4,1},{5,0},{6,3},{7,2},{8,13},{9,12},{10,... | collective-permute-start | bytes 122888 | tf_op jit(solution)/shard_map/gates/ppermute | solution.py:415
  52.5 0.0 collective-permute-done.refs_1_
  52.5 3.1 %collective-permute-start.5 = (bf16[32,640]{1,0:T(8,128)(2,1)S(1)}, bf16[32,640]{1,0:T(8,128)(2,1)S(1)}, u32[]{:S(2)}, u32[]{:S(2)}) collective-permute-start(bf16[32,640]{1,0:T(8,128)(2,1)S(1)} %get-tuple-element.21), channel_id=1, source_target_pairs={{0,6},{1,7},{2,4},{3,5},{4,2},{5,3},{6,0},{7,1},{8,14},{9,15},{10,... | collective-permute-start | bytes 122888 | tf_op jit(solution)/shard_map/gates/ppermute | solution.py:415
  55.6 0.0 collective-permute-done.1.refs_2_
  55.6 3.8 %collective-permute-start.6 = (bf16[32,640]{1,0:T(8,128)(2,1)S(1)}, bf16[32,640]{1,0:T(8,128)(2,1)S(1)}, u32[]{:S(2)}, u32[]{:S(2)}) collective-permute-start(bf16[32,640]{1,0:T(8,128)(2,1)S(1)} %get-tuple-element.22), channel_id=1, source_target_pairs={{0,7},{1,6},{2,5},{3,4},{4,3},{5,2},{6,1},{7,0},{8,15},{9,14},{10,... | collective-permute-start | bytes 122888 | tf_op jit(solution)/shard_map/gates/ppermute | solution.py:415
  59.4 0.0 collective-permute-done.2.refs_3_
  59.4 0.0 collective-permute-done.3.refs_4_
  59.4 0.0 collective-permute-done.4.refs_5_
  59.4 0.2 collective-permute-done.5.refs_6_
  59.6 2.6 %collective-permute-done.6.refs_7_ = bf16[32,640]{1,0:T(8,128)(2,1)S(1)} collective-permute-done((bf16[32,640]{1,0:T(8,128)(2,1)S(1)}, bf16[32,640]{1,0:T(8,128)(2,1)S(1)}, u32[]{:S(2)}, u32[]{:S(2)}) %collective-permute-start.6) | collective-permute-done | bytes 40992 | tf_op jit(solution)/shard_map/gates/ppermute | solution.py:415
  62.2 0.7 copy-done.13
  62.9 2.5 %inner.1 = (f32[256,512]{1,0:T(8,128)S(1)}, f32[256,512]{1,0:T(8,128)S(1)}, bf16[256,384]{1,0:T(8,128)(2,1)S(1)}) custom-call(s32[1,3]{1,0:T(1,128)S(1)} %copy-done.12, s32[1]{0:T(128)} %bitcast.1.me_ref, f32[1,8]{1,0:T(1,128)S(1)} %bitcast.23, f32[1,8]{1,0:T(1,128)S(1)} %bitcast.24, bf16[256,768]{1,0:T(8,128)(2,1)S(1)} %bitcast.20, ...), custom_call_target="tpu_custom_call" | custom-call | flops 400000000 | bytes 1500000 | tf_op jit(solution)/shard_map/inner/pallas_call | solution.py:419
  65.3 0.0 copy-start.2
  65.3 0.8 copy-done.2
  66.2 1.4 %all-to-all-done.1.recv_ref = bf16[64,8,1024]{2,1,0:T(8,128)(2,1)S(1)} async-done(((bf16[64,8,1024]{2,1,0:T(8,128)(2,1)}), bf16[64,8,1024]{2,1,0:T(8,128)(2,1)S(1)}, u32[]{:S(2)}, u32[]{:S(2)}) %all-to-all-start.1) | async-done | bytes 1048608 | tf_op jit(solution)/shard_map/local/all_to_all | solution.py:352
  67.6 2.1 %combine.1 = bf16[64,8,768]{2,1,0:T(8,128)(2,1)} custom-call(s32[192]{0:T(256)S(1)} %copy-done.11, s32[192]{0:T(256)S(1)} %fusion.4.place_ref, bf16[256,384]{1,0:T(8,128)(2,1)S(1)} %get-tuple-element.25.after_ref.read_ref, bf16[64,8,1024]{2,1,0:T(8,128)(2,1)S(1)} %all-to-all-done.1.recv_ref), custom_call_target="tpu_custom_call" | custom-call | bytes 4000000 | tf_op jit(solution)/shard_map/combine/pallas_call | solution.py:436
  69.7 12.1 %all-to-all-start.2 = ((bf16[64,8,768]{2,1,0:T(8,128)(2,1)}), bf16[64,8,768]{2,1,0:T(8,128)(2,1)S(1)}, u32[]{:S(2)}, u32[]{:S(2)}) async-start(bf16[64,8,768]{2,1,0:T(8,128)(2,1)} %combine.1), calls=%async_computation.2 | async-start | bytes 1572864 | tf_op jit(solution)/shard_map/combine/all_to_all | solution.py:352
  81.8 0.0 copy-done.18
  81.8 0.0 copy-start.16
  81.9 0.7 copy-done.16
  82.5 0.1 reshape.137
  82.6 0.6 copy-done.19
  83.2 0.0 copy-done.17
  83.2 0.1 reshape.139
  83.3 0.6 copy-done.9
  83.9 0.1 mul.111
  84.0 0.1 broadcast_multiply_fusion
  84.0 1.3 %multiply_add_fusion = f32[2,8,64,128]{3,2,1,0:T(8,128)S(1)} fusion(f32[2,8,64,128]{3,2,1,0:T(8,128)} %param.32, f32[2,128]{1,0:T(2,128)S(1)} %convert_element_type.20, f32[2,8,64]{2,1,0:T(8,128)S(1)} %broadcast_multiply_fusion, f32[2,8]{1,0:T(2,128)S(1)} %get-tuple-element.28), kind=kLoop, calls=%fused_computation | loop fusion | flops 393216 | bytes 1053760 | tf_op jit(solution)/shard_map/add | solution.py:311
  85.3 0.0 copy-start.14
  85.3 0.7 fusion.5
  86.0 0.2 multiply_reduce_fusion
  86.2 0.0 copy-done.14
  86.2 0.1 multiply_convert_fusion
  86.3 0.7 convert_element_type.22
  87.0 0.6 fusion.7
  88.3 18.7 %all-to-all-done.2 = bf16[64,8,768]{2,1,0:T(8,128)(2,1)S(1)} async-done(((bf16[64,8,768]{2,1,0:T(8,128)(2,1)}), bf16[64,8,768]{2,1,0:T(8,128)(2,1)S(1)}, u32[]{:S(2)}, u32[]{:S(2)}) %all-to-all-start.2) | async-done | bytes 786464 | tf_op jit(solution)/shard_map/combine/all_to_all | solution.py:352
  107.0 1.1 outputs.3
  108.0 0.1 copy-done.3
  108.1 1.1 %outputs.2 = bf16[256,512]{1,0:T(8,128)(2,1)} custom-call(f32[1,512]{1,0:T(1,128)S(1)} %bitcast.21, f32[256,512]{1,0:T(8,128)S(1)} %get-tuple-element.23.base_ref, f32[256,512]{1,0:T(8,128)S(1)} %copy-done.3, bf16[256,384]{1,0:T(8,128)(2,1)S(1)} %get-tuple-element.25.after_ref.read_ref, bf16[512,768]{1,0:T(8,128)(2,1)S(1)} %bitcast.16), custom_call_target="tpu_custom_call" | custom-call | flops 200000000 | bytes 1500000 | tf_op jit(solution)/shard_map/outputs/pallas_call | solution.py:450
  (19 shorter events, 0.1 us)
Async XLA Ops:
  0.6 84.7 %copy-start = (bf16[2,128]{1,0:T(2,128)(2,1)S(1)}, bf16[2,128]{1,0:T(2,128)(2,1)}, u32[]{:S(2)}) copy-start(bf16[2,128]{1,0:T(2,128)(2,1)} %param.30) | copy-start | bytes 1540
  0.6 7.8 %copy-start.1 = (f32[4,8,64,128]{3,2,1,0:T(8,128)S(1)}, f32[4,8,64,128]{3,2,1,0:T(8,128)}, u32[]{:S(2)}) copy-start(f32[4,8,64,128]{3,2,1,0:T(8,128)} %param.26) | copy-start | bytes 3145732
  0.7 1.0 copy-start.5
  1.7 0.8 copy-start.6
  2.5 0.7 copy-start.8
  4.1 13.3 %all-to-all-start = ((bf16[8,32,768]{2,1,0:T(8,128)(2,1)}), bf16[8,32,768]{2,1,0:T(8,128)(2,1)S(1)}, u32[]{:S(2)}, u32[]{:S(2)}) async-start(bf16[8,32,768]{2,1,0:T(8,128)(2,1)} %tokens.1), calls=%async_computation | async-start | bytes 786432 | tf_op jit(solution)/shard_map/tokens/all_to_all | solution.py:352
  17.4 0.7 copy-start.10
  17.4 0.7 copy-start.12
  20.7 16.6 %copy-start.4 = (bf16[32,4096]{1,0:T(8,128)(2,1)S(1)}, bf16[32,4096]{1,0:T(8,128)(2,1)}, u32[]{:S(2)}) copy-start(bf16[32,4096]{1,0:T(8,128)(2,1)} %z_ref.1) | copy-start | bytes 786436
  20.7 16.6 %copy-start.7 = (bf16[32,1024]{1,0:T(8,128)(2,1)S(1)}, bf16[32,1024]{1,0:T(8,128)(2,1)}, u32[]{:S(2)}) copy-start(bf16[32,1024]{1,0:T(8,128)(2,1)} %c_ref.1) | copy-start | bytes 196612
  20.7 46.9 %all-to-all-start.1 = ((bf16[64,8,1024]{2,1,0:T(8,128)(2,1)}), bf16[64,8,1024]{2,1,0:T(8,128)(2,1)S(1)}, u32[]{:S(2)}, u32[]{:S(2)}) async-start(bf16[64,8,1024]{2,1,0:T(8,128)(2,1)} %bitcast.6), calls=%async_computation.1 | async-start | bytes 2097152 | tf_op jit(solution)/shard_map/local/all_to_all | solution.py:352
  37.7 4.4 %copy-start.15 = (s32[192]{0:T(256)S(1)}, s32[192]{0:T(256)}, u32[]{:S(2)}) copy-start(s32[192]{0:T(256)} %param.25) | copy-start | bytes 2308
  37.7 14.8 %collective-permute-start = (bf16[32,640]{1,0:T(8,128)(2,1)S(1)}, bf16[32,640]{1,0:T(8,128)(2,1)S(1)}, u32[]{:S(2)}, u32[]{:S(2)}) collective-permute-start(bf16[32,640]{1,0:T(8,128)(2,1)S(1)} %get-tuple-element.16), channel_id=1, source_target_pairs={{0,1},{1,0},{2,3},{3,2},{4,5},{5,4},{6,7},{7,6},{8,9},{9,8},{10,11... | collective-permute-start | bytes 122888 | tf_op jit(solution)/shard_map/gates/ppermute | solution.py:415
  39.6 15.9 %collective-permute-start.1 = (bf16[32,640]{1,0:T(8,128)(2,1)S(1)}, bf16[32,640]{1,0:T(8,128)(2,1)S(1)}, u32[]{:S(2)}, u32[]{:S(2)}) collective-permute-start(bf16[32,640]{1,0:T(8,128)(2,1)S(1)} %get-tuple-element.17), channel_id=1, source_target_pairs={{0,2},{1,3},{2,0},{3,1},{4,6},{5,7},{6,4},{7,5},{8,10},{9,11},{10,... | collective-permute-start | bytes 122888 | tf_op jit(solution)/shard_map/gates/ppermute | solution.py:415
  42.3 17.1 %collective-permute-start.2 = (bf16[32,640]{1,0:T(8,128)(2,1)S(1)}, bf16[32,640]{1,0:T(8,128)(2,1)S(1)}, u32[]{:S(2)}, u32[]{:S(2)}) collective-permute-start(bf16[32,640]{1,0:T(8,128)(2,1)S(1)} %get-tuple-element.18), channel_id=1, source_target_pairs={{0,3},{1,2},{2,1},{3,0},{4,7},{5,6},{6,5},{7,4},{8,11},{9,10},{10,... | collective-permute-start | bytes 122888 | tf_op jit(solution)/shard_map/gates/ppermute | solution.py:415
  45.5 13.9 %collective-permute-start.3 = (bf16[32,640]{1,0:T(8,128)(2,1)S(1)}, bf16[32,640]{1,0:T(8,128)(2,1)S(1)}, u32[]{:S(2)}, u32[]{:S(2)}) collective-permute-start(bf16[32,640]{1,0:T(8,128)(2,1)S(1)} %get-tuple-element.19), channel_id=1, source_target_pairs={{0,4},{1,5},{2,6},{3,7},{4,0},{5,1},{6,2},{7,3},{8,12},{9,13},{10,... | collective-permute-start | bytes 122888 | tf_op jit(solution)/shard_map/gates/ppermute | solution.py:415
  48.3 11.1 %collective-permute-start.4 = (bf16[32,640]{1,0:T(8,128)(2,1)S(1)}, bf16[32,640]{1,0:T(8,128)(2,1)S(1)}, u32[]{:S(2)}, u32[]{:S(2)}) collective-permute-start(bf16[32,640]{1,0:T(8,128)(2,1)S(1)} %get-tuple-element.20), channel_id=1, source_target_pairs={{0,5},{1,4},{2,7},{3,6},{4,1},{5,0},{6,3},{7,2},{8,13},{9,12},{10,... | collective-permute-start | bytes 122888 | tf_op jit(solution)/shard_map/gates/ppermute | solution.py:415
  52.5 7.1 %collective-permute-start.5 = (bf16[32,640]{1,0:T(8,128)(2,1)S(1)}, bf16[32,640]{1,0:T(8,128)(2,1)S(1)}, u32[]{:S(2)}, u32[]{:S(2)}) collective-permute-start(bf16[32,640]{1,0:T(8,128)(2,1)S(1)} %get-tuple-element.21), channel_id=1, source_target_pairs={{0,6},{1,7},{2,4},{3,5},{4,2},{5,3},{6,0},{7,1},{8,14},{9,15},{10,... | collective-permute-start | bytes 122888 | tf_op jit(solution)/shard_map/gates/ppermute | solution.py:415
  55.6 6.7 %collective-permute-start.6 = (bf16[32,640]{1,0:T(8,128)(2,1)S(1)}, bf16[32,640]{1,0:T(8,128)(2,1)S(1)}, u32[]{:S(2)}, u32[]{:S(2)}) collective-permute-start(bf16[32,640]{1,0:T(8,128)(2,1)S(1)} %get-tuple-element.22), channel_id=1, source_target_pairs={{0,7},{1,6},{2,5},{3,4},{4,3},{5,2},{6,1},{7,0},{8,15},{9,14},{10,... | collective-permute-start | bytes 122888 | tf_op jit(solution)/shard_map/gates/ppermute | solution.py:415
  62.2 0.7 copy-start.13
  65.3 0.8 copy-start.2
  66.2 1.5 %copy-start.11 = (s32[192]{0:T(256)S(1)}, s32[192]{0:T(256)}, u32[]{:S(2)}) copy-start(s32[192]{0:T(256)} %hit_ref.1) | copy-start | bytes 2308
  69.7 12.1 %copy-start.18 = (bf16[2,8]{1,0:T(2,128)(2,1)S(1)}, bf16[2,8]{1,0:T(2,128)(2,1)}, u32[]{:S(2)}) copy-start(bf16[2,8]{1,0:T(2,128)(2,1)} %param.31) | copy-start | bytes 100
  69.7 13.4 %copy-start.17 = (bf16[2,512]{1,0:T(2,128)(2,1)S(1)}, bf16[2,512]{1,0:T(2,128)(2,1)}, u32[]{:S(2)}) copy-start(bf16[2,512]{1,0:T(2,128)(2,1)} %param.28) | copy-start | bytes 6148
  69.7 37.2 %all-to-all-start.2 = ((bf16[64,8,768]{2,1,0:T(8,128)(2,1)}), bf16[64,8,768]{2,1,0:T(8,128)(2,1)S(1)}, u32[]{:S(2)}, u32[]{:S(2)}) async-start(bf16[64,8,768]{2,1,0:T(8,128)(2,1)} %combine.1), calls=%async_computation.2 | async-start | bytes 1572864 | tf_op jit(solution)/shard_map/combine/all_to_all | solution.py:352
  81.8 0.7 copy-start.16
  82.5 0.7 copy-start.19
  83.2 0.7 copy-start.9
  85.3 0.9 copy-start.14
  107.0 1.2 %copy-start.3 = (f32[256,512]{1,0:T(8,128)S(1)}, f32[256,512]{1,0:T(8,128)}, u32[]{:S(2)}) copy-start(f32[256,512]{1,0:T(8,128)} %copy-done.2) | copy-start | bytes 1572868

commit v2 on v1

--- a/solution.py
+++ b/solution.py
@@ -10,6 +10,7 @@
 REQS = 3
 SLOTS = 4
 ROWS = 8
+STRIDE = 37
 
 f32 = jnp.float32
 bf16 = jnp.bfloat16
@@ -194,18 +195,23 @@
     out_ref[:, REQS * STATE :] = dot(chosen, jnp.ones((STATE, STATE), bf16)).astype(bf16)
 
 
+def partners(count):
+    return [i * STRIDE % count for i in range(count)]
+
+
 def combine(hit_ref, place_ref, after_ref, recv_ref, out_ref, held):
     del after_ref
-    for s in range(recv_ref.shape[0]):
-        block = recv_ref[s, :, 0 : SLOTS * STATE].astype(f32)
+    order = partners(recv_ref.shape[0])
+    for i, s in enumerate(order):
+        block = recv_ref[i, :, 0 : SLOTS * STATE].astype(f32)
         for k in range(SLOTS):
             held[s * SLOTS + k] = block[:, k * STATE : (k + 1) * STATE]
-    for s in range(recv_ref.shape[0]):
-        block = recv_ref[s, :, SLOTS * STATE :].astype(f32)
+    for i, s in enumerate(order):
+        block = recv_ref[i, :, SLOTS * STATE :].astype(f32)
         kept = block[:, REQS * STATE :]
         for j in range(REQS):
             prefix = held[hit_ref[s * REQS + j]]
-            out_ref[s, :, j * STATE : (j + 1) * STATE] = prefix.astype(bf16)
+            out_ref[i, :, j * STATE : (j + 1) * STATE] = prefix.astype(bf16)
             factor = kept[j : j + 1, :] + kept[REQS + j : REQS + j + 1, :]
             new = factor * prefix + block[:, j * STATE : (j + 1) * STATE]
             place = place_ref[s * REQS + j]
@@ -349,7 +355,10 @@
     shape = jax.ShapeDtypeStruct
 
     def swap(value, axis):
-        return lax.all_to_all(value, axis, split_axis=0, concat_axis=0, tiled=True)
+        groups = [partners(n_serve)] if axis == "serve" else None
+        return lax.all_to_all(
+            value, axis, split_axis=0, concat_axis=0, tiled=True, axis_index_groups=groups
+        )
 
     with jax.named_scope("tokens"):
         first = pl.pallas_call(
@@ -362,7 +371,7 @@
                 pltpu.VMEM((n_head, rows, STATE), bf16),
                 pltpu.SemaphoreType.DMA((2, n_head + 1)),
             ],
-            compiler_params=params(),
+            compiler_params=params(56),
             cost_estimate=cost(0, 800_000),
         )(pre_x, pre_b, pre_dt)
         tokens = swap(first, "head").reshape(length, width + 2 * STATE)
@@ -381,7 +390,8 @@
         rank = jnp.sum(
             (snapshot_slots[None, :] < snapshot_slots[:, None]).astype(jnp.int32), axis=1
         )
-        place = (rank // REQS) * 4 + rank % REQS
+        seat = (rank // REQS) * pow(STRIDE, -1, n_serve) % n_serve
+        place = seat * 4 + rank % REQS
         serve_me = lax.axis_index("serve")
         missing = (
             sum(range(SLOTS))

time: 110 us -> 119 us (1.082)
  the two profiles are of different devices: /device:TPU:16 before, /device:TPU:8 now
where the time goes in v2:
time: 119 us; the launch traced here: 118 us
  starting transfers between devices  53.6 us (45%)
  waiting for transfers between devices  32.9 us (28%)
  Pallas kernels  21.8 us (18%)
  local copies, waits for them, and re-layouts  5 us (4%)
  other arithmetic  2.45 us (2%)
  between operations  1.56 us (1%)
    all_to_all x3, starting transfers between devices, swap(): lax.all_to_all(value, axis, split_axis=0, concat_axis=0, tiled=True, axis...  32.2 us
    all_to_all x3, waiting for transfers between devices, swap(): lax.all_to_all(value, axis, split_axis=0, concat_axis=0, tiled=True, axis...  30.1 us
    ppermute x7, starting transfers between devices, local(): lax.ppermute(mine[k], 'head', [(i, i ^ k) for i in range(n_head)])  21.4 us
    pallas_call x1, Pallas kernels, local(): pl.pallas_call(pack_first, out_shape=shape((n_head, rows, width + 2 * STA...  11.2 us
    unnamed x34, local copies, waits for them, and re-layouts  4.1 us
    ppermute x7, waiting for transfers between devices, local(): lax.ppermute(mine[k], 'head', [(i, i ^ k) for i in range(n_head)])  2.81 us
    pallas_call x1, Pallas kernels, local(): pl.pallas_call(local_state, out_shape=shape((width, tiles * STATE), bf16)...  2.61 us
    pallas_call x1, Pallas kernels, local(): pl.pallas_call(token_inner, out_shape=(shape((length, width), f32), shape...  2.45 us
  transfers between devices with their start and end apart: 10, of which 5 were waited for; matrix products, arithmetic and copies ran while one was open for 3% of the time, Pallas kernels for 3%

profile of v2, /device:TPU:8, one launch (start us, length us, event | category | flops | bytes accessed | tf_op | source)
XLA Modules:
  0.0 118.1 jit_solution(11368563027508854321)
XLA Ops:
  0.6 0.0 copy-start
  0.6 0.0 copy-start.1
  0.7 11.2 %tokens.1 = bf16[8,32,768]{2,1,0:T(8,128)(2,1)} custom-call(bf16[32,4096]{1,0:T(8,128)(2,1)} %x_ref.1, bf16[32,1024]{1,0:T(8,128)(2,1)} %b_ref.1, bf16[32,64]{1,0:T(8,128)(2,1)} %dt_ref.1), custom_call_target="tpu_custom_call" | custom-call | bytes 800000 | tf_op jit(solution)/shard_map/tokens/pallas_call | solution.py:364
  11.9 4.3 %all-to-all-start = ((bf16[8,32,768]{2,1,0:T(8,128)(2,1)}), bf16[8,32,768]{2,1,0:T(8,128)(2,1)S(1)}, u32[]{:S(2)}, u32[]{:S(2)}) async-start(bf16[8,32,768]{2,1,0:T(8,128)(2,1)} %tokens.1), calls=%async_computation | async-start | bytes 786432 | tf_op jit(solution)/shard_map/tokens/all_to_all | solution.py:359
  16.2 0.0 copy-done.1
  16.2 0.9 cache.1.send_ref
  17.0 8.1 %all-to-all-done = bf16[8,32,768]{2,1,0:T(8,128)(2,1)S(1)} async-done(((bf16[8,32,768]{2,1,0:T(8,128)(2,1)}), bf16[8,32,768]{2,1,0:T(8,128)(2,1)S(1)}, u32[]{:S(2)}, u32[]{:S(2)}) %all-to-all-start) | async-done | bytes 393248 | tf_op jit(solution)/shard_map/tokens/all_to_all | solution.py:359
  25.1 0.0 copy-start.7
  25.1 0.0 copy-start.9
  25.1 0.7 copy-done.7
  25.8 0.0 copy-done.9
  25.8 2.6 %local.1.after_ref = bf16[512,1024]{1,0:T(8,128)(2,1)} custom-call(s32[1,3]{1,0:T(1,128)S(1)} %copy-done.9, f32[1,8]{1,0:T(1,128)S(1)} %bitcast.22, bf16[256,768]{1,0:T(8,128)(2,1)S(1)} %bitcast.19, bf16[512,1024]{1,0:T(8,128)(2,1)} %cache.1.send_ref), custom_call_target="tpu_custom_call", output_to_operand_aliasing={{}: (3, {})} | custom-call | flops 300000000 | bytes 800000 | tf_op jit(solution)/shard_map/local/pallas_call | solution.py:403
  28.4 16.9 %all-to-all-start.1 = ((bf16[64,8,1024]{2,1,0:T(8,128)(2,1)}), bf16[64,8,1024]{2,1,0:T(8,128)(2,1)S(1)}, u32[]{:S(2)}, u32[]{:S(2)}) async-start(bf16[64,8,1024]{2,1,0:T(8,128)(2,1)} %bitcast.6), calls=%async_computation.1 | async-start | bytes 2097152 | tf_op jit(solution)/shard_map/local/all_to_all | solution.py:359
  45.3 0.0 copy-done.4
  45.3 0.0 copy-done.5
  45.3 0.3 gates.1
  45.6 0.0 copy-start.12
  45.6 1.9 %collective-permute-start = (bf16[32,640]{1,0:T(8,128)(2,1)S(1)}, bf16[32,640]{1,0:T(8,128)(2,1)S(1)}, u32[]{:S(2)}, u32[]{:S(2)}) collective-permute-start(bf16[32,640]{1,0:T(8,128)(2,1)S(1)} %get-tuple-element.16), channel_id=1, source_target_pairs={{0,1},{1,0},{2,3},{3,2},{4,5},{5,4},{6,7},{7,6},{8,9},{9,8},{10,11... | collective-permute-start | bytes 122888 | tf_op jit(solution)/shard_map/gates/ppermute | solution.py:425
  47.6 2.5 %collective-permute-start.1 = (bf16[32,640]{1,0:T(8,128)(2,1)S(1)}, bf16[32,640]{1,0:T(8,128)(2,1)S(1)}, u32[]{:S(2)}, u32[]{:S(2)}) collective-permute-start(bf16[32,640]{1,0:T(8,128)(2,1)S(1)} %get-tuple-element.17), channel_id=1, source_target_pairs={{0,2},{1,3},{2,0},{3,1},{4,6},{5,7},{6,4},{7,5},{8,10},{9,11},{10,... | collective-permute-start | bytes 122888 | tf_op jit(solution)/shard_map/gates/ppermute | solution.py:425
  50.1 0.0 copy-done.12
  50.1 0.2 convert_reduce_fusion
  50.3 3.2 %collective-permute-start.2 = (bf16[32,640]{1,0:T(8,128)(2,1)S(1)}, bf16[32,640]{1,0:T(8,128)(2,1)S(1)}, u32[]{:S(2)}, u32[]{:S(2)}) collective-permute-start(bf16[32,640]{1,0:T(8,128)(2,1)S(1)} %get-tuple-element.18), channel_id=1, source_target_pairs={{0,3},{1,2},{2,1},{3,0},{4,7},{5,6},{6,5},{7,4},{8,11},{9,10},{10,... | collective-permute-start | bytes 122888 | tf_op jit(solution)/shard_map/gates/ppermute | solution.py:425
  53.5 2.8 %collective-permute-start.3 = (bf16[32,640]{1,0:T(8,128)(2,1)S(1)}, bf16[32,640]{1,0:T(8,128)(2,1)S(1)}, u32[]{:S(2)}, u32[]{:S(2)}) collective-permute-start(bf16[32,640]{1,0:T(8,128)(2,1)S(1)} %get-tuple-element.19), channel_id=1, source_target_pairs={{0,4},{1,5},{2,6},{3,7},{4,0},{5,1},{6,2},{7,3},{8,12},{9,13},{10,... | collective-permute-start | bytes 122888 | tf_op jit(solution)/shard_map/gates/ppermute | solution.py:425
  56.3 4.2 %collective-permute-start.4 = (bf16[32,640]{1,0:T(8,128)(2,1)S(1)}, bf16[32,640]{1,0:T(8,128)(2,1)S(1)}, u32[]{:S(2)}, u32[]{:S(2)}) collective-permute-start(bf16[32,640]{1,0:T(8,128)(2,1)S(1)} %get-tuple-element.20), channel_id=1, source_target_pairs={{0,5},{1,4},{2,7},{3,6},{4,1},{5,0},{6,3},{7,2},{8,13},{9,12},{10,... | collective-permute-start | bytes 122888 | tf_op jit(solution)/shard_map/gates/ppermute | solution.py:425
  60.4 0.0 collective-permute-done.refs_1_
  60.4 3.1 %collective-permute-start.5 = (bf16[32,640]{1,0:T(8,128)(2,1)S(1)}, bf16[32,640]{1,0:T(8,128)(2,1)S(1)}, u32[]{:S(2)}, u32[]{:S(2)}) collective-permute-start(bf16[32,640]{1,0:T(8,128)(2,1)S(1)} %get-tuple-element.21), channel_id=1, source_target_pairs={{0,6},{1,7},{2,4},{3,5},{4,2},{5,3},{6,0},{7,1},{8,14},{9,15},{10,... | collective-permute-start | bytes 122888 | tf_op jit(solution)/shard_map/gates/ppermute | solution.py:425
  63.5 0.0 collective-permute-done.1.refs_2_
  63.5 3.8 %collective-permute-start.6 = (bf16[32,640]{1,0:T(8,128)(2,1)S(1)}, bf16[32,640]{1,0:T(8,128)(2,1)S(1)}, u32[]{:S(2)}, u32[]{:S(2)}) collective-permute-start(bf16[32,640]{1,0:T(8,128)(2,1)S(1)} %get-tuple-element.22), channel_id=1, source_target_pairs={{0,7},{1,6},{2,5},{3,4},{4,3},{5,2},{6,1},{7,0},{8,15},{9,14},{10,... | collective-permute-start | bytes 122888 | tf_op jit(solution)/shard_map/gates/ppermute | solution.py:425
  67.4 0.0 collective-permute-done.2.refs_3_
  67.4 0.0 collective-permute-done.3.refs_4_
  67.4 0.0 collective-permute-done.4.refs_5_
  67.4 0.1 collective-permute-done.5.refs_6_
  67.5 2.6 %collective-permute-done.6.refs_7_ = bf16[32,640]{1,0:T(8,128)(2,1)S(1)} collective-permute-done((bf16[32,640]{1,0:T(8,128)(2,1)S(1)}, bf16[32,640]{1,0:T(8,128)(2,1)S(1)}, u32[]{:S(2)}, u32[]{:S(2)}) %collective-permute-start.6) | collective-permute-done | bytes 40992 | tf_op jit(solution)/shard_map/gates/ppermute | solution.py:425
  70.2 0.7 copy-done.10
  70.8 2.5 %inner.1 = (f32[256,512]{1,0:T(8,128)S(1)}, f32[256,512]{1,0:T(8,128)S(1)}, bf16[256,384]{1,0:T(8,128)(2,1)S(1)}) custom-call(s32[1,3]{1,0:T(1,128)S(1)} %copy-done.9, s32[1]{0:T(128)} %bitcast.1.me_ref, f32[1,8]{1,0:T(1,128)S(1)} %bitcast.23, f32[1,8]{1,0:T(1,128)S(1)} %bitcast.24, bf16[256,768]{1,0:T(8,128)(2,1)S(1)} %bitcast.20, ...), custom_call_target="tpu_custom_call" | custom-call | flops 400000000 | bytes 1500000 | tf_op jit(solution)/shard_map/inner/pallas_call | solution.py:429
  73.3 0.0 copy-start.2
  73.3 0.8 copy-done.2
  74.1 2.4 %all-to-all-done.1.recv_ref = bf16[64,8,1024]{2,1,0:T(8,128)(2,1)S(1)} async-done(((bf16[64,8,1024]{2,1,0:T(8,128)(2,1)}), bf16[64,8,1024]{2,1,0:T(8,128)(2,1)S(1)}, u32[]{:S(2)}, u32[]{:S(2)}) %all-to-all-start.1) | async-done | bytes 1048608 | tf_op jit(solution)/shard_map/local/all_to_all | solution.py:359
  76.5 0.0 copy-done.8
  76.5 2.1 %combine.1 = bf16[64,8,768]{2,1,0:T(8,128)(2,1)} custom-call(s32[192]{0:T(256)S(1)} %copy-done.8, s32[192]{0:T(256)S(1)} %fusion.5.place_ref, bf16[256,384]{1,0:T(8,128)(2,1)S(1)} %get-tuple-element.25.after_ref.read_ref, bf16[64,8,1024]{2,1,0:T(8,128)(2,1)S(1)} %all-to-all-done.1.recv_ref), custom_call_target="tpu_custom_call" | custom-call | bytes 4000000 | tf_op jit(solution)/shard_map/combine/pallas_call | solution.py:446
  78.6 11.0 %all-to-all-start.2 = ((bf16[64,8,768]{2,1,0:T(8,128)(2,1)}), bf16[64,8,768]{2,1,0:T(8,128)(2,1)S(1)}, u32[]{:S(2)}, u32[]{:S(2)}) async-start(bf16[64,8,768]{2,1,0:T(8,128)(2,1)} %combine.1), calls=%async_computation.2 | async-start | bytes 1572864 | tf_op jit(solution)/shard_map/combine/all_to_all | solution.py:359
  89.7 0.0 copy-done.15
  89.7 0.0 copy-start.13
  89.7 0.7 copy-done.13
  90.4 0.1 reshape.137
  90.5 0.6 copy-done.16
  91.0 0.0 copy-done.14
  91.1 0.1 reshape.139
  91.1 0.6 copy-done.6
  91.7 0.1 mul.119
  91.8 0.1 broadcast_multiply_fusion
  91.9 1.3 %multiply_add_fusion = f32[2,8,64,128]{3,2,1,0:T(8,128)S(1)} fusion(f32[2,8,64,128]{3,2,1,0:T(8,128)} %param.32, f32[2,128]{1,0:T(2,128)S(1)} %convert_element_type.20, f32[2,8,64]{2,1,0:T(8,128)S(1)} %broadcast_multiply_fusion, f32[2,8]{1,0:T(2,128)S(1)} %get-tuple-element.28), kind=kLoop, calls=%fused_computation | loop fusion | flops 393216 | bytes 1053760 | tf_op jit(solution)/shard_map/add | solution.py:317
  93.1 0.0 copy-done
  93.2 0.0 copy-start.11
  93.2 0.7 fusion.7
  93.9 0.2 multiply_reduce_fusion
  94.1 0.0 copy-done.11
  94.1 0.1 multiply_convert_fusion
  94.1 0.7 convert_element_type.22
  94.8 0.6 fusion.9
  96.1 19.7 %all-to-all-done.2 = bf16[64,8,768]{2,1,0:T(8,128)(2,1)S(1)} async-done(((bf16[64,8,768]{2,1,0:T(8,128)(2,1)}), bf16[64,8,768]{2,1,0:T(8,128)(2,1)S(1)}, u32[]{:S(2)}, u32[]{:S(2)}) %all-to-all-start.2) | async-done | bytes 786464 | tf_op jit(solution)/shard_map/combine/all_to_all | solution.py:359
  115.8 1.1 outputs.3
  116.9 0.1 copy-done.3
  116.9 1.1 outputs.2
  (13 shorter events, 0.1 us)
Async XLA Ops:
  0.6 92.5 %copy-start = (bf16[2,128]{1,0:T(2,128)(2,1)S(1)}, bf16[2,128]{1,0:T(2,128)(2,1)}, u32[]{:S(2)}) copy-start(bf16[2,128]{1,0:T(2,128)(2,1)} %param.30) | copy-start | bytes 1540
  0.6 15.5 %copy-start.1 = (f32[4,8,64,128]{3,2,1,0:T(8,128)S(1)}, f32[4,8,64,128]{3,2,1,0:T(8,128)}, u32[]{:S(2)}) copy-start(f32[4,8,64,128]{3,2,1,0:T(8,128)} %param.26) | copy-start | bytes 3145732
  11.9 13.3 %all-to-all-start = ((bf16[8,32,768]{2,1,0:T(8,128)(2,1)}), bf16[8,32,768]{2,1,0:T(8,128)(2,1)S(1)}, u32[]{:S(2)}, u32[]{:S(2)}) async-start(bf16[8,32,768]{2,1,0:T(8,128)(2,1)} %tokens.1), calls=%async_computation | async-start | bytes 786432 | tf_op jit(solution)/shard_map/tokens/all_to_all | solution.py:359
  25.1 0.7 copy-start.7
  25.1 0.7 copy-start.9
  28.4 16.9 %copy-start.4 = (bf16[32,4096]{1,0:T(8,128)(2,1)S(1)}, bf16[32,4096]{1,0:T(8,128)(2,1)}, u32[]{:S(2)}) copy-start(bf16[32,4096]{1,0:T(8,128)(2,1)} %z_ref.1) | copy-start | bytes 786436
  28.4 16.9 %copy-start.5 = (bf16[32,1024]{1,0:T(8,128)(2,1)S(1)}, bf16[32,1024]{1,0:T(8,128)(2,1)}, u32[]{:S(2)}) copy-start(bf16[32,1024]{1,0:T(8,128)(2,1)} %c_ref.1) | copy-start | bytes 196612
  28.4 48.1 %all-to-all-start.1 = ((bf16[64,8,1024]{2,1,0:T(8,128)(2,1)}), bf16[64,8,1024]{2,1,0:T(8,128)(2,1)S(1)}, u32[]{:S(2)}, u32[]{:S(2)}) async-start(bf16[64,8,1024]{2,1,0:T(8,128)(2,1)} %bitcast.6), calls=%async_computation.1 | async-start | bytes 2097152 | tf_op jit(solution)/shard_map/local/all_to_all | solution.py:359
  45.6 4.4 %copy-start.12 = (s32[192]{0:T(256)S(1)}, s32[192]{0:T(256)}, u32[]{:S(2)}) copy-start(s32[192]{0:T(256)} %param.25) | copy-start | bytes 2308
  45.6 14.8 %collective-permute-start = (bf16[32,640]{1,0:T(8,128)(2,1)S(1)}, bf16[32,640]{1,0:T(8,128)(2,1)S(1)}, u32[]{:S(2)}, u32[]{:S(2)}) collective-permute-start(bf16[32,640]{1,0:T(8,128)(2,1)S(1)} %get-tuple-element.16), channel_id=1, source_target_pairs={{0,1},{1,0},{2,3},{3,2},{4,5},{5,4},{6,7},{7,6},{8,9},{9,8},{10,11... | collective-permute-start | bytes 122888 | tf_op jit(solution)/shard_map/gates/ppermute | solution.py:425
  47.6 16.0 %collective-permute-start.1 = (bf16[32,640]{1,0:T(8,128)(2,1)S(1)}, bf16[32,640]{1,0:T(8,128)(2,1)S(1)}, u32[]{:S(2)}, u32[]{:S(2)}) collective-permute-start(bf16[32,640]{1,0:T(8,128)(2,1)S(1)} %get-tuple-element.17), channel_id=1, source_target_pairs={{0,2},{1,3},{2,0},{3,1},{4,6},{5,7},{6,4},{7,5},{8,10},{9,11},{10,... | collective-permute-start | bytes 122888 | tf_op jit(solution)/shard_map/gates/ppermute | solution.py:425
  50.3 17.1 %collective-permute-start.2 = (bf16[32,640]{1,0:T(8,128)(2,1)S(1)}, bf16[32,640]{1,0:T(8,128)(2,1)S(1)}, u32[]{:S(2)}, u32[]{:S(2)}) collective-permute-start(bf16[32,640]{1,0:T(8,128)(2,1)S(1)} %get-tuple-element.18), channel_id=1, source_target_pairs={{0,3},{1,2},{2,1},{3,0},{4,7},{5,6},{6,5},{7,4},{8,11},{9,10},{10,... | collective-permute-start | bytes 122888 | tf_op jit(solution)/shard_map/gates/ppermute | solution.py:425
  53.5 13.9 %collective-permute-start.3 = (bf16[32,640]{1,0:T(8,128)(2,1)S(1)}, bf16[32,640]{1,0:T(8,128)(2,1)S(1)}, u32[]{:S(2)}, u32[]{:S(2)}) collective-permute-start(bf16[32,640]{1,0:T(8,128)(2,1)S(1)} %get-tuple-element.19), channel_id=1, source_target_pairs={{0,4},{1,5},{2,6},{3,7},{4,0},{5,1},{6,2},{7,3},{8,12},{9,13},{10,... | collective-permute-start | bytes 122888 | tf_op jit(solution)/shard_map/gates/ppermute | solution.py:425
  56.3 11.1 %collective-permute-start.4 = (bf16[32,640]{1,0:T(8,128)(2,1)S(1)}, bf16[32,640]{1,0:T(8,128)(2,1)S(1)}, u32[]{:S(2)}, u32[]{:S(2)}) collective-permute-start(bf16[32,640]{1,0:T(8,128)(2,1)S(1)} %get-tuple-element.20), channel_id=1, source_target_pairs={{0,5},{1,4},{2,7},{3,6},{4,1},{5,0},{6,3},{7,2},{8,13},{9,12},{10,... | collective-permute-start | bytes 122888 | tf_op jit(solution)/shard_map/gates/ppermute | solution.py:425
  60.4 7.1 %collective-permute-start.5 = (bf16[32,640]{1,0:T(8,128)(2,1)S(1)}, bf16[32,640]{1,0:T(8,128)(2,1)S(1)}, u32[]{:S(2)}, u32[]{:S(2)}) collective-permute-start(bf16[32,640]{1,0:T(8,128)(2,1)S(1)} %get-tuple-element.21), channel_id=1, source_target_pairs={{0,6},{1,7},{2,4},{3,5},{4,2},{5,3},{6,0},{7,1},{8,14},{9,15},{10,... | collective-permute-start | bytes 122888 | tf_op jit(solution)/shard_map/gates/ppermute | solution.py:425
  63.5 6.7 %collective-permute-start.6 = (bf16[32,640]{1,0:T(8,128)(2,1)S(1)}, bf16[32,640]{1,0:T(8,128)(2,1)S(1)}, u32[]{:S(2)}, u32[]{:S(2)}) collective-permute-start(bf16[32,640]{1,0:T(8,128)(2,1)S(1)} %get-tuple-element.22), channel_id=1, source_target_pairs={{0,7},{1,6},{2,5},{3,4},{4,3},{5,2},{6,1},{7,0},{8,15},{9,14},{10,... | collective-permute-start | bytes 122888 | tf_op jit(solution)/shard_map/gates/ppermute | solution.py:425
  70.2 0.7 copy-start.10
  73.3 0.8 copy-start.2
  74.1 2.4 %copy-start.8 = (s32[192]{0:T(256)S(1)}, s32[192]{0:T(256)}, u32[]{:S(2)}) copy-start(s32[192]{0:T(256)} %hit_ref.1) | copy-start | bytes 2308
  78.6 11.0 %copy-start.15 = (bf16[2,8]{1,0:T(2,128)(2,1)S(1)}, bf16[2,8]{1,0:T(2,128)(2,1)}, u32[]{:S(2)}) copy-start(bf16[2,8]{1,0:T(2,128)(2,1)} %param.31) | copy-start | bytes 100
  78.6 12.4 %copy-start.14 = (bf16[2,512]{1,0:T(2,128)(2,1)S(1)}, bf16[2,512]{1,0:T(2,128)(2,1)}, u32[]{:S(2)}) copy-start(bf16[2,512]{1,0:T(2,128)(2,1)} %param.28) | copy-start | bytes 6148
  78.6 37.2 %all-to-all-start.2 = ((bf16[64,8,768]{2,1,0:T(8,128)(2,1)}), bf16[64,8,768]{2,1,0:T(8,128)(2,1)S(1)}, u32[]{:S(2)}, u32[]{:S(2)}) async-start(bf16[64,8,768]{2,1,0:T(8,128)(2,1)} %combine.1), calls=%async_computation.2 | async-start | bytes 1572864 | tf_op jit(solution)/shard_map/combine/all_to_all | solution.py:359
  89.7 0.7 copy-start.13
  90.4 0.7 copy-start.16
  91.1 0.7 copy-start.6
  93.2 0.9 copy-start.11
  115.8 1.1 copy-start.3

commit v3 on v1

--- a/solution.py
+++ b/solution.py
@@ -66,71 +66,75 @@
     return total
 
 
-def pack_first(x_ref, b_ref, dt_ref, out_ref, steps, held, sems):
-    count = out_ref.shape[0]
-    heads_dev = dt_ref.shape[1] // count
-    width = x_ref.shape[1] // count
+def pack_tokens(me_ref, after_ref, x_ref, b_ref, dt_ref, keep_ref, give_ref):
+    del after_ref
+    chips = keep_ref.shape[0]
+    heads_dev = dt_ref.shape[1] // (2 * chips)
+    width = x_ref.shape[1] // (2 * chips)
+    raw = dt_ref[...].astype(f32)
+    raw = jnp.concatenate([raw, jnp.zeros((raw.shape[0], STATE - raw.shape[1]), f32)], axis=1)
+    for side, ref in enumerate((keep_ref, give_ref)):
+        for k in range(chips):
+            peer = me_ref[0] ^ (2 * k + side)
+            x_start = pl.multiple_of(peer * width, STATE)
+            b_start = pl.multiple_of(peer * STATE, STATE)
+            ref[k, :, 0:width] = x_ref[:, pl.ds(x_start, width)]
+            ref[k, :, width : width + STATE] = b_ref[:, pl.ds(b_start, STATE)]
+            mine = pltpu.roll(raw, (STATE - peer * heads_dev) % STATE, 1)
+            ref[k, :, width + STATE : width + 2 * STATE] = mine.astype(bf16)
+
+
+def pack_gates(me_ref, after_ref, z_ref, c_ref, keep_ref, give_ref):
+    del after_ref
+    chips = keep_ref.shape[0]
+    width = z_ref.shape[1] // (2 * chips)
+    for side, ref in enumerate((keep_ref, give_ref)):
+        for k in range(chips):
+            peer = me_ref[0] ^ (2 * k + side)
+            z_start = pl.multiple_of(peer * width, STATE)
+            c_start = pl.multiple_of(peer * STATE, STATE)
+            ref[k, :, 0:width] = z_ref[:, pl.ds(z_start, width)]
+            ref[k, :, width : width + STATE] = c_ref[:, pl.ds(c_start, STATE)]
+
+
+def pair_up(keep_ref, got_ref, *out_refs):
+    for k, ref in enumerate(out_refs):
+        ref[0] = keep_ref[k]
+        ref[1] = got_ref[k]
+
+
+def exchange(keep, give, n_head):
+    chips = n_head // 2
+    shape = jax.ShapeDtypeStruct((2,) + keep.shape[1:], bf16)
+    got = lax.ppermute(give, "head", [(i, i ^ 1) for i in range(n_head)])
+    pairs = pl.pallas_call(
+        pair_up,
+        out_shape=[shape] * chips,
+        in_specs=[VMEM] * 2,
+        out_specs=[VMEM] * chips,
+        compiler_params=params(),
+        cost_estimate=cost(0, 800_000),
+    )(keep, got)
+    return [pairs[0]] + [
+        lax.ppermute(pairs[k], "head", [(i, i ^ (2 * k)) for i in range(n_head)])
+        for k in range(1, chips)
+    ]
+
+
+def fetch(me, pair_refs, rows_ref, sems):
+    rows = pair_refs[0].shape[1]
     copies = []
-    for d in range(count):
-        copies.append(
-            pltpu.make_async_copy(
-                x_ref.at[:, d * width : (d + 1) * width],
-                out_ref.at[d, :, 0:width],
-                sems.at[0, d],
+    for k, ref in enumerate(pair_refs):
+        for side in range(2):
+            start = pl.multiple_of((me ^ (2 * k + side)) * rows, rows)
+            copies.append(
+                pltpu.make_async_copy(
+                    ref.at[side], rows_ref.at[pl.ds(start, rows), :], sems.at[2 * k + side]
+                )
             )
-        )
-        copies.append(
-            pltpu.make_async_copy(
-                b_ref.at[:, d * STATE : (d + 1) * STATE],
-                out_ref.at[d, :, width : width + STATE],
-                sems.at[1, d],
-            )
-        )
-    early = pltpu.make_async_copy(dt_ref, steps, sems.at[1, count])
-    early.start()
     for copy in copies:
         copy.start()
-    early.wait()
-    raw = steps[...].astype(f32)
-    raw = jnp.concatenate([raw, jnp.zeros((raw.shape[0], STATE - raw.shape[1]), f32)], axis=1)
-    for d in range(count):
-        mine = raw if d == 0 else pltpu.roll(raw, STATE - d * heads_dev, 1)
-        held[d] = mine.astype(bf16)
-    last = pltpu.make_async_copy(
-        held, out_ref.at[:, :, width + STATE : width + 2 * STATE], sems.at[0, count]
-    )
-    last.start()
-    for copy in copies:
-        copy.wait()
-    last.wait()
-
-
-def pack_second(me_ref, after_ref, z_ref, c_ref, *refs):
-    del after_ref
-    out_refs, sems = refs[:-1], refs[-1]
-    count = len(out_refs)
-    width = z_ref.shape[1] // count
-    copies = []
-    for k in range(count):
-        peer = me_ref[0] ^ k
-        z_start = pl.multiple_of(peer * width, STATE)
-        c_start = pl.multiple_of(peer * STATE, STATE)
-        copies.append(
-            pltpu.make_async_copy(
-                z_ref.at[:, pl.ds(z_start, width)], out_refs[k].at[:, 0:width], sems.at[0, k]
-            )
-        )
-        copies.append(
-            pltpu.make_async_copy(
-                c_ref.at[:, pl.ds(c_start, STATE)],
-                out_refs[k].at[:, width : width + STATE],
-                sems.at[1, k],
-            )
-        )
-    for copy in copies:
-        copy.start()
-    for copy in copies:
-        copy.wait()
+    return copies
 
 
 def pack_cache(cache_ref, out_ref):
@@ -153,11 +157,14 @@
     return (row == column // (width // heads)).astype(bf16)
 
 
-def local_state(len_ref, rate_ref, tok_ref, send_ref, out_ref):
+def local_state(len_ref, me_ref, rate_ref, *refs):
+    pair_refs, (send_ref, out_ref, tok_ref, made, sems, last_sem) = refs[:-6], refs[-6:]
     del send_ref
     length = tok_ref.shape[0]
     heads = rate_ref.shape[1]
     width = heads * HEAD_DIM
+    for copy in fetch(me_ref[0], pair_refs, tok_ref, sems):
+        copy.wait()
     ends = segment_ends(len_ref)
     step_size = jax.nn.softplus(tok_ref[:, width + STATE : width + STATE + heads].astype(f32))
     log_decay = -step_size * rate_ref[...]
@@ -174,7 +181,7 @@
     b_parts = jnp.concatenate(
         [jnp.where(seg_index == j, b_half, 0.0).astype(bf16) for j in range(REQS)], axis=1
     )
-    out_ref[:, 0 : REQS * STATE] = dot_tn(scaled, b_parts).astype(bf16)
+    made[:, 0 : REQS * STATE] = dot_tn(scaled, b_parts).astype(bf16)
     member = (seg_index == lane % REQS).astype(f32).astype(bf16)
     total = None
     for piece in split(log_decay, 3):
@@ -191,25 +198,37 @@
     row_s = lax.broadcasted_iota(jnp.int32, (width, STATE), 0)
     lane_s = lax.broadcasted_iota(jnp.int32, (width, STATE), 1)
     chosen = jnp.where(lane_s == row_s % ROWS, spread, 0.0).astype(bf16)
-    out_ref[:, REQS * STATE :] = dot(chosen, jnp.ones((STATE, STATE), bf16)).astype(bf16)
-
-
-def combine(hit_ref, place_ref, after_ref, recv_ref, out_ref, held):
-    del after_ref
+    made[:, REQS * STATE :] = dot(chosen, jnp.ones((STATE, STATE), bf16)).astype(bf16)
+    last = pltpu.make_async_copy(made, out_ref.at[:, REQS * STATE :], last_sem)
+    last.start()
+    last.wait()
+
+
+def pick_prefix(hit_ref, recv_ref, out_ref, picked_ref, held, sem):
     for s in range(recv_ref.shape[0]):
-        block = recv_ref[s, :, 0 : SLOTS * STATE].astype(f32)
+        block = recv_ref[s].astype(f32)
         for k in range(SLOTS):
             held[s * SLOTS + k] = block[:, k * STATE : (k + 1) * STATE]
     for s in range(recv_ref.shape[0]):
-        block = recv_ref[s, :, SLOTS * STATE :].astype(f32)
+        for j in range(REQS):
+            picked_ref[s, :, j * STATE : (j + 1) * STATE] = held[hit_ref[s * REQS + j]].astype(bf16)
+    copy = pltpu.make_async_copy(picked_ref, out_ref.at[:, :, 0 : REQS * STATE], sem)
+    copy.start()
+    copy.wait()
+
+
+def make_snapshots(place_ref, after_ref, picked_ref, recv_ref, out_ref):
+    del after_ref
+    for s in range(recv_ref.shape[0]):
+        prefix = picked_ref[s].astype(f32)
+        block = recv_ref[s, :, REQS * STATE :].astype(f32)
         kept = block[:, REQS * STATE :]
         for j in range(REQS):
-            prefix = held[hit_ref[s * REQS + j]]
-            out_ref[s, :, j * STATE : (j + 1) * STATE] = prefix.astype(bf16)
+            columns = slice(j * STATE, (j + 1) * STATE)
             factor = kept[j : j + 1, :] + kept[REQS + j : REQS + j + 1, :]
-            new = factor * prefix + block[:, j * STATE : (j + 1) * STATE]
+            new = factor * prefix[:, columns] + block[:, columns]
             place = place_ref[s * REQS + j]
-            start = pl.multiple_of((REQS + (place & 3)) * STATE, STATE)
+            start = pl.multiple_of((place & 3) * STATE, STATE)
             out_ref[place >> 2, :, pl.ds(start, STATE)] = new.astype(bf16)
 
 
@@ -225,29 +244,24 @@
 
             @pl.when(missing > s)
             def _():
-                out_ref[s] = recv_ref[:, (REQS + s) * STATE : (REQS + s + 1) * STATE].astype(f32)
+                out_ref[s] = recv_ref[:, s * STATE : (s + 1) * STATE].astype(f32)
 
         if s > 0:
 
             @pl.when(missing < s)
             def _():
-                out_ref[s] = recv_ref[:, (REQS + s - 1) * STATE : (REQS + s) * STATE].astype(f32)
-
-
-def token_inner(len_ref, me_ref, rate_ref, skip_ref, tok_ref, *refs):
-    gate_refs, (base_ref, factor_ref, read_ref, gates, sems) = refs[:-5], refs[-5:]
+                out_ref[s] = recv_ref[:, (s - 1) * STATE : s * STATE].astype(f32)
+
+
+def token_inner(len_ref, me_ref, rate_ref, skip_ref, *refs):
+    pair_refs, (base_ref, factor_ref, read_ref, tok_ref, gates, sems) = refs[:-6], refs[-6:]
+    chips = len(pair_refs) // 2
     length = tok_ref.shape[0]
     heads = rate_ref.shape[1]
     width = heads * HEAD_DIM
-    rows = length // len(gate_refs)
-    copies = []
-    for k in range(len(gate_refs)):
-        start = pl.multiple_of((me_ref[0] ^ k) * rows, rows)
-        copies.append(
-            pltpu.make_async_copy(gate_refs[k], gates.at[pl.ds(start, rows), :], sems.at[k])
-        )
-    for copy in copies:
-        copy.start()
+    for copy in fetch(me_ref[0], pair_refs[:chips], tok_ref, sems.at[0]):
+        copy.wait()
+    copies = fetch(me_ref[0], pair_refs[chips:], gates, sems.at[1])
     ends = segment_ends(len_ref)
     step_size = jax.nn.softplus(tok_ref[:, width + STATE : width + STATE + heads].astype(f32))
     log_decay = -step_size * rate_ref[...]
@@ -345,39 +359,15 @@
     heads = cache_states.shape[1]
     width = heads * HEAD_DIM
     length = rows * n_head
-    tiles = SLOTS + REQS + 1
+    tiles = 2 * REQS + 1
     shape = jax.ShapeDtypeStruct
 
-    def swap(value, axis):
-        return lax.all_to_all(value, axis, split_axis=0, concat_axis=0, tiled=True)
-
-    with jax.named_scope("tokens"):
-        first = pl.pallas_call(
-            pack_first,
-            out_shape=shape((n_head, rows, width + 2 * STATE), bf16),
-            in_specs=[HBM] * 3,
-            out_specs=HBM,
-            scratch_shapes=[
-                pltpu.VMEM(pre_dt.shape, bf16),
-                pltpu.VMEM((n_head, rows, STATE), bf16),
-                pltpu.SemaphoreType.DMA((2, n_head + 1)),
-            ],
-            compiler_params=params(),
-            cost_estimate=cost(0, 800_000),
-        )(pre_x, pre_b, pre_dt)
-        tokens = swap(first, "head").reshape(length, width + 2 * STATE)
-    with jax.named_scope("cache"):
-        cache_rows = cache_states.reshape(SLOTS, width, STATE)
-        send = pl.pallas_call(
-            pack_cache,
-            out_shape=shape((width, tiles * STATE), bf16),
-            grid=(1,),
-            in_specs=[VMEM],
-            out_specs=pl.BlockSpec((width, SLOTS * STATE), lambda i: (0, 0)),
-            compiler_params=params(),
-            cost_estimate=cost(0, 1_600_000),
-        )(cache_rows)
+    def swap(value):
+        return lax.all_to_all(value, "serve", split_axis=0, concat_axis=0, tiled=True)
+
+    chips = n_head // 2
     with jax.named_scope("orders"):
+        head_me = lax.axis_index("head").astype(jnp.int32).reshape(1)
         rank = jnp.sum(
             (snapshot_slots[None, :] < snapshot_slots[:, None]).astype(jnp.int32), axis=1
         )
@@ -387,34 +377,71 @@
             sum(range(SLOTS))
             - jnp.sum(jnp.where(snapshot_slots // SLOTS == serve_me, snapshot_slots % SLOTS, 0))
         ).reshape(1)
-        head_me = lax.axis_index("head").astype(jnp.int32).reshape(1)
+    with jax.named_scope("cache"):
+        cache_rows = cache_states.reshape(SLOTS, width, STATE)
+        spread = pl.pallas_call(
+            pack_cache,
+            out_shape=shape((width, SLOTS * STATE), bf16),
+            in_specs=[VMEM],
+            out_specs=VMEM,
+            compiler_params=params(),
+            cost_estimate=cost(0, 1_600_000),
+        )(cache_rows)
+        pieces = swap(spread.reshape(n_serve, ROWS, SLOTS * STATE))
+    with jax.named_scope("tokens"):
+        keep, give = pl.pallas_call(
+            pack_tokens,
+            out_shape=[shape((chips, rows, width + 2 * STATE), bf16)] * 2,
+            in_specs=[SMEM, ANY] + [VMEM] * 3,
+            out_specs=[VMEM] * 2,
+            compiler_params=params(),
+            cost_estimate=cost(0, 800_000),
+        )(head_me, spread, pre_x, pre_b, pre_dt)
+        tokens = exchange(keep, give, n_head)
     rates = decay_rate.reshape(1, heads)
+    with jax.named_scope("prefix"):
+        send, picked = pl.pallas_call(
+            pick_prefix,
+            out_shape=(
+                shape((n_serve, ROWS, tiles * STATE), bf16),
+                shape((n_serve, ROWS, REQS * STATE), bf16),
+            ),
+            in_specs=[SMEM, VMEM],
+            out_specs=(HBM, VMEM),
+            scratch_shapes=[
+                pltpu.VMEM((n_serve * SLOTS, ROWS, STATE), f32),
+                pltpu.SemaphoreType.DMA,
+            ],
+            compiler_params=params(),
+            cost_estimate=cost(0, 2_000_000),
+        )(prefix_hits, pieces)
     with jax.named_scope("local"):
         send = pl.pallas_call(
             local_state,
             out_shape=shape((width, tiles * STATE), bf16),
-            grid=(1,),
-            in_specs=[SMEM, VMEM, VMEM, ANY],
-            out_specs=pl.BlockSpec((width, SLOTS * STATE), lambda i: (0, 1)),
-            input_output_aliases={3: 0},
+            in_specs=[SMEM] * 2 + [VMEM] + [ANY] * chips + [HBM],
+            out_specs=HBM,
+            scratch_shapes=[
+                pltpu.VMEM((length, width + 2 * STATE), bf16),
+                pltpu.VMEM((width, (REQS + 1) * STATE), bf16),
+                pltpu.SemaphoreType.DMA((n_head,)),
+                pltpu.SemaphoreType.DMA,
+            ],
+            input_output_aliases={3 + chips: 0},
             compiler_params=params(),
             cost_estimate=cost(300_000_000, 800_000),
-        )(suffix_lengths, rates, tokens, send)
-        pieces = swap(send.reshape(n_serve, ROWS, tiles * STATE), "serve")
+        )(suffix_lengths, head_me, rates, *tokens, send.reshape(width, tiles * STATE))
+        got = swap(send.reshape(n_serve, ROWS, tiles * STATE))
     with jax.named_scope("gates"):
-        mine = pl.pallas_call(
-            pack_second,
-            out_shape=[shape((rows, width + STATE), bf16)] * n_head,
-            in_specs=[SMEM, ANY, HBM, HBM],
-            out_specs=[ANY] * n_head,
-            scratch_shapes=[pltpu.SemaphoreType.DMA((2, n_head))],
+        keep, give = pl.pallas_call(
+            pack_gates,
+            out_shape=[shape((chips, rows, width + STATE), bf16)] * 2,
+            in_specs=[SMEM, ANY] + [VMEM] * 2,
+            out_specs=[VMEM] * 2,
             compiler_params=params(),
             cost_estimate=cost(0, 650_000),
         )(head_me, send, pre_z, pre_c)
-        gates = [mine[0]] + [
-            lax.ppermute(mine[k], "head", [(i, i ^ k) for i in range(n_head)])
-            for k in range(1, n_head)
-        ]
+        gates = exchange(keep, give, n_head)
     with jax.named_scope("inner"):
         base, factor, read = pl.pallas_call(
             token_inner,
@@ -423,26 +450,26 @@
                 shape((length, width), f32),
                 shape((length, REQS * STATE), bf16),
             ),
-            in_specs=[SMEM] * 2 + [VMEM] * 3 + [ANY] * n_head,
+            in_specs=[SMEM] * 2 + [VMEM] * 2 + [ANY] * n_head,
             out_specs=[VMEM] * 3,
             scratch_shapes=[
+                pltpu.VMEM((length, width + 2 * STATE), bf16),
                 pltpu.VMEM((length, width + STATE), bf16),
-                pltpu.SemaphoreType.DMA((n_head,)),
+                pltpu.SemaphoreType.DMA((2, n_head)),
             ],
             compiler_params=params(),
             cost_estimate=cost(400_000_000, 1_500_000),
-        )(suffix_lengths, head_me, rates, d_skip.reshape(1, heads), tokens, *gates)
-    with jax.named_scope("combine"):
+        )(suffix_lengths, head_me, rates, d_skip.reshape(1, heads), *tokens, *gates)
+    with jax.named_scope("snapshots"):
         answer = pl.pallas_call(
-            combine,
-            out_shape=shape((n_serve, ROWS, 2 * REQS * STATE), bf16),
-            in_specs=[SMEM, SMEM, ANY, VMEM],
+            make_snapshots,
+            out_shape=shape((n_serve, ROWS, REQS * STATE), bf16),
+            in_specs=[SMEM, ANY, VMEM, VMEM],
             out_specs=VMEM,
-            scratch_shapes=[pltpu.VMEM((n_serve * SLOTS, ROWS, STATE), f32)],
-            compiler_params=params(),
-            cost_estimate=cost(0, 4_000_000),
-        )(prefix_hits, place, read, pieces)
-        got = swap(answer, "serve").reshape(width, 2 * REQS * STATE)
+            compiler_params=params(),
+            cost_estimate=cost(0, 2_000_000),
+        )(place, read, picked, got)
+        new = swap(answer).reshape(width, REQS * STATE)
     dec_out, dec_new = decode_block(
         dec_x, dec_z, dec_b, dec_c, dec_dt, dec_states, decay_rate, d_skip, norm_weight
     )
@@ -454,7 +481,7 @@
             out_specs=VMEM,
             compiler_params=params(),
             cost_estimate=cost(200_000_000, 1_500_000),
-        )(norm_weight.reshape(1, width), base, factor, read, got)
+        )(norm_weight.reshape(1, width), base, factor, read, got.reshape(width, tiles * STATE))
         cache_out = pl.pallas_call(
             write_cache,
             out_shape=shape((SLOTS, width, STATE), f32),
@@ -462,7 +489,7 @@
             out_specs=VMEM,
             compiler_params=params(),
             cost_estimate=cost(0, 2_500_000),
-        )(missing, cache_rows, got).reshape(cache_states.shape)
+        )(missing, cache_rows, new).reshape(cache_states.shape)
     return (pre_out, cache_out, dec_out, dec_new)
 
 

time: 110 us -> 110 us (level)
  the two profiles are of different devices: /device:TPU:16 before, /device:TPU:6 now
where the time goes in v3:
time: 110 us; the launch traced here: 109 us
  starting transfers between devices  62.3 us (57%)
  waiting for transfers between devices  23.2 us (21%)
  Pallas kernels  12.8 us (12%)
  local copies, waits for them, and re-layouts  7.11 us (6%)
  between operations  1.65 us (2%)
  other arithmetic  1.43 us (1%)
    all_to_all x3, starting transfers between devices, swap(): lax.all_to_all(value, 'serve', split_axis=0, concat_axis=0, tiled=True)  37.6 us
    ppermute x6, starting transfers between devices, exchange(): lax.ppermute(pairs[k], 'head', [(i, i ^ 2 * k) for i in range(n_head)])  20.8 us
    all_to_all x3, waiting for transfers between devices, swap(): lax.all_to_all(value, 'serve', split_axis=0, concat_axis=0, tiled=True)  17.7 us
    unnamed x44, local copies, waits for them, and re-layouts  6.21 us
    ppermute x2, starting transfers between devices, exchange(): got = lax.ppermute(give, 'head', [(i, i ^ 1) for i in range(n_head)])  3.83 us
    ppermute x6, waiting for transfers between devices, exchange(): lax.ppermute(pairs[k], 'head', [(i, i ^ 2 * k) for i in range(n_head)])  3.69 us
    pallas_call x1, Pallas kernels, local(): pl.pallas_call(local_state, out_shape=shape((width, tiles * STATE), bf16)...  3.22 us
    pallas_call x1, Pallas kernels, local(): pl.pallas_call(token_inner, out_shape=(shape((length, width), f32), shape...  3.07 us
  transfers between devices with their start and end apart: 11, of which 6 were waited for; matrix products, arithmetic and copies ran while one was open for 3% of the time, Pallas kernels for 5%

profile of v3, /device:TPU:6, one launch (start us, length us, event | category | flops | bytes accessed | tf_op | source)
XLA Modules:
  0.0 109.3 jit_solution(11586980713102498587)
XLA Ops:
  0.6 0.0 copy-start
  0.6 0.0 copy-start.1
  0.7 1.2 %copy-done.1 = f32[4,8,64,128]{3,2,1,0:T(8,128)S(1)} copy-done((f32[4,8,64,128]{3,2,1,0:T(8,128)S(1)}, f32[4,8,64,128]{3,2,1,0:T(8,128)}, u32[]{:S(2)}) %copy-start.1) | copy-done | bytes 1048600
  1.9 0.9 cache.1.after_ref
  2.8 16.7 %all-to-all-start = ((bf16[64,8,512]{2,1,0:T(8,128)(2,1)}), bf16[64,8,512]{2,1,0:T(8,128)(2,1)S(1)}, u32[]{:S(2)}, u32[]{:S(2)}) async-start(bf16[64,8,512]{2,1,0:T(8,128)(2,1)} %bitcast.5), calls=%async_computation | async-start | bytes 1048576 | tf_op jit(solution)/shard_map/cache/all_to_all | solution.py:366
  19.5 0.1 tokens.2
  19.6 1.9 %collective-permute-start = (bf16[4,32,768]{2,1,0:T(8,128)(2,1)S(1)}, bf16[4,32,768]{2,1,0:T(8,128)(2,1)S(1)}, u32[]{:S(2)}, u32[]{:S(2)}) collective-permute-start(bf16[4,32,768]{2,1,0:T(8,128)(2,1)S(1)} %get-tuple-element.22), channel_id=1, source_target_pairs={{0,1},{1,0},{2,3},{3,2},{4,5},{5,4},{6,7},{7,6},{8,9},{9,8},{10,11... | collective-permute-start | bytes 589832 | tf_op jit(solution)/shard_map/tokens/ppermute | solution.py:109
  21.6 1.4 %collective-permute-done.got_ref = bf16[4,32,768]{2,1,0:T(8,128)(2,1)S(1)} collective-permute-done((bf16[4,32,768]{2,1,0:T(8,128)(2,1)S(1)}, bf16[4,32,768]{2,1,0:T(8,128)(2,1)S(1)}, u32[]{:S(2)}, u32[]{:S(2)}) %collective-permute-start) | collective-permute-done | bytes 196640 | tf_op jit(solution)/shard_map/tokens/ppermute | solution.py:109
  23.0 2.7 %collective-permute-start.1 = (bf16[2,32,768]{2,1,0:T(8,128)(2,1)S(1)}, bf16[2,32,768]{2,1,0:T(8,128)(2,1)S(1)}, u32[]{:S(2)}, u32[]{:S(2)}) collective-permute-start(bf16[2,32,768]{2,1,0:T(8,128)(2,1)S(1)} %get-tuple-element.24), channel_id=1, source_target_pairs={{0,2},{1,3},{2,0},{3,1},{4,6},{5,7},{6,4},{7,5},{8,10},{9,11},{10,... | collective-permute-start | bytes 294920 | tf_op jit(solution)/shard_map/tokens/ppermute | solution.py:119
  25.7 0.0 copy-start.12
  25.8 3.0 %collective-permute-start.2 = (bf16[2,32,768]{2,1,0:T(8,128)(2,1)S(1)}, bf16[2,32,768]{2,1,0:T(8,128)(2,1)S(1)}, u32[]{:S(2)}, u32[]{:S(2)}) collective-permute-start(bf16[2,32,768]{2,1,0:T(8,128)(2,1)S(1)} %get-tuple-element.25), channel_id=1, source_target_pairs={{0,4},{1,5},{2,6},{3,7},{4,0},{5,1},{6,2},{7,3},{8,12},{9,13},{10,... | collective-permute-start | bytes 294920 | tf_op jit(solution)/shard_map/tokens/ppermute | solution.py:119
  28.8 4.7 %collective-permute-start.3 = (bf16[2,32,768]{2,1,0:T(8,128)(2,1)S(1)}, bf16[2,32,768]{2,1,0:T(8,128)(2,1)S(1)}, u32[]{:S(2)}, u32[]{:S(2)}) collective-permute-start(bf16[2,32,768]{2,1,0:T(8,128)(2,1)S(1)} %get-tuple-element.26), channel_id=1, source_target_pairs={{0,6},{1,7},{2,4},{3,5},{4,2},{5,3},{6,0},{7,1},{8,14},{9,15},{10,... | collective-permute-start | bytes 294920 | tf_op jit(solution)/shard_map/tokens/ppermute | solution.py:119
  33.5 5.3 %all-to-all-done.recv_ref = bf16[64,8,512]{2,1,0:T(8,128)(2,1)S(1)} async-done(((bf16[64,8,512]{2,1,0:T(8,128)(2,1)}), bf16[64,8,512]{2,1,0:T(8,128)(2,1)S(1)}, u32[]{:S(2)}, u32[]{:S(2)}) %all-to-all-start) | async-done | bytes 524320 | tf_op jit(solution)/shard_map/cache/all_to_all | solution.py:366
  38.8 1.5 %prefix.1 = (bf16[64,8,896]{2,1,0:T(8,128)(2,1)}, bf16[64,8,384]{2,1,0:T(8,128)(2,1)S(1)}) custom-call(s32[192]{0:T(256)S(1)} %copy-done.12, bf16[64,8,512]{2,1,0:T(8,128)(2,1)S(1)} %all-to-all-done.recv_ref), custom_call_target="tpu_custom_call" | custom-call | bytes 2000000 | tf_op jit(solution)/shard_map/prefix/pallas_call | solution.py:403
  40.3 0.0 collective-permute-done.1.refs_1_
  40.3 0.0 collective-permute-done.2.refs_2_
  40.3 0.0 collective-permute-done.3.refs_3_
  40.3 0.0 copy-start.11
  40.3 0.0 copy-start.13
  40.3 0.6 copy-done.11
  41.0 0.0 copy-done.13
  41.0 3.2 %local.1.after_ref = bf16[512,896]{1,0:T(8,128)(2,1)} custom-call(s32[1,3]{1,0:T(1,128)S(1)} %copy-done.13, s32[1]{0:T(128)} %bitcast.1.me_ref, f32[1,8]{1,0:T(1,128)S(1)} %bitcast.22, bf16[2,32,768]{2,1,0:T(8,128)(2,1)S(1)} %get-tuple-element.23.refs_0_, bf16[2,32,768]{2,1,0:T(8,128)(2,1)S(1)} %collective-permute-done.1.refs_1_, ...), custom_call_target="tpu_custom_call", output_to_operand_aliasing={{}: (7, {})} | custom-call | flops 300000000 | bytes 800000 | tf_op jit(solution)/shard_map/local/pallas_call | solution.py:419
  44.2 0.0 copy-start.21
  44.2 0.0 copy-start.18
  44.2 0.0 copy-start.16
  44.3 9.0 %all-to-all-start.1 = ((bf16[64,8,896]{2,1,0:T(8,128)(2,1)}), bf16[64,8,896]{2,1,0:T(8,128)(2,1)S(1)}, u32[]{:S(2)}, u32[]{:S(2)}) async-start(bf16[64,8,896]{2,1,0:T(8,128)(2,1)} %bitcast.7), calls=%async_computation.1 | async-start | bytes 1835008 | tf_op jit(solution)/shard_map/local/all_to_all | solution.py:366
  53.3 0.0 copy-done.18
  53.3 0.0 copy-start.20
  53.3 0.1 reshape.145
  53.4 0.6 copy-done.20
  54.0 0.1 broadcast_multiply_fusion
  54.1 0.0 copy-done.16
  54.1 0.0 copy-start.8
  54.1 0.2 multiply_add_fusion
  54.3 0.7 copy-done.6
  55.1 1.9 %collective-permute-start.4 = (bf16[4,32,640]{2,1,0:T(8,128)(2,1)S(1)}, bf16[4,32,640]{2,1,0:T(8,128)(2,1)S(1)}, u32[]{:S(2)}, u32[]{:S(2)}) collective-permute-start(bf16[4,32,640]{2,1,0:T(8,128)(2,1)S(1)} %get-tuple-element.29), channel_id=1, source_target_pairs={{0,1},{1,0},{2,3},{3,2},{4,5},{5,4},{6,7},{7,6},{8,9},{9,8},{10,11... | collective-permute-start | bytes 491528 | tf_op jit(solution)/shard_map/gates/ppermute | solution.py:109
  57.0 0.0 copy-start.17
  57.0 0.7 fusion.5
  57.7 0.2 convert_reduce_fusion
  58.0 0.4 collective-permute-done.4.got_ref
  58.4 2.4 %collective-permute-start.5 = (bf16[2,32,640]{2,1,0:T(8,128)(2,1)S(1)}, bf16[2,32,640]{2,1,0:T(8,128)(2,1)S(1)}, u32[]{:S(2)}, u32[]{:S(2)}) collective-permute-start(bf16[2,32,640]{2,1,0:T(8,128)(2,1)S(1)} %get-tuple-element.31), channel_id=1, source_target_pairs={{0,2},{1,3},{2,0},{3,1},{4,6},{5,7},{6,4},{7,5},{8,10},{9,11},{10,... | collective-permute-start | bytes 245768 | tf_op jit(solution)/shard_map/gates/ppermute | solution.py:119
  60.8 5.6 %collective-permute-start.6 = (bf16[2,32,640]{2,1,0:T(8,128)(2,1)S(1)}, bf16[2,32,640]{2,1,0:T(8,128)(2,1)S(1)}, u32[]{:S(2)}, u32[]{:S(2)}) collective-permute-start(bf16[2,32,640]{2,1,0:T(8,128)(2,1)S(1)} %get-tuple-element.32), channel_id=1, source_target_pairs={{0,4},{1,5},{2,6},{3,7},{4,0},{5,1},{6,2},{7,3},{8,12},{9,13},{10,... | collective-permute-start | bytes 245768 | tf_op jit(solution)/shard_map/gates/ppermute | solution.py:119
  66.4 2.4 %collective-permute-start.7 = (bf16[2,32,640]{2,1,0:T(8,128)(2,1)S(1)}, bf16[2,32,640]{2,1,0:T(8,128)(2,1)S(1)}, u32[]{:S(2)}, u32[]{:S(2)}) collective-permute-start(bf16[2,32,640]{2,1,0:T(8,128)(2,1)S(1)} %get-tuple-element.33), channel_id=1, source_target_pairs={{0,6},{1,7},{2,4},{3,5},{4,2},{5,3},{6,0},{7,1},{8,14},{9,15},{10,... | collective-permute-start | bytes 245768 | tf_op jit(solution)/shard_map/gates/ppermute | solution.py:119
  68.9 0.0 copy-start.19
  68.9 0.7 copy-done.19
  69.6 0.1 reshape.147
  69.6 0.6 copy-done.10
  70.2 0.1 mul.108
  70.3 0.0 collective-permute-done.5.refs_5_
  70.3 0.0 collective-permute-done.6.refs_6_
  70.3 3.7 %collective-permute-done.7.refs_7_ = bf16[2,32,640]{2,1,0:T(8,128)(2,1)S(1)} collective-permute-done((bf16[2,32,640]{2,1,0:T(8,128)(2,1)S(1)}, bf16[2,32,640]{2,1,0:T(8,128)(2,1)S(1)}, u32[]{:S(2)}, u32[]{:S(2)}) %collective-permute-start.7) | collective-permute-done | bytes 81952 | tf_op jit(solution)/shard_map/gates/ppermute | solution.py:119
  74.0 0.7 copy-done.14
  74.7 3.1 %inner.1 = (f32[256,512]{1,0:T(8,128)S(1)}, f32[256,512]{1,0:T(8,128)S(1)}, bf16[256,384]{1,0:T(8,128)(2,1)S(1)}) custom-call(s32[1,3]{1,0:T(1,128)S(1)} %copy-done.13, s32[1]{0:T(128)} %bitcast.1.me_ref, f32[1,8]{1,0:T(1,128)S(1)} %bitcast.23, f32[1,8]{1,0:T(1,128)S(1)} %bitcast.24, bf16[2,32,768]{2,1,0:T(8,128)(2,1)S(1)} %get-tuple-element.23.refs_0_, ...), custom_call_target="tpu_custom_call" | custom-call | flops 400000000 | bytes 1500000 | tf_op jit(solution)/shard_map/inner/pallas_call | solution.py:446
  77.7 0.8 all-to-all-done.1.recv_ref
  78.6 1.8 %snapshots.1 = bf16[64,8,384]{2,1,0:T(8,128)(2,1)} custom-call(s32[192]{0:T(256)S(1)} %fusion.4.place_ref, bf16[256,384]{1,0:T(8,128)(2,1)S(1)} %get-tuple-element.36.read_ref.after_ref, bf16[64,8,384]{2,1,0:T(8,128)(2,1)S(1)} %get-tuple-element.37.picked_ref, bf16[64,8,896]{2,1,0:T(8,128)(2,1)S(1)} %all-to-all-done.1.recv_ref), custom_call_target="tpu_custom_call" | custom-call | bytes 2000000 | tf_op jit(solution)/shard_map/snapshots/pallas_call | solution.py:464
  80.3 11.9 %all-to-all-start.2 = ((bf16[64,8,384]{2,1,0:T(8,128)(2,1)}), bf16[64,8,384]{2,1,0:T(8,128)(2,1)S(1)}, u32[]{:S(2)}, u32[]{:S(2)}) async-start(bf16[64,8,384]{2,1,0:T(8,128)(2,1)} %snapshots.1), calls=%async_computation.2 | async-start | bytes 786432 | tf_op jit(solution)/shard_map/snapshots/all_to_all | solution.py:366
  92.2 0.2 multiply_reduce_fusion
  92.4 0.1 multiply_convert_fusion
  92.5 0.7 convert_element_type.22
  93.1 0.6 fusion.7
  94.4 1.0 copy-done.4
  95.5 1.1 %outputs.2 = bf16[256,512]{1,0:T(8,128)(2,1)} custom-call(f32[1,512]{1,0:T(1,128)S(1)} %bitcast.21, f32[256,512]{1,0:T(8,128)S(1)} %get-tuple-element.34.base_ref, f32[256,512]{1,0:T(8,128)S(1)} %copy-done.4, bf16[256,384]{1,0:T(8,128)(2,1)S(1)} %get-tuple-element.36.read_ref.after_ref, bf16[512,896]{1,0:T(8,128)(2,1)S(1)} %bitcast.17), custom_call_target="tpu_custom_call" | custom-call | flops 200000000 | bytes 1500000 | tf_op jit(solution)/shard_map/outputs/pallas_call | solution.py:477
  96.6 11.6 %all-to-all-done.2 = bf16[64,8,384]{2,1,0:T(8,128)(2,1)S(1)} async-done(((bf16[64,8,384]{2,1,0:T(8,128)(2,1)}), bf16[64,8,384]{2,1,0:T(8,128)(2,1)S(1)}, u32[]{:S(2)}, u32[]{:S(2)}) %all-to-all-start.2) | async-done | bytes 393248 | tf_op jit(solution)/shard_map/snapshots/all_to_all | solution.py:366
  108.2 1.1 outputs.3
  (28 shorter events, 0.2 us)
Async XLA Ops:
  0.6 56.4 %copy-start = (bf16[2,128]{1,0:T(2,128)(2,1)S(1)}, bf16[2,128]{1,0:T(2,128)(2,1)}, u32[]{:S(2)}) copy-start(bf16[2,128]{1,0:T(2,128)(2,1)} %param.30) | copy-start | bytes 1540
  0.6 1.2 %copy-start.1 = (f32[4,8,64,128]{3,2,1,0:T(8,128)S(1)}, f32[4,8,64,128]{3,2,1,0:T(8,128)}, u32[]{:S(2)}) copy-start(f32[4,8,64,128]{3,2,1,0:T(8,128)} %param.26) | copy-start | bytes 3145732
  2.7 16.7 %copy-start.5 = (bf16[32,4096]{1,0:T(8,128)(2,1)S(1)}, bf16[32,4096]{1,0:T(8,128)(2,1)}, u32[]{:S(2)}) copy-start(bf16[32,4096]{1,0:T(8,128)(2,1)} %x_ref.1) | copy-start | bytes 786436
  2.8 16.7 %copy-start.7 = (bf16[32,1024]{1,0:T(8,128)(2,1)S(1)}, bf16[32,1024]{1,0:T(8,128)(2,1)}, u32[]{:S(2)}) copy-start(bf16[32,1024]{1,0:T(8,128)(2,1)} %b_ref.1) | copy-start | bytes 196612
  2.8 16.8 %copy-start.9 = (bf16[32,64]{1,0:T(8,128)(2,1)S(1)}, bf16[32,64]{1,0:T(8,128)(2,1)}, u32[]{:S(2)}) copy-start(bf16[32,64]{1,0:T(8,128)(2,1)} %dt_ref.1) | copy-start | bytes 12292
  2.8 36.0 %all-to-all-start = ((bf16[64,8,512]{2,1,0:T(8,128)(2,1)}), bf16[64,8,512]{2,1,0:T(8,128)(2,1)S(1)}, u32[]{:S(2)}, u32[]{:S(2)}) async-start(bf16[64,8,512]{2,1,0:T(8,128)(2,1)} %bitcast.5), calls=%async_computation | async-start | bytes 1048576 | tf_op jit(solution)/shard_map/cache/all_to_all | solution.py:366
  19.6 3.3 %collective-permute-start = (bf16[4,32,768]{2,1,0:T(8,128)(2,1)S(1)}, bf16[4,32,768]{2,1,0:T(8,128)(2,1)S(1)}, u32[]{:S(2)}, u32[]{:S(2)}) collective-permute-start(bf16[4,32,768]{2,1,0:T(8,128)(2,1)S(1)} %get-tuple-element.22), channel_id=1, source_target_pairs={{0,1},{1,0},{2,3},{3,2},{4,5},{5,4},{6,7},{7,6},{8,9},{9,8},{10,11... | collective-permute-start | bytes 589832 | tf_op jit(solution)/shard_map/tokens/ppermute | solution.py:109
  23.0 17.3 %collective-permute-start.1 = (bf16[2,32,768]{2,1,0:T(8,128)(2,1)S(1)}, bf16[2,32,768]{2,1,0:T(8,128)(2,1)S(1)}, u32[]{:S(2)}, u32[]{:S(2)}) collective-permute-start(bf16[2,32,768]{2,1,0:T(8,128)(2,1)S(1)} %get-tuple-element.24), channel_id=1, source_target_pairs={{0,2},{1,3},{2,0},{3,1},{4,6},{5,7},{6,4},{7,5},{8,10},{9,11},{10,... | collective-permute-start | bytes 294920 | tf_op jit(solution)/shard_map/tokens/ppermute | solution.py:119
  25.7 13.0 %copy-start.12 = (s32[192]{0:T(256)S(1)}, s32[192]{0:T(256)}, u32[]{:S(2)}) copy-start(s32[192]{0:T(256)} %hit_ref.1) | copy-start | bytes 2308
  25.8 14.5 %collective-permute-start.2 = (bf16[2,32,768]{2,1,0:T(8,128)(2,1)S(1)}, bf16[2,32,768]{2,1,0:T(8,128)(2,1)S(1)}, u32[]{:S(2)}, u32[]{:S(2)}) collective-permute-start(bf16[2,32,768]{2,1,0:T(8,128)(2,1)S(1)} %get-tuple-element.25), channel_id=1, source_target_pairs={{0,4},{1,5},{2,6},{3,7},{4,0},{5,1},{6,2},{7,3},{8,12},{9,13},{10,... | collective-permute-start | bytes 294920 | tf_op jit(solution)/shard_map/tokens/ppermute | solution.py:119
  28.8 11.5 %collective-permute-start.3 = (bf16[2,32,768]{2,1,0:T(8,128)(2,1)S(1)}, bf16[2,32,768]{2,1,0:T(8,128)(2,1)S(1)}, u32[]{:S(2)}, u32[]{:S(2)}) collective-permute-start(bf16[2,32,768]{2,1,0:T(8,128)(2,1)S(1)} %get-tuple-element.26), channel_id=1, source_target_pairs={{0,6},{1,7},{2,4},{3,5},{4,2},{5,3},{6,0},{7,1},{8,14},{9,15},{10,... | collective-permute-start | bytes 294920 | tf_op jit(solution)/shard_map/tokens/ppermute | solution.py:119
  40.3 0.7 copy-start.11
  40.3 0.7 copy-start.13
  44.2 9.1 %copy-start.21 = (bf16[2,128]{1,0:T(2,128)(2,1)S(1)}, bf16[2,128]{1,0:T(2,128)(2,1)}, u32[]{:S(2)}) copy-start(bf16[2,128]{1,0:T(2,128)(2,1)} %param.29) | copy-start | bytes 1540
  44.2 9.1 %copy-start.18 = (bf16[2,512]{1,0:T(2,128)(2,1)S(1)}, bf16[2,512]{1,0:T(2,128)(2,1)}, u32[]{:S(2)}) copy-start(bf16[2,512]{1,0:T(2,128)(2,1)} %param.27) | copy-start | bytes 6148
  44.2 9.8 %copy-start.16 = (f32[2,8,64,128]{3,2,1,0:T(8,128)S(1)}, f32[2,8,64,128]{3,2,1,0:T(8,128)}, u32[]{:S(2)}) copy-start(f32[2,8,64,128]{3,2,1,0:T(8,128)} %param.32) | copy-start | bytes 1572868
  44.3 34.3 %all-to-all-start.1 = ((bf16[64,8,896]{2,1,0:T(8,128)(2,1)}), bf16[64,8,896]{2,1,0:T(8,128)(2,1)S(1)}, u32[]{:S(2)}, u32[]{:S(2)}) async-start(bf16[64,8,896]{2,1,0:T(8,128)(2,1)} %bitcast.7), calls=%async_computation.1 | async-start | bytes 1835008 | tf_op jit(solution)/shard_map/local/all_to_all | solution.py:366
  53.3 0.7 copy-start.20
  54.1 1.0 copy-start.6
  54.1 1.0 copy-start.8
  55.0 2.0 %copy-start.15 = (f32[2,8,64,128]{3,2,1,0:T(8,128)}, f32[2,8,64,128]{3,2,1,0:T(8,128)S(1)}, u32[]{:S(2)}) copy-start(f32[2,8,64,128]{3,2,1,0:T(8,128)S(1)} %multiply_add_fusion) | copy-start | bytes 1572868
  55.1 3.3 %collective-permute-start.4 = (bf16[4,32,640]{2,1,0:T(8,128)(2,1)S(1)}, bf16[4,32,640]{2,1,0:T(8,128)(2,1)S(1)}, u32[]{:S(2)}, u32[]{:S(2)}) collective-permute-start(bf16[4,32,640]{2,1,0:T(8,128)(2,1)S(1)} %get-tuple-element.29), channel_id=1, source_target_pairs={{0,1},{1,0},{2,3},{3,2},{4,5},{5,4},{6,7},{7,6},{8,9},{9,8},{10,11... | collective-permute-start | bytes 491528 | tf_op jit(solution)/shard_map/gates/ppermute | solution.py:109
  57.0 0.7 copy-start.17
  58.4 11.9 %collective-permute-start.5 = (bf16[2,32,640]{2,1,0:T(8,128)(2,1)S(1)}, bf16[2,32,640]{2,1,0:T(8,128)(2,1)S(1)}, u32[]{:S(2)}, u32[]{:S(2)}) collective-permute-start(bf16[2,32,640]{2,1,0:T(8,128)(2,1)S(1)} %get-tuple-element.31), channel_id=1, source_target_pairs={{0,2},{1,3},{2,0},{3,1},{4,6},{5,7},{6,4},{7,5},{8,10},{9,11},{10,... | collective-permute-start | bytes 245768 | tf_op jit(solution)/shard_map/gates/ppermute | solution.py:119
  60.8 9.5 %collective-permute-start.6 = (bf16[2,32,640]{2,1,0:T(8,128)(2,1)S(1)}, bf16[2,32,640]{2,1,0:T(8,128)(2,1)S(1)}, u32[]{:S(2)}, u32[]{:S(2)}) collective-permute-start(bf16[2,32,640]{2,1,0:T(8,128)(2,1)S(1)} %get-tuple-element.32), channel_id=1, source_target_pairs={{0,4},{1,5},{2,6},{3,7},{4,0},{5,1},{6,2},{7,3},{8,12},{9,13},{10,... | collective-permute-start | bytes 245768 | tf_op jit(solution)/shard_map/gates/ppermute | solution.py:119
  66.4 7.5 %collective-permute-start.7 = (bf16[2,32,640]{2,1,0:T(8,128)(2,1)S(1)}, bf16[2,32,640]{2,1,0:T(8,128)(2,1)S(1)}, u32[]{:S(2)}, u32[]{:S(2)}) collective-permute-start(bf16[2,32,640]{2,1,0:T(8,128)(2,1)S(1)} %get-tuple-element.33), channel_id=1, source_target_pairs={{0,6},{1,7},{2,4},{3,5},{4,2},{5,3},{6,0},{7,1},{8,14},{9,15},{10,... | collective-permute-start | bytes 245768 | tf_op jit(solution)/shard_map/gates/ppermute | solution.py:119
  68.9 0.7 copy-start.19
  69.6 0.7 copy-start.10
  74.0 0.7 copy-start.14
  77.7 2.6 %copy-start.3 = (f32[256,512]{1,0:T(8,128)}, f32[256,512]{1,0:T(8,128)S(1)}, u32[]{:S(2)}) copy-start(f32[256,512]{1,0:T(8,128)S(1)} %get-tuple-element.35.factor_ref) | copy-start | bytes 1572868
  80.3 27.9 %all-to-all-start.2 = ((bf16[64,8,384]{2,1,0:T(8,128)(2,1)}), bf16[64,8,384]{2,1,0:T(8,128)(2,1)S(1)}, u32[]{:S(2)}, u32[]{:S(2)}) async-start(bf16[64,8,384]{2,1,0:T(8,128)(2,1)} %snapshots.1), calls=%async_computation.2 | async-start | bytes 786432 | tf_op jit(solution)/shard_map/snapshots/all_to_all | solution.py:366
  94.4 1.0 copy-start.4
  95.5 12.8 %copy-start.2 = (f32[4,8,64,128]{3,2,1,0:T(8,128)S(1)}, f32[4,8,64,128]{3,2,1,0:T(8,128)}, u32[]{:S(2)}) copy-start(f32[4,8,64,128]{3,2,1,0:T(8,128)} %param.26) | copy-start | bytes 3145732

commit v4 on v3

--- a/solution.py
+++ b/solution.py
@@ -158,8 +158,7 @@
 
 
 def local_state(len_ref, me_ref, rate_ref, *refs):
-    pair_refs, (send_ref, out_ref, tok_ref, made, sems, last_sem) = refs[:-6], refs[-6:]
-    del send_ref
+    pair_refs, (out_ref, tok_ref, made, sems, last_sem) = refs[:-5], refs[-5:]
     length = tok_ref.shape[0]
     heads = rate_ref.shape[1]
     width = heads * HEAD_DIM
@@ -204,7 +203,8 @@
     last.wait()
 
 
-def pick_prefix(hit_ref, recv_ref, out_ref, picked_ref, held, sem):
+def pick_prefix(hit_ref, recv_ref, send_ref, out_ref, picked_ref, held, sem):
+    del send_ref
     for s in range(recv_ref.shape[0]):
         block = recv_ref[s].astype(f32)
         for k in range(SLOTS):
@@ -217,8 +217,8 @@
     copy.wait()
 
 
-def make_snapshots(place_ref, after_ref, picked_ref, recv_ref, out_ref):
-    del after_ref
+def make_snapshots(place_ref, picked_ref, recv_ref, *refs):
+    out_ref = refs[-1]
     for s in range(recv_ref.shape[0]):
         prefix = picked_ref[s].astype(f32)
         block = recv_ref[s, :, REQS * STATE :].astype(f32)
@@ -399,6 +399,21 @@
         )(head_me, spread, pre_x, pre_b, pre_dt)
         tokens = exchange(keep, give, n_head)
     rates = decay_rate.reshape(1, heads)
+    with jax.named_scope("local"):
+        send = pl.pallas_call(
+            local_state,
+            out_shape=shape((width, tiles * STATE), bf16),
+            in_specs=[SMEM] * 2 + [VMEM] + [ANY] * chips,
+            out_specs=HBM,
+            scratch_shapes=[
+                pltpu.VMEM((length, width + 2 * STATE), bf16),
+                pltpu.VMEM((width, (REQS + 1) * STATE), bf16),
+                pltpu.SemaphoreType.DMA((n_head,)),
+                pltpu.SemaphoreType.DMA,
+            ],
+            compiler_params=params(),
+            cost_estimate=cost(300_000_000, 800_000),
+        )(suffix_lengths, head_me, rates, *tokens)
     with jax.named_scope("prefix"):
         send, picked = pl.pallas_call(
             pick_prefix,
@@ -406,32 +421,17 @@
                 shape((n_serve, ROWS, tiles * STATE), bf16),
                 shape((n_serve, ROWS, REQS * STATE), bf16),
             ),
-            in_specs=[SMEM, VMEM],
+            in_specs=[SMEM, VMEM, HBM],
             out_specs=(HBM, VMEM),
             scratch_shapes=[
                 pltpu.VMEM((n_serve * SLOTS, ROWS, STATE), f32),
                 pltpu.SemaphoreType.DMA,
             ],
+            input_output_aliases={2: 0},
             compiler_params=params(),
             cost_estimate=cost(0, 2_000_000),
-        )(prefix_hits, pieces)
-    with jax.named_scope("local"):
-        send = pl.pallas_call(
-            local_state,
-            out_shape=shape((width, tiles * STATE), bf16),
-            in_specs=[SMEM] * 2 + [VMEM] + [ANY] * chips + [HBM],
-            out_specs=HBM,
-            scratch_shapes=[
-                pltpu.VMEM((length, width + 2 * STATE), bf16),
-                pltpu.VMEM((width, (REQS + 1) * STATE), bf16),
-                pltpu.SemaphoreType.DMA((n_head,)),
-                pltpu.SemaphoreType.DMA,
-            ],
-            input_output_aliases={3 + chips: 0},
-            compiler_params=params(),
-            cost_estimate=cost(300_000_000, 800_000),
-        )(suffix_lengths, head_me, rates, *tokens, send.reshape(width, tiles * STATE))
-        got = swap(send.reshape(n_serve, ROWS, tiles * STATE))
+        )(prefix_hits, pieces, send.reshape(n_serve, ROWS, tiles * STATE))
+        got = swap(send)
     with jax.named_scope("gates"):
         keep, give = pl.pallas_call(
             pack_gates,
@@ -464,11 +464,11 @@
         answer = pl.pallas_call(
             make_snapshots,
             out_shape=shape((n_serve, ROWS, REQS * STATE), bf16),
-            in_specs=[SMEM, ANY, VMEM, VMEM],
+            in_specs=[SMEM, VMEM, VMEM] + [ANY] * (chips - 1),
             out_specs=VMEM,
             compiler_params=params(),
             cost_estimate=cost(0, 2_000_000),
-        )(place, read, picked, got)
+        )(place, picked, got, *gates[1:])
         new = swap(answer).reshape(width, REQS * STATE)
     dec_out, dec_new = decode_block(
         dec_x, dec_z, dec_b, dec_c, dec_dt, dec_states, decay_rate, d_skip, norm_weight

time: 110 us -> 109 us (level)
  the two profiles are of different devices: /device:TPU:6 before, /device:TPU:4 now
where the time goes in v4:
time: 109 us; the launch traced here: 108 us
  starting transfers between devices  58.3 us (53%)
  waiting for transfers between devices  26.2 us (24%)
  Pallas kernels  12.8 us (12%)
  local copies, waits for them, and re-layouts  6.74 us (6%)
  between operations  1.61 us (1%)
  other arithmetic  1.5 us (1%)
    all_to_all x3, starting transfers between devices, swap(): lax.all_to_all(value, 'serve', split_axis=0, concat_axis=0, tiled=True)  35.9 us
    ppermute x6, starting transfers between devices, exchange(): lax.ppermute(pairs[k], 'head', [(i, i ^ 2 * k) for i in range(n_head)])  18.6 us
    all_to_all x3, waiting for transfers between devices, swap(): lax.all_to_all(value, 'serve', split_axis=0, concat_axis=0, tiled=True)  18.1 us
    ppermute x6, waiting for transfers between devices, exchange(): lax.ppermute(pairs[k], 'head', [(i, i ^ 2 * k) for i in range(n_head)])  6.32 us
    unnamed x40, local copies, waits for them, and re-layouts  5.84 us
    ppermute x2, starting transfers between devices, exchange(): got = lax.ppermute(give, 'head', [(i, i ^ 1) for i in range(n_head)])  3.83 us
    pallas_call x1, Pallas kernels, local(): pl.pallas_call(local_state, out_shape=shape((width, tiles * STATE), bf16)...  3.22 us
    pallas_call x1, Pallas kernels, local(): pl.pallas_call(token_inner, out_shape=(shape((length, width), f32), shape...  3.05 us
  transfers between devices with their start and end apart: 11, of which 8 were waited for; matrix products, arithmetic and copies ran while one was open for 3% of the time, Pallas kernels for 7%

profile of v4, /device:TPU:4, one launch (start us, length us, event | category | flops | bytes accessed | tf_op | source)
XLA Modules:
  0.0 107.9 jit_solution(4095227586139392327)
XLA Ops:
  0.6 0.0 copy-start
  0.6 0.0 copy-start.1
  0.7 1.2 %copy-done.1 = f32[4,8,64,128]{3,2,1,0:T(8,128)S(1)} copy-done((f32[4,8,64,128]{3,2,1,0:T(8,128)S(1)}, f32[4,8,64,128]{3,2,1,0:T(8,128)}, u32[]{:S(2)}) %copy-start.1) | copy-done | bytes 1048600
  1.9 0.9 cache.1.after_ref
  2.8 16.7 %all-to-all-start = ((bf16[64,8,512]{2,1,0:T(8,128)(2,1)}), bf16[64,8,512]{2,1,0:T(8,128)(2,1)S(1)}, u32[]{:S(2)}, u32[]{:S(2)}) async-start(bf16[64,8,512]{2,1,0:T(8,128)(2,1)} %bitcast.5), calls=%async_computation | async-start | bytes 1048576 | tf_op jit(solution)/shard_map/cache/all_to_all | solution.py:366
  19.5 0.1 tokens.2
  19.6 1.9 %collective-permute-start = (bf16[4,32,768]{2,1,0:T(8,128)(2,1)S(1)}, bf16[4,32,768]{2,1,0:T(8,128)(2,1)S(1)}, u32[]{:S(2)}, u32[]{:S(2)}) collective-permute-start(bf16[4,32,768]{2,1,0:T(8,128)(2,1)S(1)} %get-tuple-element.22), channel_id=1, source_target_pairs={{0,1},{1,0},{2,3},{3,2},{4,5},{5,4},{6,7},{7,6},{8,9},{9,8},{10,11... | collective-permute-start | bytes 589832 | tf_op jit(solution)/shard_map/tokens/ppermute | solution.py:109
  21.6 1.4 %collective-permute-done.got_ref = bf16[4,32,768]{2,1,0:T(8,128)(2,1)S(1)} collective-permute-done((bf16[4,32,768]{2,1,0:T(8,128)(2,1)S(1)}, bf16[4,32,768]{2,1,0:T(8,128)(2,1)S(1)}, u32[]{:S(2)}, u32[]{:S(2)}) %collective-permute-start) | collective-permute-done | bytes 196640 | tf_op jit(solution)/shard_map/tokens/ppermute | solution.py:109
  23.0 3.1 %collective-permute-start.1 = (bf16[2,32,768]{2,1,0:T(8,128)(2,1)S(1)}, bf16[2,32,768]{2,1,0:T(8,128)(2,1)S(1)}, u32[]{:S(2)}, u32[]{:S(2)}) collective-permute-start(bf16[2,32,768]{2,1,0:T(8,128)(2,1)S(1)} %get-tuple-element.24), channel_id=1, source_target_pairs={{0,2},{1,3},{2,0},{3,1},{4,6},{5,7},{6,4},{7,5},{8,10},{9,11},{10,... | collective-permute-start | bytes 294920 | tf_op jit(solution)/shard_map/tokens/ppermute | solution.py:119
  26.1 2.7 %collective-permute-start.2 = (bf16[2,32,768]{2,1,0:T(8,128)(2,1)S(1)}, bf16[2,32,768]{2,1,0:T(8,128)(2,1)S(1)}, u32[]{:S(2)}, u32[]{:S(2)}) collective-permute-start(bf16[2,32,768]{2,1,0:T(8,128)(2,1)S(1)} %get-tuple-element.25), channel_id=1, source_target_pairs={{0,4},{1,5},{2,6},{3,7},{4,0},{5,1},{6,2},{7,3},{8,12},{9,13},{10,... | collective-permute-start | bytes 294920 | tf_op jit(solution)/shard_map/tokens/ppermute | solution.py:119
  28.8 3.4 %collective-permute-start.3 = (bf16[2,32,768]{2,1,0:T(8,128)(2,1)S(1)}, bf16[2,32,768]{2,1,0:T(8,128)(2,1)S(1)}, u32[]{:S(2)}, u32[]{:S(2)}) collective-permute-start(bf16[2,32,768]{2,1,0:T(8,128)(2,1)S(1)} %get-tuple-element.26), channel_id=1, source_target_pairs={{0,6},{1,7},{2,4},{3,5},{4,2},{5,3},{6,0},{7,1},{8,14},{9,15},{10,... | collective-permute-start | bytes 294920 | tf_op jit(solution)/shard_map/tokens/ppermute | solution.py:119
  32.2 0.0 collective-permute-done.1.refs_1_
  32.2 1.9 %collective-permute-done.2.refs_2_ = bf16[2,32,768]{2,1,0:T(8,128)(2,1)S(1)} collective-permute-done((bf16[2,32,768]{2,1,0:T(8,128)(2,1)S(1)}, bf16[2,32,768]{2,1,0:T(8,128)(2,1)S(1)}, u32[]{:S(2)}, u32[]{:S(2)}) %collective-permute-start.2) | collective-permute-done | bytes 98336 | tf_op jit(solution)/shard_map/tokens/ppermute | solution.py:119
  34.2 2.0 %collective-permute-done.3.refs_3_ = bf16[2,32,768]{2,1,0:T(8,128)(2,1)S(1)} collective-permute-done((bf16[2,32,768]{2,1,0:T(8,128)(2,1)S(1)}, bf16[2,32,768]{2,1,0:T(8,128)(2,1)S(1)}, u32[]{:S(2)}, u32[]{:S(2)}) %collective-permute-start.3) | collective-permute-done | bytes 98336 | tf_op jit(solution)/shard_map/tokens/ppermute | solution.py:119
  36.2 0.7 copy-done.9
  36.8 0.0 copy-done.11
  36.9 3.2 %local.1 = bf16[512,896]{1,0:T(8,128)(2,1)} custom-call(s32[1,3]{1,0:T(1,128)S(1)} %copy-done.11, s32[1]{0:T(128)} %bitcast.1.me_ref, f32[1,8]{1,0:T(1,128)S(1)} %bitcast.21, bf16[2,32,768]{2,1,0:T(8,128)(2,1)S(1)} %get-tuple-element.23.refs_0_, bf16[2,32,768]{2,1,0:T(8,128)(2,1)S(1)} %collective-permute-done.1.refs_1_, ...), custom_call_target="tpu_custom_call" | custom-call | flops 300000000 | bytes 800000 | tf_op jit(solution)/shard_map/local/pallas_call | solution.py:403
  40.1 0.0 copy-start.10
  40.1 0.0 all-to-all-done.recv_ref
  40.1 0.7 copy-done.10
  40.8 1.5 %prefix.1 = (bf16[64,8,896]{2,1,0:T(8,128)(2,1)}, bf16[64,8,384]{2,1,0:T(8,128)(2,1)S(1)}) custom-call(s32[192]{0:T(256)S(1)} %copy-done.10, bf16[64,8,512]{2,1,0:T(8,128)(2,1)S(1)} %all-to-all-done.recv_ref, bf16[64,8,896]{2,1,0:T(8,128)(2,1)} %bitcast.6.send_ref), custom_call_target="tpu_custom_call", output_to_operand_aliasing={{0}: (2, {})} | custom-call | bytes 2000000 | tf_op jit(solution)/shard_map/prefix/pallas_call | solution.py:418
  42.3 0.0 copy-start.19
  42.3 0.0 copy-start.16
  42.3 0.0 copy-start.14
  42.3 12.8 %all-to-all-start.1 = ((bf16[64,8,896]{2,1,0:T(8,128)(2,1)}), bf16[64,8,896]{2,1,0:T(8,128)(2,1)S(1)}, u32[]{:S(2)}, u32[]{:S(2)}) async-start(bf16[64,8,896]{2,1,0:T(8,128)(2,1)} %get-tuple-element.27.after_ref), calls=%async_computation.1 | async-start | bytes 1835008 | tf_op jit(solution)/shard_map/prefix/all_to_all | solution.py:366
  55.2 0.0 copy-done.19
  55.2 0.0 copy-start.18
  55.2 0.1 reshape.141
  55.3 0.6 copy-done.18
  55.9 0.1 broadcast_multiply_fusion
  55.9 0.0 copy-start.6
  56.0 0.2 multiply_add_fusion
  56.2 0.7 copy-done.4
  57.0 1.9 %collective-permute-start.4 = (bf16[4,32,640]{2,1,0:T(8,128)(2,1)S(1)}, bf16[4,32,640]{2,1,0:T(8,128)(2,1)S(1)}, u32[]{:S(2)}, u32[]{:S(2)}) collective-permute-start(bf16[4,32,640]{2,1,0:T(8,128)(2,1)S(1)} %get-tuple-element.29), channel_id=1, source_target_pairs={{0,1},{1,0},{2,3},{3,2},{4,5},{5,4},{6,7},{7,6},{8,9},{9,8},{10,11... | collective-permute-start | bytes 491528 | tf_op jit(solution)/shard_map/gates/ppermute | solution.py:109
  58.9 0.0 copy-start.15
  58.9 0.7 fusion.5
  59.6 0.0 copy-done.15
  59.6 0.2 convert_reduce_fusion
  59.8 0.4 collective-permute-done.4.got_ref
  60.3 3.4 %collective-permute-start.5 = (bf16[2,32,640]{2,1,0:T(8,128)(2,1)S(1)}, bf16[2,32,640]{2,1,0:T(8,128)(2,1)S(1)}, u32[]{:S(2)}, u32[]{:S(2)}) collective-permute-start(bf16[2,32,640]{2,1,0:T(8,128)(2,1)S(1)} %get-tuple-element.31), channel_id=1, source_target_pairs={{0,2},{1,3},{2,0},{3,1},{4,6},{5,7},{6,4},{7,5},{8,10},{9,11},{10,... | collective-permute-start | bytes 245768 | tf_op jit(solution)/shard_map/gates/ppermute | solution.py:119
  63.7 3.5 %collective-permute-start.6 = (bf16[2,32,640]{2,1,0:T(8,128)(2,1)S(1)}, bf16[2,32,640]{2,1,0:T(8,128)(2,1)S(1)}, u32[]{:S(2)}, u32[]{:S(2)}) collective-permute-start(bf16[2,32,640]{2,1,0:T(8,128)(2,1)S(1)} %get-tuple-element.32), channel_id=1, source_target_pairs={{0,4},{1,5},{2,6},{3,7},{4,0},{5,1},{6,2},{7,3},{8,12},{9,13},{10,... | collective-permute-start | bytes 245768 | tf_op jit(solution)/shard_map/gates/ppermute | solution.py:119
  67.2 2.5 %collective-permute-start.7 = (bf16[2,32,640]{2,1,0:T(8,128)(2,1)S(1)}, bf16[2,32,640]{2,1,0:T(8,128)(2,1)S(1)}, u32[]{:S(2)}, u32[]{:S(2)}) collective-permute-start(bf16[2,32,640]{2,1,0:T(8,128)(2,1)S(1)} %get-tuple-element.33), channel_id=1, source_target_pairs={{0,6},{1,7},{2,4},{3,5},{4,2},{5,3},{6,0},{7,1},{8,14},{9,15},{10,... | collective-permute-start | bytes 245768 | tf_op jit(solution)/shard_map/gates/ppermute | solution.py:119
  69.7 0.0 copy-start.17
  69.7 0.7 copy-done.17
  70.4 0.1 reshape.143
  70.5 0.6 copy-done.8
  71.1 0.1 mul.108
  71.2 0.0 collective-permute-done.5.refs_5_.refs_0_
  71.2 0.4 collective-permute-done.6.refs_6_.refs_1_
  71.5 2.0 %collective-permute-done.7.refs_7_.refs_2_ = bf16[2,32,640]{2,1,0:T(8,128)(2,1)S(1)} collective-permute-done((bf16[2,32,640]{2,1,0:T(8,128)(2,1)S(1)}, bf16[2,32,640]{2,1,0:T(8,128)(2,1)S(1)}, u32[]{:S(2)}, u32[]{:S(2)}) %collective-permute-start.7) | collective-permute-done | bytes 81952 | tf_op jit(solution)/shard_map/gates/ppermute | solution.py:119
  73.6 8.5 %all-to-all-done.1.recv_ref = bf16[64,8,896]{2,1,0:T(8,128)(2,1)S(1)} async-done(((bf16[64,8,896]{2,1,0:T(8,128)(2,1)}), bf16[64,8,896]{2,1,0:T(8,128)(2,1)S(1)}, u32[]{:S(2)}, u32[]{:S(2)}) %all-to-all-start.1) | async-done | bytes 917536 | tf_op jit(solution)/shard_map/prefix/all_to_all | solution.py:366
  82.1 1.8 %snapshots.1 = bf16[64,8,384]{2,1,0:T(8,128)(2,1)} custom-call(s32[192]{0:T(256)S(1)} %fusion.4.place_ref, bf16[64,8,384]{2,1,0:T(8,128)(2,1)S(1)} %get-tuple-element.37.picked_ref, bf16[64,8,896]{2,1,0:T(8,128)(2,1)S(1)} %all-to-all-done.1.recv_ref, bf16[2,32,640]{2,1,0:T(8,128)(2,1)S(1)} %collective-permute-done.5.refs_5_.refs_0_, ...), custom_call_target="tpu_custom_call" | custom-call | bytes 2000000 | tf_op jit(solution)/shard_map/snapshots/pallas_call | solution.py:464
  83.8 6.3 %all-to-all-start.2 = ((bf16[64,8,384]{2,1,0:T(8,128)(2,1)}), bf16[64,8,384]{2,1,0:T(8,128)(2,1)S(1)}, u32[]{:S(2)}, u32[]{:S(2)}) async-start(bf16[64,8,384]{2,1,0:T(8,128)(2,1)} %snapshots.1), calls=%async_computation.2 | async-start | bytes 786432 | tf_op jit(solution)/shard_map/snapshots/all_to_all | solution.py:366
  90.1 0.0 copy-start.12
  90.2 0.6 copy-done.12
  90.8 0.2 multiply_reduce_fusion
  91.0 0.1 multiply_convert_fusion
  91.0 0.7 convert_element_type.22
  91.7 0.7 fusion.7
  93.1 3.0 %inner.1 = (f32[256,512]{1,0:T(8,128)S(1)}, f32[256,512]{1,0:T(8,128)S(1)}, bf16[256,384]{1,0:T(8,128)(2,1)S(1)}) custom-call(s32[1,3]{1,0:T(1,128)S(1)} %copy-done.11, s32[1]{0:T(128)} %bitcast.1.me_ref, f32[1,8]{1,0:T(1,128)S(1)} %bitcast.22, f32[1,8]{1,0:T(1,128)S(1)} %bitcast.23, bf16[2,32,768]{2,1,0:T(8,128)(2,1)S(1)} %get-tuple-element.23.refs_0_, ...), custom_call_target="tpu_custom_call" | custom-call | flops 400000000 | bytes 1500000 | tf_op jit(solution)/shard_map/inner/pallas_call | solution.py:446
  96.1 0.0 copy-start.2
  96.1 1.1 %outputs.2 = bf16[256,512]{1,0:T(8,128)(2,1)} custom-call(f32[1,512]{1,0:T(1,128)S(1)} %bitcast.20, f32[256,512]{1,0:T(8,128)S(1)} %get-tuple-element.34.base_ref, f32[256,512]{1,0:T(8,128)S(1)} %get-tuple-element.35.factor_ref, bf16[256,384]{1,0:T(8,128)(2,1)S(1)} %get-tuple-element.36.read_ref, bf16[512,896]{1,0:T(8,128)(2,1)S(1)} %bitcast.16), custom_call_target="tpu_custom_call" | custom-call | flops 200000000 | bytes 1500000 | tf_op jit(solution)/shard_map/outputs/pallas_call | solution.py:477
  97.3 9.5 %all-to-all-done.2 = bf16[64,8,384]{2,1,0:T(8,128)(2,1)S(1)} async-done(((bf16[64,8,384]{2,1,0:T(8,128)(2,1)}), bf16[64,8,384]{2,1,0:T(8,128)(2,1)S(1)}, u32[]{:S(2)}, u32[]{:S(2)}) %all-to-all-start.2) | async-done | bytes 393248 | tf_op jit(solution)/shard_map/snapshots/all_to_all | solution.py:366
  106.8 1.1 outputs.3
  (24 shorter events, 0.2 us)
Async XLA Ops:
  0.6 58.3 %copy-start = (bf16[2,128]{1,0:T(2,128)(2,1)S(1)}, bf16[2,128]{1,0:T(2,128)(2,1)}, u32[]{:S(2)}) copy-start(bf16[2,128]{1,0:T(2,128)(2,1)} %param.30) | copy-start | bytes 1540
  0.6 1.2 %copy-start.1 = (f32[4,8,64,128]{3,2,1,0:T(8,128)S(1)}, f32[4,8,64,128]{3,2,1,0:T(8,128)}, u32[]{:S(2)}) copy-start(f32[4,8,64,128]{3,2,1,0:T(8,128)} %param.26) | copy-start | bytes 3145732
  2.7 16.7 %copy-start.3 = (bf16[32,4096]{1,0:T(8,128)(2,1)S(1)}, bf16[32,4096]{1,0:T(8,128)(2,1)}, u32[]{:S(2)}) copy-start(bf16[32,4096]{1,0:T(8,128)(2,1)} %x_ref.1) | copy-start | bytes 786436
  2.8 16.7 %copy-start.5 = (bf16[32,1024]{1,0:T(8,128)(2,1)S(1)}, bf16[32,1024]{1,0:T(8,128)(2,1)}, u32[]{:S(2)}) copy-start(bf16[32,1024]{1,0:T(8,128)(2,1)} %b_ref.1) | copy-start | bytes 196612
  2.8 16.8 %copy-start.7 = (bf16[32,64]{1,0:T(8,128)(2,1)S(1)}, bf16[32,64]{1,0:T(8,128)(2,1)}, u32[]{:S(2)}) copy-start(bf16[32,64]{1,0:T(8,128)(2,1)} %dt_ref.1) | copy-start | bytes 12292
  2.8 37.3 %all-to-all-start = ((bf16[64,8,512]{2,1,0:T(8,128)(2,1)}), bf16[64,8,512]{2,1,0:T(8,128)(2,1)S(1)}, u32[]{:S(2)}, u32[]{:S(2)}) async-start(bf16[64,8,512]{2,1,0:T(8,128)(2,1)} %bitcast.5), calls=%async_computation | async-start | bytes 1048576 | tf_op jit(solution)/shard_map/cache/all_to_all | solution.py:366
  19.6 3.3 %collective-permute-start = (bf16[4,32,768]{2,1,0:T(8,128)(2,1)S(1)}, bf16[4,32,768]{2,1,0:T(8,128)(2,1)S(1)}, u32[]{:S(2)}, u32[]{:S(2)}) collective-permute-start(bf16[4,32,768]{2,1,0:T(8,128)(2,1)S(1)} %get-tuple-element.22), channel_id=1, source_target_pairs={{0,1},{1,0},{2,3},{3,2},{4,5},{5,4},{6,7},{7,6},{8,9},{9,8},{10,11... | collective-permute-start | bytes 589832 | tf_op jit(solution)/shard_map/tokens/ppermute | solution.py:109
  23.0 9.2 %collective-permute-start.1 = (bf16[2,32,768]{2,1,0:T(8,128)(2,1)S(1)}, bf16[2,32,768]{2,1,0:T(8,128)(2,1)S(1)}, u32[]{:S(2)}, u32[]{:S(2)}) collective-permute-start(bf16[2,32,768]{2,1,0:T(8,128)(2,1)S(1)} %get-tuple-element.24), channel_id=1, source_target_pairs={{0,2},{1,3},{2,0},{3,1},{4,6},{5,7},{6,4},{7,5},{8,10},{9,11},{10,... | collective-permute-start | bytes 294920 | tf_op jit(solution)/shard_map/tokens/ppermute | solution.py:119
  26.1 8.1 %collective-permute-start.2 = (bf16[2,32,768]{2,1,0:T(8,128)(2,1)S(1)}, bf16[2,32,768]{2,1,0:T(8,128)(2,1)S(1)}, u32[]{:S(2)}, u32[]{:S(2)}) collective-permute-start(bf16[2,32,768]{2,1,0:T(8,128)(2,1)S(1)} %get-tuple-element.25), channel_id=1, source_target_pairs={{0,4},{1,5},{2,6},{3,7},{4,0},{5,1},{6,2},{7,3},{8,12},{9,13},{10,... | collective-permute-start | bytes 294920 | tf_op jit(solution)/shard_map/tokens/ppermute | solution.py:119
  28.8 7.3 %collective-permute-start.3 = (bf16[2,32,768]{2,1,0:T(8,128)(2,1)S(1)}, bf16[2,32,768]{2,1,0:T(8,128)(2,1)S(1)}, u32[]{:S(2)}, u32[]{:S(2)}) collective-permute-start(bf16[2,32,768]{2,1,0:T(8,128)(2,1)S(1)} %get-tuple-element.26), channel_id=1, source_target_pairs={{0,6},{1,7},{2,4},{3,5},{4,2},{5,3},{6,0},{7,1},{8,14},{9,15},{10,... | collective-permute-start | bytes 294920 | tf_op jit(solution)/shard_map/tokens/ppermute | solution.py:119
  36.2 0.7 copy-start.9
  36.2 0.7 copy-start.11
  40.1 0.7 copy-start.10
  42.3 12.9 %copy-start.19 = (bf16[2,128]{1,0:T(2,128)(2,1)S(1)}, bf16[2,128]{1,0:T(2,128)(2,1)}, u32[]{:S(2)}) copy-start(bf16[2,128]{1,0:T(2,128)(2,1)} %param.29) | copy-start | bytes 1540
  42.3 12.9 %copy-start.16 = (bf16[2,512]{1,0:T(2,128)(2,1)S(1)}, bf16[2,512]{1,0:T(2,128)(2,1)}, u32[]{:S(2)}) copy-start(bf16[2,512]{1,0:T(2,128)(2,1)} %param.27) | copy-start | bytes 6148
  42.3 13.6 %copy-start.14 = (f32[2,8,64,128]{3,2,1,0:T(8,128)S(1)}, f32[2,8,64,128]{3,2,1,0:T(8,128)}, u32[]{:S(2)}) copy-start(f32[2,8,64,128]{3,2,1,0:T(8,128)} %param.32) | copy-start | bytes 1572868
  42.3 39.7 %all-to-all-start.1 = ((bf16[64,8,896]{2,1,0:T(8,128)(2,1)}), bf16[64,8,896]{2,1,0:T(8,128)(2,1)S(1)}, u32[]{:S(2)}, u32[]{:S(2)}) async-start(bf16[64,8,896]{2,1,0:T(8,128)(2,1)} %get-tuple-element.27.after_ref), calls=%async_computation.1 | async-start | bytes 1835008 | tf_op jit(solution)/shard_map/prefix/all_to_all | solution.py:366
  55.2 0.7 copy-start.18
  55.9 1.0 copy-start.4
  55.9 1.0 copy-start.6
  56.9 2.0 %copy-start.13 = (f32[2,8,64,128]{3,2,1,0:T(8,128)}, f32[2,8,64,128]{3,2,1,0:T(8,128)S(1)}, u32[]{:S(2)}) copy-start(f32[2,8,64,128]{3,2,1,0:T(8,128)S(1)} %multiply_add_fusion) | copy-start | bytes 1572868
  57.0 3.3 %collective-permute-start.4 = (bf16[4,32,640]{2,1,0:T(8,128)(2,1)S(1)}, bf16[4,32,640]{2,1,0:T(8,128)(2,1)S(1)}, u32[]{:S(2)}, u32[]{:S(2)}) collective-permute-start(bf16[4,32,640]{2,1,0:T(8,128)(2,1)S(1)} %get-tuple-element.29), channel_id=1, source_target_pairs={{0,1},{1,0},{2,3},{3,2},{4,5},{5,4},{6,7},{7,6},{8,9},{9,8},{10,11... | collective-permute-start | bytes 491528 | tf_op jit(solution)/shard_map/gates/ppermute | solution.py:109
  58.9 0.7 copy-start.15
  60.3 10.9 %collective-permute-start.5 = (bf16[2,32,640]{2,1,0:T(8,128)(2,1)S(1)}, bf16[2,32,640]{2,1,0:T(8,128)(2,1)S(1)}, u32[]{:S(2)}, u32[]{:S(2)}) collective-permute-start(bf16[2,32,640]{2,1,0:T(8,128)(2,1)S(1)} %get-tuple-element.31), channel_id=1, source_target_pairs={{0,2},{1,3},{2,0},{3,1},{4,6},{5,7},{6,4},{7,5},{8,10},{9,11},{10,... | collective-permute-start | bytes 245768 | tf_op jit(solution)/shard_map/gates/ppermute | solution.py:119
  63.7 7.8 %collective-permute-start.6 = (bf16[2,32,640]{2,1,0:T(8,128)(2,1)S(1)}, bf16[2,32,640]{2,1,0:T(8,128)(2,1)S(1)}, u32[]{:S(2)}, u32[]{:S(2)}) collective-permute-start(bf16[2,32,640]{2,1,0:T(8,128)(2,1)S(1)} %get-tuple-element.32), channel_id=1, source_target_pairs={{0,4},{1,5},{2,6},{3,7},{4,0},{5,1},{6,2},{7,3},{8,12},{9,13},{10,... | collective-permute-start | bytes 245768 | tf_op jit(solution)/shard_map/gates/ppermute | solution.py:119
  67.2 6.3 %collective-permute-start.7 = (bf16[2,32,640]{2,1,0:T(8,128)(2,1)S(1)}, bf16[2,32,640]{2,1,0:T(8,128)(2,1)S(1)}, u32[]{:S(2)}, u32[]{:S(2)}) collective-permute-start(bf16[2,32,640]{2,1,0:T(8,128)(2,1)S(1)} %get-tuple-element.33), channel_id=1, source_target_pairs={{0,6},{1,7},{2,4},{3,5},{4,2},{5,3},{6,0},{7,1},{8,14},{9,15},{10,... | collective-permute-start | bytes 245768 | tf_op jit(solution)/shard_map/gates/ppermute | solution.py:119
  69.7 0.7 copy-start.17
  70.4 0.7 copy-start.8
  83.8 23.0 %all-to-all-start.2 = ((bf16[64,8,384]{2,1,0:T(8,128)(2,1)}), bf16[64,8,384]{2,1,0:T(8,128)(2,1)S(1)}, u32[]{:S(2)}, u32[]{:S(2)}) async-start(bf16[64,8,384]{2,1,0:T(8,128)(2,1)} %snapshots.1), calls=%async_computation.2 | async-start | bytes 786432 | tf_op jit(solution)/shard_map/snapshots/all_to_all | solution.py:366
  90.1 0.7 copy-start.12
  96.1 10.7 %copy-start.2 = (f32[4,8,64,128]{3,2,1,0:T(8,128)S(1)}, f32[4,8,64,128]{3,2,1,0:T(8,128)}, u32[]{:S(2)}) copy-start(f32[4,8,64,128]{3,2,1,0:T(8,128)} %param.26) | copy-start | bytes 3145732

commit v5 on v3

--- a/solution.py
+++ b/solution.py
@@ -66,22 +66,33 @@
     return total
 
 
-def pack_tokens(me_ref, after_ref, x_ref, b_ref, dt_ref, keep_ref, give_ref):
-    del after_ref
-    chips = keep_ref.shape[0]
-    heads_dev = dt_ref.shape[1] // (2 * chips)
-    width = x_ref.shape[1] // (2 * chips)
-    raw = dt_ref[...].astype(f32)
+def pack_first(
+    x_ref, b_ref, dt_ref, rate_ref, len_ref, out_ref, meta_ref, xs, bs, steps, rates, lens, sems
+):
+    count = out_ref.shape[0]
+    heads_dev = dt_ref.shape[1] // count
+    width = x_ref.shape[1] // count
+    copies = [
+        pltpu.make_async_copy(src, dst, sems.at[i])
+        for i, (src, dst) in enumerate(
+            ((x_ref, xs), (b_ref, bs), (dt_ref, steps), (rate_ref, rates), (len_ref, lens))
+        )
+    ]
+    for copy in copies:
+        copy.start()
+    for copy in copies:
+        copy.wait()
+    raw = steps[...].astype(f32)
     raw = jnp.concatenate([raw, jnp.zeros((raw.shape[0], STATE - raw.shape[1]), f32)], axis=1)
-    for side, ref in enumerate((keep_ref, give_ref)):
-        for k in range(chips):
-            peer = me_ref[0] ^ (2 * k + side)
-            x_start = pl.multiple_of(peer * width, STATE)
-            b_start = pl.multiple_of(peer * STATE, STATE)
-            ref[k, :, 0:width] = x_ref[:, pl.ds(x_start, width)]
-            ref[k, :, width : width + STATE] = b_ref[:, pl.ds(b_start, STATE)]
-            mine = pltpu.roll(raw, (STATE - peer * heads_dev) % STATE, 1)
-            ref[k, :, width + STATE : width + 2 * STATE] = mine.astype(bf16)
+    for d in range(count):
+        out_ref[d, :, 0:width] = xs[:, d * width : (d + 1) * width]
+        out_ref[d, :, width : width + STATE] = bs[:, d * STATE : (d + 1) * STATE]
+        mine = raw if d == 0 else pltpu.roll(raw, STATE - d * heads_dev, 1)
+        out_ref[d, :, width + STATE : width + 2 * STATE] = mine.astype(bf16)
+    meta_ref[...] = jnp.zeros_like(meta_ref)
+    meta_ref[0:1, 0 : rates.shape[1]] = rates[...]
+    meta_ref[1:2, 0:1] = lens[:, 0:1].astype(f32)
+    meta_ref[2:3, 0:1] = (lens[:, 0:1] + lens[:, 1:2]).astype(f32)
 
 
 def pack_gates(me_ref, after_ref, z_ref, c_ref, keep_ref, give_ref):
@@ -146,9 +157,8 @@
     return (position >= ends[0]).astype(jnp.int32) + (position >= ends[1]).astype(jnp.int32)
 
 
-def segment_ends(len_ref):
-    first = len_ref[0, 0]
-    return first, first + len_ref[0, 1]
+def segment_ends(meta_ref):
+    return meta_ref[1:2, 0:1].astype(jnp.int32), meta_ref[2:3, 0:1].astype(jnp.int32)
 
 
 def spread_heads(heads, width):
@@ -157,17 +167,14 @@
     return (row == column // (width // heads)).astype(bf16)
 
 
-def local_state(len_ref, me_ref, rate_ref, *refs):
-    pair_refs, (send_ref, out_ref, tok_ref, made, sems, last_sem) = refs[:-6], refs[-6:]
+def local_state(meta_ref, tok_ref, send_ref, out_ref):
     del send_ref
     length = tok_ref.shape[0]
-    heads = rate_ref.shape[1]
-    width = heads * HEAD_DIM
-    for copy in fetch(me_ref[0], pair_refs, tok_ref, sems):
-        copy.wait()
-    ends = segment_ends(len_ref)
+    width = out_ref.shape[0]
+    heads = width // HEAD_DIM
+    ends = segment_ends(meta_ref)
     step_size = jax.nn.softplus(tok_ref[:, width + STATE : width + STATE + heads].astype(f32))
-    log_decay = -step_size * rate_ref[...]
+    log_decay = -step_size * meta_ref[0:1, 0:heads]
     row = lax.broadcasted_iota(jnp.int32, (length, length), 0)
     column = lax.broadcasted_iota(jnp.int32, (length, length), 1)
     later = (segment_of(row, ends) == segment_of(column, ends)) & (column > row)
@@ -181,7 +188,7 @@
     b_parts = jnp.concatenate(
         [jnp.where(seg_index == j, b_half, 0.0).astype(bf16) for j in range(REQS)], axis=1
     )
-    made[:, 0 : REQS * STATE] = dot_tn(scaled, b_parts).astype(bf16)
+    out_ref[:, 0 : REQS * STATE] = dot_tn(scaled, b_parts).astype(bf16)
     member = (seg_index == lane % REQS).astype(f32).astype(bf16)
     total = None
     for piece in split(log_decay, 3):
@@ -198,73 +205,37 @@
     row_s = lax.broadcasted_iota(jnp.int32, (width, STATE), 0)
     lane_s = lax.broadcasted_iota(jnp.int32, (width, STATE), 1)
     chosen = jnp.where(lane_s == row_s % ROWS, spread, 0.0).astype(bf16)
-    made[:, REQS * STATE :] = dot(chosen, jnp.ones((STATE, STATE), bf16)).astype(bf16)
-    last = pltpu.make_async_copy(made, out_ref.at[:, REQS * STATE :], last_sem)
-    last.start()
-    last.wait()
-
-
-def pick_prefix(hit_ref, recv_ref, out_ref, picked_ref, held, sem):
+    out_ref[:, REQS * STATE :] = dot(chosen, jnp.ones((STATE, STATE), bf16)).astype(bf16)
+
+
+def combine(hit_ref, place_ref, recv_ref, *refs):
+    out_ref, held = refs[-2:]
     for s in range(recv_ref.shape[0]):
-        block = recv_ref[s].astype(f32)
+        block = recv_ref[s, :, 0 : SLOTS * STATE].astype(f32)
         for k in range(SLOTS):
             held[s * SLOTS + k] = block[:, k * STATE : (k + 1) * STATE]
     for s in range(recv_ref.shape[0]):
-        for j in range(REQS):
-            picked_ref[s, :, j * STATE : (j + 1) * STATE] = held[hit_ref[s * REQS + j]].astype(bf16)
-    copy = pltpu.make_async_copy(picked_ref, out_ref.at[:, :, 0 : REQS * STATE], sem)
-    copy.start()
-    copy.wait()
-
-
-def make_snapshots(place_ref, after_ref, picked_ref, recv_ref, out_ref):
-    del after_ref
-    for s in range(recv_ref.shape[0]):
-        prefix = picked_ref[s].astype(f32)
-        block = recv_ref[s, :, REQS * STATE :].astype(f32)
+        block = recv_ref[s, :, SLOTS * STATE :].astype(f32)
         kept = block[:, REQS * STATE :]
         for j in range(REQS):
-            columns = slice(j * STATE, (j + 1) * STATE)
+            prefix = held[hit_ref[s * REQS + j]]
+            out_ref[s, :, j * STATE : (j + 1) * STATE] = prefix.astype(bf16)
             factor = kept[j : j + 1, :] + kept[REQS + j : REQS + j + 1, :]
-            new = factor * prefix[:, columns] + block[:, columns]
+            new = factor * prefix + block[:, j * STATE : (j + 1) * STATE]
             place = place_ref[s * REQS + j]
-            start = pl.multiple_of((place & 3) * STATE, STATE)
+            start = pl.multiple_of((REQS + (place & 3)) * STATE, STATE)
             out_ref[place >> 2, :, pl.ds(start, STATE)] = new.astype(bf16)
 
 
-def write_cache(missing_ref, cache_ref, recv_ref, out_ref):
-    missing = missing_ref[0]
-    for s in range(SLOTS):
-
-        @pl.when(missing == s)
-        def _():
-            out_ref[s] = cache_ref[s]
-
-        if s < REQS:
-
-            @pl.when(missing > s)
-            def _():
-                out_ref[s] = recv_ref[:, s * STATE : (s + 1) * STATE].astype(f32)
-
-        if s > 0:
-
-            @pl.when(missing < s)
-            def _():
-                out_ref[s] = recv_ref[:, (s - 1) * STATE : s * STATE].astype(f32)
-
-
-def token_inner(len_ref, me_ref, rate_ref, skip_ref, *refs):
-    pair_refs, (base_ref, factor_ref, read_ref, tok_ref, gates, sems) = refs[:-6], refs[-6:]
-    chips = len(pair_refs) // 2
+def token_inner(me_ref, meta_ref, skip_ref, tok_ref, *refs):
+    pair_refs, (base_ref, factor_ref, read_ref, gates, sems) = refs[:-5], refs[-5:]
     length = tok_ref.shape[0]
-    heads = rate_ref.shape[1]
+    heads = skip_ref.shape[1]
     width = heads * HEAD_DIM
-    for copy in fetch(me_ref[0], pair_refs[:chips], tok_ref, sems.at[0]):
-        copy.wait()
-    copies = fetch(me_ref[0], pair_refs[chips:], gates, sems.at[1])
-    ends = segment_ends(len_ref)
+    copies = fetch(me_ref[0], pair_refs, gates, sems)
+    ends = segment_ends(meta_ref)
     step_size = jax.nn.softplus(tok_ref[:, width + STATE : width + STATE + heads].astype(f32))
-    log_decay = -step_size * rate_ref[...]
+    log_decay = -step_size * meta_ref[0:1, 0:heads]
     row = lax.broadcasted_iota(jnp.int32, (length, length), 0)
     column = lax.broadcasted_iota(jnp.int32, (length, length), 1)
     upto = (segment_of(row, ends) == segment_of(column, ends)) & (column <= row)
@@ -292,11 +263,41 @@
     factor_ref[...] = gate * decay
 
 
-def token_outputs(gain_ref, base_ref, factor_ref, read_ref, recv_ref, out_ref):
-    carried = dot_nt(read_ref[...], recv_ref[:, 0 : REQS * STATE])
+def finish(
+    missing_ref, cache_ref, gain_ref, base_ref, factor_ref, read_ref, recv_ref,
+    rows_ref, states_ref, rows, states, sems,
+):
+    missing = missing_ref[0]
+    first = REQS * STATE
+    copies = []
+    for s in range(SLOTS):
+
+        @pl.when(missing == s)
+        def _():
+            states[s] = cache_ref[s]
+
+        if s < REQS:
+
+            @pl.when(missing > s)
+            def _():
+                states[s] = recv_ref[:, first + s * STATE : first + (s + 1) * STATE].astype(f32)
+
+        if s > 0:
+
+            @pl.when(missing < s)
+            def _():
+                states[s] = recv_ref[:, first + (s - 1) * STATE : first + s * STATE].astype(f32)
+
+        copies.append(pltpu.make_async_copy(states.at[s], states_ref.at[s], sems.at[s]))
+        copies[-1].start()
+    carried = dot_nt(read_ref[...], recv_ref[:, 0:first])
     gated = base_ref[...] + factor_ref[...] * carried
     square_mean = jnp.mean(gated * gated, axis=1, keepdims=True)
-    out_ref[...] = (gated * lax.rsqrt(square_mean + 1e-05) * gain_ref[...]).astype(bf16)
+    rows[...] = (gated * lax.rsqrt(square_mean + 1e-05) * gain_ref[...]).astype(bf16)
+    copies.append(pltpu.make_async_copy(rows, rows_ref, sems.at[SLOTS]))
+    copies[-1].start()
+    for copy in copies:
+        copy.wait()
 
 
 def gated_norm(values, gate_in, norm_weight):
@@ -359,15 +360,46 @@
     heads = cache_states.shape[1]
     width = heads * HEAD_DIM
     length = rows * n_head
-    tiles = 2 * REQS + 1
+    tiles = SLOTS + REQS + 1
     shape = jax.ShapeDtypeStruct
 
-    def swap(value):
-        return lax.all_to_all(value, "serve", split_axis=0, concat_axis=0, tiled=True)
+    def swap(value, axis):
+        return lax.all_to_all(value, axis, split_axis=0, concat_axis=0, tiled=True)
 
     chips = n_head // 2
+    with jax.named_scope("tokens"):
+        first, meta = pl.pallas_call(
+            pack_first,
+            out_shape=(
+                shape((n_head, rows, width + 2 * STATE), bf16),
+                shape((8, STATE), f32),
+            ),
+            in_specs=[HBM] * 5,
+            out_specs=(VMEM, VMEM),
+            scratch_shapes=[
+                pltpu.VMEM(pre_x.shape, bf16),
+                pltpu.VMEM(pre_b.shape, bf16),
+                pltpu.VMEM(pre_dt.shape, bf16),
+                pltpu.VMEM((1, heads), f32),
+                pltpu.VMEM(suffix_lengths.shape, jnp.int32),
+                pltpu.SemaphoreType.DMA((5,)),
+            ],
+            compiler_params=params(56),
+            cost_estimate=cost(0, 800_000),
+        )(pre_x, pre_b, pre_dt, decay_rate.reshape(1, heads), suffix_lengths)
+        tokens = swap(first, "head").reshape(length, width + 2 * STATE)
+    with jax.named_scope("cache"):
+        cache_rows = cache_states.reshape(SLOTS, width, STATE)
+        send = pl.pallas_call(
+            pack_cache,
+            out_shape=shape((width, tiles * STATE), bf16),
+            grid=(1,),
+            in_specs=[VMEM],
+            out_specs=pl.BlockSpec((width, SLOTS * STATE), lambda i: (0, 0)),
+            compiler_params=params(),
+            cost_estimate=cost(0, 1_600_000),
+        )(cache_rows)
     with jax.named_scope("orders"):
-        head_me = lax.axis_index("head").astype(jnp.int32).reshape(1)
         rank = jnp.sum(
             (snapshot_slots[None, :] < snapshot_slots[:, None]).astype(jnp.int32), axis=1
         )
@@ -377,61 +409,19 @@
             sum(range(SLOTS))
             - jnp.sum(jnp.where(snapshot_slots // SLOTS == serve_me, snapshot_slots % SLOTS, 0))
         ).reshape(1)
-    with jax.named_scope("cache"):
-        cache_rows = cache_states.reshape(SLOTS, width, STATE)
-        spread = pl.pallas_call(
-            pack_cache,
-            out_shape=shape((width, SLOTS * STATE), bf16),
-            in_specs=[VMEM],
-            out_specs=VMEM,
-            compiler_params=params(),
-            cost_estimate=cost(0, 1_600_000),
-        )(cache_rows)
-        pieces = swap(spread.reshape(n_serve, ROWS, SLOTS * STATE))
-    with jax.named_scope("tokens"):
-        keep, give = pl.pallas_call(
-            pack_tokens,
-            out_shape=[shape((chips, rows, width + 2 * STATE), bf16)] * 2,
-            in_specs=[SMEM, ANY] + [VMEM] * 3,
-            out_specs=[VMEM] * 2,
-            compiler_params=params(),
-            cost_estimate=cost(0, 800_000),
-        )(head_me, spread, pre_x, pre_b, pre_dt)
-        tokens = exchange(keep, give, n_head)
-    rates = decay_rate.reshape(1, heads)
-    with jax.named_scope("prefix"):
-        send, picked = pl.pallas_call(
-            pick_prefix,
-            out_shape=(
-                shape((n_serve, ROWS, tiles * STATE), bf16),
-                shape((n_serve, ROWS, REQS * STATE), bf16),
-            ),
-            in_specs=[SMEM, VMEM],
-            out_specs=(HBM, VMEM),
-            scratch_shapes=[
-                pltpu.VMEM((n_serve * SLOTS, ROWS, STATE), f32),
-                pltpu.SemaphoreType.DMA,
-            ],
-            compiler_params=params(),
-            cost_estimate=cost(0, 2_000_000),
-        )(prefix_hits, pieces)
+        head_me = lax.axis_index("head").astype(jnp.int32).reshape(1)
     with jax.named_scope("local"):
         send = pl.pallas_call(
             local_state,
             out_shape=shape((width, tiles * STATE), bf16),
-            in_specs=[SMEM] * 2 + [VMEM] + [ANY] * chips + [HBM],
-            out_specs=HBM,
-            scratch_shapes=[
-                pltpu.VMEM((length, width + 2 * STATE), bf16),
-                pltpu.VMEM((width, (REQS + 1) * STATE), bf16),
-                pltpu.SemaphoreType.DMA((n_head,)),
-                pltpu.SemaphoreType.DMA,
-            ],
-            input_output_aliases={3 + chips: 0},
+            grid=(1,),
+            in_specs=[VMEM, VMEM, ANY],
+            out_specs=pl.BlockSpec((width, SLOTS * STATE), lambda i: (0, 1)),
+            input_output_aliases={2: 0},
             compiler_params=params(),
             cost_estimate=cost(300_000_000, 800_000),
-        )(suffix_lengths, head_me, rates, *tokens, send.reshape(width, tiles * STATE))
-        got = swap(send.reshape(n_serve, ROWS, tiles * STATE))
+        )(meta, tokens, send)
+        pieces = swap(send.reshape(n_serve, ROWS, tiles * STATE), "serve")
     with jax.named_scope("gates"):
         keep, give = pl.pallas_call(
             pack_gates,
@@ -442,6 +432,17 @@
             cost_estimate=cost(0, 650_000),
         )(head_me, send, pre_z, pre_c)
         gates = exchange(keep, give, n_head)
+    with jax.named_scope("combine"):
+        answer = pl.pallas_call(
+            combine,
+            out_shape=shape((n_serve, ROWS, 2 * REQS * STATE), bf16),
+            in_specs=[SMEM, SMEM, VMEM] + [ANY] * (chips - 1),
+            out_specs=VMEM,
+            scratch_shapes=[pltpu.VMEM((n_serve * SLOTS, ROWS, STATE), f32)],
+            compiler_params=params(),
+            cost_estimate=cost(0, 4_000_000),
+        )(prefix_hits, place, pieces, *gates[1:])
+        got = swap(answer, "serve").reshape(width, 2 * REQS * STATE)
     with jax.named_scope("inner"):
         base, factor, read = pl.pallas_call(
             token_inner,
@@ -450,46 +451,33 @@
                 shape((length, width), f32),
                 shape((length, REQS * STATE), bf16),
             ),
-            in_specs=[SMEM] * 2 + [VMEM] * 2 + [ANY] * n_head,
+            in_specs=[SMEM] + [VMEM] * 3 + [ANY] * chips,
             out_specs=[VMEM] * 3,
             scratch_shapes=[
-                pltpu.VMEM((length, width + 2 * STATE), bf16),
                 pltpu.VMEM((length, width + STATE), bf16),
-                pltpu.SemaphoreType.DMA((2, n_head)),
+                pltpu.SemaphoreType.DMA((n_head,)),
             ],
             compiler_params=params(),
             cost_estimate=cost(400_000_000, 1_500_000),
-        )(suffix_lengths, head_me, rates, d_skip.reshape(1, heads), *tokens, *gates)
-    with jax.named_scope("snapshots"):
-        answer = pl.pallas_call(
-            make_snapshots,
-            out_shape=shape((n_serve, ROWS, REQS * STATE), bf16),
-            in_specs=[SMEM, ANY, VMEM, VMEM],
-            out_specs=VMEM,
-            compiler_params=params(),
-            cost_estimate=cost(0, 2_000_000),
-        )(place, read, picked, got)
-        new = swap(answer).reshape(width, REQS * STATE)
+        )(head_me, meta, d_skip.reshape(1, heads), tokens, *gates)
     dec_out, dec_new = decode_block(
         dec_x, dec_z, dec_b, dec_c, dec_dt, dec_states, decay_rate, d_skip, norm_weight
     )
     with jax.named_scope("outputs"):
-        pre_out = pl.pallas_call(
-            token_outputs,
-            out_shape=shape((length, width), bf16),
-            in_specs=[VMEM] * 5,
-            out_specs=VMEM,
+        pre_out, cache_out = pl.pallas_call(
+            finish,
+            out_shape=(shape((length, width), bf16), shape((SLOTS, width, STATE), f32)),
+            in_specs=[SMEM] + [VMEM] * 6,
+            out_specs=(HBM, HBM),
+            scratch_shapes=[
+                pltpu.VMEM((length, width), bf16),
+                pltpu.VMEM((SLOTS, width, STATE), f32),
+                pltpu.SemaphoreType.DMA((SLOTS + 1,)),
+            ],
             compiler_params=params(),
-            cost_estimate=cost(200_000_000, 1_500_000),
-        )(norm_weight.reshape(1, width), base, factor, read, got.reshape(width, tiles * STATE))
-        cache_out = pl.pallas_call(
-            write_cache,
-            out_shape=shape((SLOTS, width, STATE), f32),
-            in_specs=[SMEM, VMEM, VMEM],
-            out_specs=VMEM,
-            compiler_params=params(),
-            cost_estimate=cost(0, 2_500_000),
-        )(missing, cache_rows, new).reshape(cache_states.shape)
+            cost_estimate=cost(200_000_000, 4_000_000),
+        )(missing, cache_rows, norm_weight.reshape(1, width), base, factor, read, got)
+        cache_out = cache_out.reshape(cache_states.shape)
     return (pre_out, cache_out, dec_out, dec_new)
 
 

time: 110 us -> 99.5 us (0.905)
  the two profiles are of different devices: /device:TPU:6 before, /device:TPU:16 now
where the time goes in v5:
time: 99.5 us; the launch traced here: 98.7 us
  starting transfers between devices  38.9 us (39%)
  waiting for transfers between devices  38.3 us (38%)
  Pallas kernels  10.2 us (10%)
  local copies, waits for them, and re-layouts  7.69 us (8%)
  between operations  1.5 us (2%)
  other arithmetic  1.38 us (1%)
    all_to_all x3, waiting for transfers between devices, swap(): return lax.all_to_all(value, axis, split_axis=0, concat_axis=0, tiled=True)  33.6 us
    all_to_all x3, starting transfers between devices, swap(): return lax.all_to_all(value, axis, split_axis=0, concat_axis=0, tiled=True)  26.6 us
    ppermute x3, starting transfers between devices, exchange(): lax.ppermute(pairs[k], 'head', [(i, i ^ 2 * k) for i in range(n_head)])  10.4 us
    unnamed x48, local copies, waits for them, and re-layouts  6.79 us
    ppermute x3, waiting for transfers between devices, exchange(): lax.ppermute(pairs[k], 'head', [(i, i ^ 2 * k) for i in range(n_head)])  3.5 us
    pallas_call x1, Pallas kernels, local(): pl.pallas_call(combine, out_shape=shape((n_serve, ROWS, 2 * REQS * STATE)...  2.14 us
    pallas_call x1, Pallas kernels, local(): pl.pallas_call(local_state, out_shape=shape((width, tiles * STATE), bf16)...  2.08 us
  transfers between devices with their start and end apart: 7, of which 5 were waited for; matrix products, arithmetic and copies ran while one was open for 3% of the time, Pallas kernels for 3%

profile of v5, /device:TPU:16, one launch (start us, length us, event | category | flops | bytes accessed | tf_op | source)
XLA Modules:
  0.0 98.7 jit_solution(16319643803989405295)
XLA Ops:
  0.6 0.0 copy-start
  0.6 0.0 copy-start.1
  0.7 1.9 %tokens.1 = (bf16[8,32,768]{2,1,0:T(8,128)(2,1)}, f32[8,128]{1,0:T(8,128)}) custom-call(bf16[32,4096]{1,0:T(8,128)(2,1)} %x_ref.1, bf16[32,1024]{1,0:T(8,128)(2,1)} %b_ref.1, bf16[32,64]{1,0:T(8,128)(2,1)} %dt_ref.1, f32[1,8]{1,0:T(1,128)} %bitcast.23, s32[1,3]{1,0:T(1,128)} %len_ref.1), custom_call_target="tpu_custom_call" | custom-call | bytes 800000 | tf_op jit(solution)/shard_map/tokens/pallas_call | solution.py:371
  2.6 4.3 %all-to-all-start = ((bf16[8,32,768]{2,1,0:T(8,128)(2,1)}), bf16[8,32,768]{2,1,0:T(8,128)(2,1)S(1)}, u32[]{:S(2)}, u32[]{:S(2)}) async-start(bf16[8,32,768]{2,1,0:T(8,128)(2,1)} %get-tuple-element.18), calls=%async_computation | async-start | bytes 786432 | tf_op jit(solution)/shard_map/tokens/all_to_all | solution.py:367
  6.9 0.0 copy-done.1
  6.9 0.0 copy-start.11
  6.9 0.9 cache.1.send_ref
  7.8 8.1 %all-to-all-done = bf16[8,32,768]{2,1,0:T(8,128)(2,1)S(1)} async-done(((bf16[8,32,768]{2,1,0:T(8,128)(2,1)}), bf16[8,32,768]{2,1,0:T(8,128)(2,1)S(1)}, u32[]{:S(2)}, u32[]{:S(2)}) %all-to-all-start) | async-done | bytes 393248 | tf_op jit(solution)/shard_map/tokens/all_to_all | solution.py:367
  15.8 0.0 copy-done.11
  15.8 2.1 %local.1.after_ref = bf16[512,1024]{1,0:T(8,128)(2,1)} custom-call(f32[8,128]{1,0:T(8,128)S(1)} %copy-done.11, bf16[256,768]{1,0:T(8,128)(2,1)S(1)} %bitcast.18, bf16[512,1024]{1,0:T(8,128)(2,1)} %cache.1.send_ref), custom_call_target="tpu_custom_call", output_to_operand_aliasing={{}: (2, {})} | custom-call | flops 300000000 | bytes 800000 | tf_op jit(solution)/shard_map/local/pallas_call | solution.py:414
  17.9 16.6 %all-to-all-start.1 = ((bf16[64,8,1024]{2,1,0:T(8,128)(2,1)}), bf16[64,8,1024]{2,1,0:T(8,128)(2,1)S(1)}, u32[]{:S(2)}, u32[]{:S(2)}) async-start(bf16[64,8,1024]{2,1,0:T(8,128)(2,1)} %bitcast.7), calls=%async_computation.1 | async-start | bytes 2097152 | tf_op jit(solution)/shard_map/local/all_to_all | solution.py:367
  34.5 0.0 copy-done.2
  34.6 0.0 copy-done.9
  34.6 0.0 copy-start.18
  34.6 1.9 %collective-permute-start = (bf16[4,32,640]{2,1,0:T(8,128)(2,1)S(1)}, bf16[4,32,640]{2,1,0:T(8,128)(2,1)S(1)}, u32[]{:S(2)}, u32[]{:S(2)}) collective-permute-start(bf16[4,32,640]{2,1,0:T(8,128)(2,1)S(1)} %get-tuple-element.20), channel_id=1, source_target_pairs={{0,1},{1,0},{2,3},{3,2},{4,5},{5,4},{6,7},{7,6},{8,9},{9,8},{10,11... | collective-permute-start | bytes 491528 | tf_op jit(solution)/shard_map/gates/ppermute | solution.py:120
  36.6 0.0 copy-done.18
  36.6 0.2 convert_reduce_fusion
  36.8 1.2 %collective-permute-done.got_ref = bf16[4,32,640]{2,1,0:T(8,128)(2,1)S(1)} collective-permute-done((bf16[4,32,640]{2,1,0:T(8,128)(2,1)S(1)}, bf16[4,32,640]{2,1,0:T(8,128)(2,1)S(1)}, u32[]{:S(2)}, u32[]{:S(2)}) %collective-permute-start) | collective-permute-done | bytes 163872 | tf_op jit(solution)/shard_map/gates/ppermute | solution.py:120
  37.9 0.0 copy-start.14
  38.0 0.6 copy-done.14
  38.6 2.5 %collective-permute-start.1 = (bf16[2,32,640]{2,1,0:T(8,128)(2,1)S(1)}, bf16[2,32,640]{2,1,0:T(8,128)(2,1)S(1)}, u32[]{:S(2)}, u32[]{:S(2)}) collective-permute-start(bf16[2,32,640]{2,1,0:T(8,128)(2,1)S(1)} %get-tuple-element.22), channel_id=1, source_target_pairs={{0,2},{1,3},{2,0},{3,1},{4,6},{5,7},{6,4},{7,5},{8,10},{9,11},{10,... | collective-permute-start | bytes 245768 | tf_op jit(solution)/shard_map/gates/ppermute | solution.py:130
  41.1 4.0 %collective-permute-start.2 = (bf16[2,32,640]{2,1,0:T(8,128)(2,1)S(1)}, bf16[2,32,640]{2,1,0:T(8,128)(2,1)S(1)}, u32[]{:S(2)}, u32[]{:S(2)}) collective-permute-start(bf16[2,32,640]{2,1,0:T(8,128)(2,1)S(1)} %get-tuple-element.23), channel_id=1, source_target_pairs={{0,4},{1,5},{2,6},{3,7},{4,0},{5,1},{6,2},{7,3},{8,12},{9,13},{10,... | collective-permute-start | bytes 245768 | tf_op jit(solution)/shard_map/gates/ppermute | solution.py:130
  45.0 0.0 copy-start.12
  45.0 4.0 %collective-permute-start.3 = (bf16[2,32,640]{2,1,0:T(8,128)(2,1)S(1)}, bf16[2,32,640]{2,1,0:T(8,128)(2,1)S(1)}, u32[]{:S(2)}, u32[]{:S(2)}) collective-permute-start(bf16[2,32,640]{2,1,0:T(8,128)(2,1)S(1)} %get-tuple-element.24), channel_id=1, source_target_pairs={{0,6},{1,7},{2,4},{3,5},{4,2},{5,3},{6,0},{7,1},{8,14},{9,15},{10,... | collective-permute-start | bytes 245768 | tf_op jit(solution)/shard_map/gates/ppermute | solution.py:130
  49.1 0.0 collective-permute-done.1.refs_1_.refs_0_
  49.1 0.0 copy-start.3
  49.1 0.0 collective-permute-done.2.refs_2_.refs_1_
  49.1 0.0 copy-start.5
  49.1 3.5 %collective-permute-done.3.refs_3_.refs_2_ = bf16[2,32,640]{2,1,0:T(8,128)(2,1)S(1)} collective-permute-done((bf16[2,32,640]{2,1,0:T(8,128)(2,1)S(1)}, bf16[2,32,640]{2,1,0:T(8,128)(2,1)S(1)}, u32[]{:S(2)}, u32[]{:S(2)}) %collective-permute-start.3) | collective-permute-done | bytes 81952 | tf_op jit(solution)/shard_map/gates/ppermute | solution.py:130
  52.6 12.2 %all-to-all-done.1.recv_ref = bf16[64,8,1024]{2,1,0:T(8,128)(2,1)S(1)} async-done(((bf16[64,8,1024]{2,1,0:T(8,128)(2,1)}), bf16[64,8,1024]{2,1,0:T(8,128)(2,1)S(1)}, u32[]{:S(2)}, u32[]{:S(2)}) %all-to-all-start.1) | async-done | bytes 1048608 | tf_op jit(solution)/shard_map/local/all_to_all | solution.py:367
  64.8 0.0 copy-done.12
  64.8 2.1 %combine.1 = bf16[64,8,768]{2,1,0:T(8,128)(2,1)} custom-call(s32[192]{0:T(256)S(1)} %copy-done.12, s32[192]{0:T(256)S(1)} %fusion.4.place_ref, bf16[64,8,1024]{2,1,0:T(8,128)(2,1)S(1)} %all-to-all-done.1.recv_ref, bf16[2,32,640]{2,1,0:T(8,128)(2,1)S(1)} %collective-permute-done.1.refs_1_.refs_0_, ...), custom_call_target="tpu_custom_call" | custom-call | bytes 4000000 | tf_op jit(solution)/shard_map/combine/pallas_call | solution.py:436
  67.0 0.0 copy-done.7
  67.0 0.0 copy-start.19
  67.0 0.0 copy-start.22
  67.0 0.0 copy-start.21
  67.0 0.0 copy-start.17
  67.0 5.7 %all-to-all-start.2 = ((bf16[64,8,768]{2,1,0:T(8,128)(2,1)}), bf16[64,8,768]{2,1,0:T(8,128)(2,1)S(1)}, u32[]{:S(2)}, u32[]{:S(2)}) async-start(bf16[64,8,768]{2,1,0:T(8,128)(2,1)} %combine.1), calls=%async_computation.2 | async-start | bytes 1572864 | tf_op jit(solution)/shard_map/combine/all_to_all | solution.py:367
  72.7 0.0 copy-done.19
  72.7 0.0 copy-done.22
  72.8 0.0 copy-start.20
  72.8 0.7 copy-done.20
  73.4 0.1 reshape.137
  73.5 0.6 copy-done.23
  74.1 0.0 copy-done.21
  74.1 0.1 reshape.139
  74.2 0.6 copy-done.10
  74.8 0.1 mul.108
  74.9 0.1 broadcast_multiply_fusion
  74.9 0.2 multiply_add_fusion
  75.2 0.0 copy-start.16
  75.2 0.7 fusion.5
  75.9 0.7 copy-done.13
  76.6 0.2 multiply_reduce_fusion
  76.8 0.1 multiply_convert_fusion
  76.8 0.7 convert_element_type.22
  77.5 0.6 fusion.7
  78.7 0.9 copy-done.4
  79.6 0.9 copy-done.6
  80.5 0.9 copy-done.8
  81.3 0.9 copy-done.15
  82.2 1.9 %inner.1 = (f32[256,512]{1,0:T(8,128)S(1)}, f32[256,512]{1,0:T(8,128)S(1)}, bf16[256,384]{1,0:T(8,128)(2,1)S(1)}) custom-call(s32[1]{0:T(128)} %bitcast.3.me_ref, f32[8,128]{1,0:T(8,128)S(1)} %copy-done.11, f32[1,8]{1,0:T(1,128)S(1)} %bitcast.21, bf16[256,768]{1,0:T(8,128)(2,1)S(1)} %bitcast.19, bf16[2,32,640]{2,1,0:T(8,128)(2,1)S(1)} %copy-done.15, ...), custom_call_target="tpu_custom_call" | custom-call | flops 400000000 | bytes 1500000 | tf_op jit(solution)/shard_map/inner/pallas_call | solution.py:447
  84.1 13.3 %all-to-all-done.2 = bf16[64,8,768]{2,1,0:T(8,128)(2,1)S(1)} async-done(((bf16[64,8,768]{2,1,0:T(8,128)(2,1)}), bf16[64,8,768]{2,1,0:T(8,128)(2,1)S(1)}, u32[]{:S(2)}, u32[]{:S(2)}) %all-to-all-start.2) | async-done | bytes 786464 | tf_op jit(solution)/shard_map/combine/all_to_all | solution.py:367
  97.4 1.3 %outputs.1 = (bf16[256,512]{1,0:T(8,128)(2,1)}, f32[4,512,128]{2,1,0:T(8,128)}) custom-call(s32[1]{0:T(128)} %bitcast.missing_ref, f32[4,512,128]{2,1,0:T(8,128)S(1)} %bitcast.16, f32[1,512]{1,0:T(1,128)S(1)} %bitcast.20, f32[256,512]{1,0:T(8,128)S(1)} %get-tuple-element.25.base_ref, f32[256,512]{1,0:T(8,128)S(1)} %get-tuple-element.26.factor_ref, ...), custom_call_target="tpu_custom_call" | custom-call | flops 200000000 | bytes 4000000 | tf_op jit(solution)/shard_map/outputs/pallas_call | solution.py:467
  (21 shorter events, 0.1 us)
Async XLA Ops:
  0.6 74.5 %copy-start = (bf16[2,128]{1,0:T(2,128)(2,1)S(1)}, bf16[2,128]{1,0:T(2,128)(2,1)}, u32[]{:S(2)}) copy-start(bf16[2,128]{1,0:T(2,128)(2,1)} %param.30) | copy-start | bytes 1540
  0.6 6.3 %copy-start.1 = (f32[4,8,64,128]{3,2,1,0:T(8,128)S(1)}, f32[4,8,64,128]{3,2,1,0:T(8,128)}, u32[]{:S(2)}) copy-start(f32[4,8,64,128]{3,2,1,0:T(8,128)} %param.26) | copy-start | bytes 3145732
  2.6 13.3 %all-to-all-start = ((bf16[8,32,768]{2,1,0:T(8,128)(2,1)}), bf16[8,32,768]{2,1,0:T(8,128)(2,1)S(1)}, u32[]{:S(2)}, u32[]{:S(2)}) async-start(bf16[8,32,768]{2,1,0:T(8,128)(2,1)} %get-tuple-element.18), calls=%async_computation | async-start | bytes 786432 | tf_op jit(solution)/shard_map/tokens/all_to_all | solution.py:367
  6.9 8.9 %copy-start.11 = (f32[8,128]{1,0:T(8,128)S(1)}, f32[8,128]{1,0:T(8,128)}, u32[]{:S(2)}) copy-start(f32[8,128]{1,0:T(8,128)} %get-tuple-element.17.meta_ref) | copy-start | bytes 12292
  17.9 16.6 %copy-start.2 = (bf16[32,4096]{1,0:T(8,128)(2,1)S(1)}, bf16[32,4096]{1,0:T(8,128)(2,1)}, u32[]{:S(2)}) copy-start(bf16[32,4096]{1,0:T(8,128)(2,1)} %z_ref.1) | copy-start | bytes 786436
  17.9 16.6 %copy-start.9 = (bf16[32,1024]{1,0:T(8,128)(2,1)S(1)}, bf16[32,1024]{1,0:T(8,128)(2,1)}, u32[]{:S(2)}) copy-start(bf16[32,1024]{1,0:T(8,128)(2,1)} %c_ref.1) | copy-start | bytes 196612
  17.9 46.9 %all-to-all-start.1 = ((bf16[64,8,1024]{2,1,0:T(8,128)(2,1)}), bf16[64,8,1024]{2,1,0:T(8,128)(2,1)S(1)}, u32[]{:S(2)}, u32[]{:S(2)}) async-start(bf16[64,8,1024]{2,1,0:T(8,128)(2,1)} %bitcast.7), calls=%async_computation.1 | async-start | bytes 2097152 | tf_op jit(solution)/shard_map/local/all_to_all | solution.py:367
  34.6 1.9 %copy-start.18 = (s32[192]{0:T(256)S(1)}, s32[192]{0:T(256)}, u32[]{:S(2)}) copy-start(s32[192]{0:T(256)} %param.25) | copy-start | bytes 2308
  34.6 3.3 %collective-permute-start = (bf16[4,32,640]{2,1,0:T(8,128)(2,1)S(1)}, bf16[4,32,640]{2,1,0:T(8,128)(2,1)S(1)}, u32[]{:S(2)}, u32[]{:S(2)}) collective-permute-start(bf16[4,32,640]{2,1,0:T(8,128)(2,1)S(1)} %get-tuple-element.20), channel_id=1, source_target_pairs={{0,1},{1,0},{2,3},{3,2},{4,5},{5,4},{6,7},{7,6},{8,9},{9,8},{10,11... | collective-permute-start | bytes 491528 | tf_op jit(solution)/shard_map/gates/ppermute | solution.py:120
  37.9 0.6 copy-start.14
  38.6 10.5 %collective-permute-start.1 = (bf16[2,32,640]{2,1,0:T(8,128)(2,1)S(1)}, bf16[2,32,640]{2,1,0:T(8,128)(2,1)S(1)}, u32[]{:S(2)}, u32[]{:S(2)}) collective-permute-start(bf16[2,32,640]{2,1,0:T(8,128)(2,1)S(1)} %get-tuple-element.22), channel_id=1, source_target_pairs={{0,2},{1,3},{2,0},{3,1},{4,6},{5,7},{6,4},{7,5},{8,10},{9,11},{10,... | collective-permute-start | bytes 245768 | tf_op jit(solution)/shard_map/gates/ppermute | solution.py:130
  41.1 8.0 %collective-permute-start.2 = (bf16[2,32,640]{2,1,0:T(8,128)(2,1)S(1)}, bf16[2,32,640]{2,1,0:T(8,128)(2,1)S(1)}, u32[]{:S(2)}, u32[]{:S(2)}) collective-permute-start(bf16[2,32,640]{2,1,0:T(8,128)(2,1)S(1)} %get-tuple-element.23), channel_id=1, source_target_pairs={{0,4},{1,5},{2,6},{3,7},{4,0},{5,1},{6,2},{7,3},{8,12},{9,13},{10,... | collective-permute-start | bytes 245768 | tf_op jit(solution)/shard_map/gates/ppermute | solution.py:130
  45.0 19.8 %copy-start.12 = (s32[192]{0:T(256)S(1)}, s32[192]{0:T(256)}, u32[]{:S(2)}) copy-start(s32[192]{0:T(256)} %hit_ref.1) | copy-start | bytes 2308
  45.0 7.5 %collective-permute-start.3 = (bf16[2,32,640]{2,1,0:T(8,128)(2,1)S(1)}, bf16[2,32,640]{2,1,0:T(8,128)(2,1)S(1)}, u32[]{:S(2)}, u32[]{:S(2)}) collective-permute-start(bf16[2,32,640]{2,1,0:T(8,128)(2,1)S(1)} %get-tuple-element.24), channel_id=1, source_target_pairs={{0,6},{1,7},{2,4},{3,5},{4,2},{5,3},{6,0},{7,1},{8,14},{9,15},{10,... | collective-permute-start | bytes 245768 | tf_op jit(solution)/shard_map/gates/ppermute | solution.py:130
  49.1 17.9 %copy-start.3 = (bf16[2,32,640]{2,1,0:T(8,128)(2,1)}, bf16[2,32,640]{2,1,0:T(8,128)(2,1)S(1)}, u32[]{:S(2)}) copy-start(bf16[2,32,640]{2,1,0:T(8,128)(2,1)S(1)} %collective-permute-done.1.refs_1_.refs_0_) | copy-start | bytes 245764
  49.1 17.9 %copy-start.5 = (bf16[2,32,640]{2,1,0:T(8,128)(2,1)}, bf16[2,32,640]{2,1,0:T(8,128)(2,1)S(1)}, u32[]{:S(2)}) copy-start(bf16[2,32,640]{2,1,0:T(8,128)(2,1)S(1)} %collective-permute-done.2.refs_2_.refs_1_) | copy-start | bytes 245764
  52.6 14.4 %copy-start.7 = (bf16[2,32,640]{2,1,0:T(8,128)(2,1)}, bf16[2,32,640]{2,1,0:T(8,128)(2,1)S(1)}, u32[]{:S(2)}) copy-start(bf16[2,32,640]{2,1,0:T(8,128)(2,1)S(1)} %collective-permute-done.3.refs_3_.refs_2_) | copy-start | bytes 245764
  67.0 5.7 %copy-start.19 = (f32[8]{0:T(128)S(1)}, f32[8]{0:T(128)}, u32[]{:S(2)}) copy-start(f32[8]{0:T(128)} %param.33) | copy-start | bytes 100
  67.0 5.7 %copy-start.22 = (bf16[2,8]{1,0:T(2,128)(2,1)S(1)}, bf16[2,8]{1,0:T(2,128)(2,1)}, u32[]{:S(2)}) copy-start(bf16[2,8]{1,0:T(2,128)(2,1)} %param.31) | copy-start | bytes 100
  67.0 7.1 %copy-start.21 = (bf16[2,512]{1,0:T(2,128)(2,1)S(1)}, bf16[2,512]{1,0:T(2,128)(2,1)}, u32[]{:S(2)}) copy-start(bf16[2,512]{1,0:T(2,128)(2,1)} %param.28) | copy-start | bytes 6148
  67.0 7.9 %copy-start.17 = (f32[2,8,64,128]{3,2,1,0:T(8,128)S(1)}, f32[2,8,64,128]{3,2,1,0:T(8,128)}, u32[]{:S(2)}) copy-start(f32[2,8,64,128]{3,2,1,0:T(8,128)} %param.32) | copy-start | bytes 1572868
  67.0 30.4 %all-to-all-start.2 = ((bf16[64,8,768]{2,1,0:T(8,128)(2,1)}), bf16[64,8,768]{2,1,0:T(8,128)(2,1)S(1)}, u32[]{:S(2)}, u32[]{:S(2)}) async-start(bf16[64,8,768]{2,1,0:T(8,128)(2,1)} %combine.1), calls=%async_computation.2 | async-start | bytes 1572864 | tf_op jit(solution)/shard_map/combine/all_to_all | solution.py:367
  72.8 0.7 copy-start.20
  73.4 0.7 copy-start.23
  74.1 0.7 copy-start.10
  75.2 3.5 %copy-start.16 = (f32[2,8,64,128]{3,2,1,0:T(8,128)}, f32[2,8,64,128]{3,2,1,0:T(8,128)S(1)}, u32[]{:S(2)}) copy-start(f32[2,8,64,128]{3,2,1,0:T(8,128)S(1)} %multiply_add_fusion) | copy-start | bytes 1572868
  75.9 0.7 copy-start.13
  78.7 0.9 copy-start.4
  79.6 0.9 copy-start.6
  80.5 0.9 copy-start.8
  81.3 0.9 copy-start.15

commit v6 on v5

--- a/solution.py
+++ b/solution.py
@@ -167,7 +167,7 @@
     return (row == column // (width // heads)).astype(bf16)
 
 
-def local_state(meta_ref, tok_ref, send_ref, out_ref):
+def local_state(meta_ref, tok_ref, send_ref, out_ref, made, sems):
     del send_ref
     length = tok_ref.shape[0]
     width = out_ref.shape[0]
@@ -188,7 +188,12 @@
     b_parts = jnp.concatenate(
         [jnp.where(seg_index == j, b_half, 0.0).astype(bf16) for j in range(REQS)], axis=1
     )
-    out_ref[:, 0 : REQS * STATE] = dot_tn(scaled, b_parts).astype(bf16)
+    made[:, 0 : REQS * STATE] = dot_tn(scaled, b_parts).astype(bf16)
+    start, middle = SLOTS * STATE, (SLOTS + REQS) * STATE
+    early = pltpu.make_async_copy(
+        made.at[:, 0 : REQS * STATE], out_ref.at[:, start:middle], sems.at[0]
+    )
+    early.start()
     member = (seg_index == lane % REQS).astype(f32).astype(bf16)
     total = None
     for piece in split(log_decay, 3):
@@ -205,23 +210,26 @@
     row_s = lax.broadcasted_iota(jnp.int32, (width, STATE), 0)
     lane_s = lax.broadcasted_iota(jnp.int32, (width, STATE), 1)
     chosen = jnp.where(lane_s == row_s % ROWS, spread, 0.0).astype(bf16)
-    out_ref[:, REQS * STATE :] = dot(chosen, jnp.ones((STATE, STATE), bf16)).astype(bf16)
+    made[:, REQS * STATE :] = dot(chosen, jnp.ones((STATE, STATE), bf16)).astype(bf16)
+    last = pltpu.make_async_copy(made.at[:, REQS * STATE :], out_ref.at[:, middle:], sems.at[1])
+    last.start()
+    early.wait()
+    last.wait()
 
 
 def combine(hit_ref, place_ref, recv_ref, *refs):
-    out_ref, held = refs[-2:]
+    out_ref = refs[-1]
+    first = SLOTS * STATE
     for s in range(recv_ref.shape[0]):
-        block = recv_ref[s, :, 0 : SLOTS * STATE].astype(f32)
-        for k in range(SLOTS):
-            held[s * SLOTS + k] = block[:, k * STATE : (k + 1) * STATE]
-    for s in range(recv_ref.shape[0]):
-        block = recv_ref[s, :, SLOTS * STATE :].astype(f32)
-        kept = block[:, REQS * STATE :]
+        kept = recv_ref[s, :, first + REQS * STATE :].astype(f32)
         for j in range(REQS):
-            prefix = held[hit_ref[s * REQS + j]]
-            out_ref[s, :, j * STATE : (j + 1) * STATE] = prefix.astype(bf16)
+            hit = hit_ref[s * REQS + j]
+            start = pl.multiple_of((hit & (SLOTS - 1)) * STATE, STATE)
+            prefix = recv_ref[hit >> 2, :, pl.ds(start, STATE)]
+            out_ref[s, :, j * STATE : (j + 1) * STATE] = prefix
             factor = kept[j : j + 1, :] + kept[REQS + j : REQS + j + 1, :]
-            new = factor * prefix + block[:, j * STATE : (j + 1) * STATE]
+            own = recv_ref[s, :, first + j * STATE : first + (j + 1) * STATE].astype(f32)
+            new = factor * prefix.astype(f32) + own
             place = place_ref[s * REQS + j]
             start = pl.multiple_of((REQS + (place & 3)) * STATE, STATE)
             out_ref[place >> 2, :, pl.ds(start, STATE)] = new.astype(bf16)
@@ -414,9 +422,12 @@
         send = pl.pallas_call(
             local_state,
             out_shape=shape((width, tiles * STATE), bf16),
-            grid=(1,),
-            in_specs=[VMEM, VMEM, ANY],
-            out_specs=pl.BlockSpec((width, SLOTS * STATE), lambda i: (0, 1)),
+            in_specs=[VMEM, VMEM, HBM],
+            out_specs=HBM,
+            scratch_shapes=[
+                pltpu.VMEM((width, (REQS + 1) * STATE), bf16),
+                pltpu.SemaphoreType.DMA((2,)),
+            ],
             input_output_aliases={2: 0},
             compiler_params=params(),
             cost_estimate=cost(300_000_000, 800_000),
@@ -438,7 +449,6 @@
             out_shape=shape((n_serve, ROWS, 2 * REQS * STATE), bf16),
             in_specs=[SMEM, SMEM, VMEM] + [ANY] * (chips - 1),
             out_specs=VMEM,
-            scratch_shapes=[pltpu.VMEM((n_serve * SLOTS, ROWS, STATE), f32)],
             compiler_params=params(),
             cost_estimate=cost(0, 4_000_000),
         )(prefix_hits, place, pieces, *gates[1:])

time: 99.5 us -> 99.6 us (level)
  no operation moved by 1% of the time
where the time goes in v6:
time: 99.6 us; the launch traced here: 98.9 us
  starting transfers between devices  38.9 us (39%)
  waiting for transfers between devices  38.3 us (38%)
  Pallas kernels  10.4 us (10%)
  local copies, waits for them, and re-layouts  7.7 us (8%)
  between operations  1.53 us (2%)
  other arithmetic  1.38 us (1%)
    all_to_all x3, waiting for transfers between devices, swap(): return lax.all_to_all(value, axis, split_axis=0, concat_axis=0, tiled=True)  33.6 us
    all_to_all x3, starting transfers between devices, swap(): return lax.all_to_all(value, axis, split_axis=0, concat_axis=0, tiled=True)  26.6 us
    ppermute x3, starting transfers between devices, exchange(): lax.ppermute(pairs[k], 'head', [(i, i ^ 2 * k) for i in range(n_head)])  10.4 us
    unnamed x48, local copies, waits for them, and re-layouts  6.8 us
    ppermute x3, waiting for transfers between devices, exchange(): lax.ppermute(pairs[k], 'head', [(i, i ^ 2 * k) for i in range(n_head)])  3.51 us
    pallas_call x1, Pallas kernels, local(): pl.pallas_call(combine, out_shape=shape((n_serve, ROWS, 2 * REQS * STATE)...  2.4 us
  transfers between devices with their start and end apart: 7, of which 5 were waited for; matrix products, arithmetic and copies ran while one was open for 3% of the time, Pallas kernels for 3%

profile of v6, /device:TPU:16, one launch (start us, length us, event | category | flops | bytes accessed | tf_op | source)
XLA Modules:
  0.0 98.9 jit_solution(11120494477335906049)
XLA Ops:
  0.6 0.0 copy-start
  0.6 0.0 copy-start.1
  0.7 1.9 %tokens.1 = (bf16[8,32,768]{2,1,0:T(8,128)(2,1)}, f32[8,128]{1,0:T(8,128)}) custom-call(bf16[32,4096]{1,0:T(8,128)(2,1)} %x_ref.1, bf16[32,1024]{1,0:T(8,128)(2,1)} %b_ref.1, bf16[32,64]{1,0:T(8,128)(2,1)} %dt_ref.1, f32[1,8]{1,0:T(1,128)} %bitcast.23, s32[1,3]{1,0:T(1,128)} %len_ref.1), custom_call_target="tpu_custom_call" | custom-call | bytes 800000 | tf_op jit(solution)/shard_map/tokens/pallas_call | solution.py:379
  2.6 4.3 %all-to-all-start = ((bf16[8,32,768]{2,1,0:T(8,128)(2,1)}), bf16[8,32,768]{2,1,0:T(8,128)(2,1)S(1)}, u32[]{:S(2)}, u32[]{:S(2)}) async-start(bf16[8,32,768]{2,1,0:T(8,128)(2,1)} %get-tuple-element.18), calls=%async_computation | async-start | bytes 786432 | tf_op jit(solution)/shard_map/tokens/all_to_all | solution.py:375
  6.9 0.0 copy-done.1
  6.9 0.0 copy-start.11
  6.9 0.9 cache.1.send_ref
  7.8 8.1 %all-to-all-done = bf16[8,32,768]{2,1,0:T(8,128)(2,1)S(1)} async-done(((bf16[8,32,768]{2,1,0:T(8,128)(2,1)}), bf16[8,32,768]{2,1,0:T(8,128)(2,1)S(1)}, u32[]{:S(2)}, u32[]{:S(2)}) %all-to-all-start) | async-done | bytes 393248 | tf_op jit(solution)/shard_map/tokens/all_to_all | solution.py:375
  15.8 0.0 copy-done.11
  15.8 2.0 %local.1.after_ref = bf16[512,1024]{1,0:T(8,128)(2,1)} custom-call(f32[8,128]{1,0:T(8,128)S(1)} %copy-done.11, bf16[256,768]{1,0:T(8,128)(2,1)S(1)} %bitcast.18, bf16[512,1024]{1,0:T(8,128)(2,1)} %cache.1.send_ref), custom_call_target="tpu_custom_call", output_to_operand_aliasing={{}: (2, {})} | custom-call | flops 300000000 | bytes 800000 | tf_op jit(solution)/shard_map/local/pallas_call | solution.py:422
  17.8 0.0 copy-start.2
  17.8 0.0 copy-start.9
  17.8 16.6 %all-to-all-start.1 = ((bf16[64,8,1024]{2,1,0:T(8,128)(2,1)}), bf16[64,8,1024]{2,1,0:T(8,128)(2,1)S(1)}, u32[]{:S(2)}, u32[]{:S(2)}) async-start(bf16[64,8,1024]{2,1,0:T(8,128)(2,1)} %bitcast.7), calls=%async_computation.1 | async-start | bytes 2097152 | tf_op jit(solution)/shard_map/local/all_to_all | solution.py:375
  34.5 0.0 copy-done.2
  34.5 0.0 copy-done.9
  34.5 0.0 copy-start.18
  34.5 1.9 %collective-permute-start = (bf16[4,32,640]{2,1,0:T(8,128)(2,1)S(1)}, bf16[4,32,640]{2,1,0:T(8,128)(2,1)S(1)}, u32[]{:S(2)}, u32[]{:S(2)}) collective-permute-start(bf16[4,32,640]{2,1,0:T(8,128)(2,1)S(1)} %get-tuple-element.20), channel_id=1, source_target_pairs={{0,1},{1,0},{2,3},{3,2},{4,5},{5,4},{6,7},{7,6},{8,9},{9,8},{10,11... | collective-permute-start | bytes 491528 | tf_op jit(solution)/shard_map/gates/ppermute | solution.py:120
  36.5 0.0 copy-done.18
  36.5 0.2 convert_reduce_fusion
  36.7 1.2 %collective-permute-done.got_ref = bf16[4,32,640]{2,1,0:T(8,128)(2,1)S(1)} collective-permute-done((bf16[4,32,640]{2,1,0:T(8,128)(2,1)S(1)}, bf16[4,32,640]{2,1,0:T(8,128)(2,1)S(1)}, u32[]{:S(2)}, u32[]{:S(2)}) %collective-permute-start) | collective-permute-done | bytes 163872 | tf_op jit(solution)/shard_map/gates/ppermute | solution.py:120
  37.9 0.0 copy-start.14
  37.9 0.6 copy-done.14
  38.5 2.5 %collective-permute-start.1 = (bf16[2,32,640]{2,1,0:T(8,128)(2,1)S(1)}, bf16[2,32,640]{2,1,0:T(8,128)(2,1)S(1)}, u32[]{:S(2)}, u32[]{:S(2)}) collective-permute-start(bf16[2,32,640]{2,1,0:T(8,128)(2,1)S(1)} %get-tuple-element.22), channel_id=1, source_target_pairs={{0,2},{1,3},{2,0},{3,1},{4,6},{5,7},{6,4},{7,5},{8,10},{9,11},{10,... | collective-permute-start | bytes 245768 | tf_op jit(solution)/shard_map/gates/ppermute | solution.py:130
  41.0 4.0 %collective-permute-start.2 = (bf16[2,32,640]{2,1,0:T(8,128)(2,1)S(1)}, bf16[2,32,640]{2,1,0:T(8,128)(2,1)S(1)}, u32[]{:S(2)}, u32[]{:S(2)}) collective-permute-start(bf16[2,32,640]{2,1,0:T(8,128)(2,1)S(1)} %get-tuple-element.23), channel_id=1, source_target_pairs={{0,4},{1,5},{2,6},{3,7},{4,0},{5,1},{6,2},{7,3},{8,12},{9,13},{10,... | collective-permute-start | bytes 245768 | tf_op jit(solution)/shard_map/gates/ppermute | solution.py:130
  45.0 0.0 copy-start.12
  45.0 4.0 %collective-permute-start.3 = (bf16[2,32,640]{2,1,0:T(8,128)(2,1)S(1)}, bf16[2,32,640]{2,1,0:T(8,128)(2,1)S(1)}, u32[]{:S(2)}, u32[]{:S(2)}) collective-permute-start(bf16[2,32,640]{2,1,0:T(8,128)(2,1)S(1)} %get-tuple-element.24), channel_id=1, source_target_pairs={{0,6},{1,7},{2,4},{3,5},{4,2},{5,3},{6,0},{7,1},{8,14},{9,15},{10,... | collective-permute-start | bytes 245768 | tf_op jit(solution)/shard_map/gates/ppermute | solution.py:130
  49.0 0.0 collective-permute-done.1.refs_1_.refs_0_
  49.0 0.0 copy-start.3
  49.0 0.0 collective-permute-done.2.refs_2_.refs_1_
  49.0 0.0 copy-start.5
  49.0 3.5 %collective-permute-done.3.refs_3_.refs_2_ = bf16[2,32,640]{2,1,0:T(8,128)(2,1)S(1)} collective-permute-done((bf16[2,32,640]{2,1,0:T(8,128)(2,1)S(1)}, bf16[2,32,640]{2,1,0:T(8,128)(2,1)S(1)}, u32[]{:S(2)}, u32[]{:S(2)}) %collective-permute-start.3) | collective-permute-done | bytes 81952 | tf_op jit(solution)/shard_map/gates/ppermute | solution.py:130
  52.5 12.2 %all-to-all-done.1.recv_ref = bf16[64,8,1024]{2,1,0:T(8,128)(2,1)S(1)} async-done(((bf16[64,8,1024]{2,1,0:T(8,128)(2,1)}), bf16[64,8,1024]{2,1,0:T(8,128)(2,1)S(1)}, u32[]{:S(2)}, u32[]{:S(2)}) %all-to-all-start.1) | async-done | bytes 1048608 | tf_op jit(solution)/shard_map/local/all_to_all | solution.py:375
  64.8 2.4 %combine.1 = bf16[64,8,768]{2,1,0:T(8,128)(2,1)} custom-call(s32[192]{0:T(256)S(1)} %copy-done.12, s32[192]{0:T(256)S(1)} %fusion.4.place_ref, bf16[64,8,1024]{2,1,0:T(8,128)(2,1)S(1)} %all-to-all-done.1.recv_ref, bf16[2,32,640]{2,1,0:T(8,128)(2,1)S(1)} %collective-permute-done.1.refs_1_.refs_0_, ...), custom_call_target="tpu_custom_call" | custom-call | bytes 4000000 | tf_op jit(solution)/shard_map/combine/pallas_call | solution.py:447
  67.2 0.0 copy-start.19
  67.2 0.0 copy-start.22
  67.2 0.0 copy-start.21
  67.2 0.0 copy-start.17
  67.2 5.7 %all-to-all-start.2 = ((bf16[64,8,768]{2,1,0:T(8,128)(2,1)}), bf16[64,8,768]{2,1,0:T(8,128)(2,1)S(1)}, u32[]{:S(2)}, u32[]{:S(2)}) async-start(bf16[64,8,768]{2,1,0:T(8,128)(2,1)} %combine.1), calls=%async_computation.2 | async-start | bytes 1572864 | tf_op jit(solution)/shard_map/combine/all_to_all | solution.py:375
  72.9 0.0 copy-done.19
  72.9 0.0 copy-done.22
  72.9 0.0 copy-start.20
  72.9 0.7 copy-done.20
  73.6 0.1 reshape.137
  73.7 0.6 copy-done.23
  74.3 0.0 copy-done.21
  74.3 0.1 reshape.139
  74.4 0.6 copy-done.10
  75.0 0.1 mul.108
  75.0 0.1 broadcast_multiply_fusion
  75.1 0.2 multiply_add_fusion
  75.4 0.0 copy-start.16
  75.4 0.7 fusion.5
  76.1 0.7 copy-done.13
  76.8 0.2 multiply_reduce_fusion
  76.9 0.1 multiply_convert_fusion
  77.0 0.7 convert_element_type.22
  77.7 0.6 fusion.7
  78.9 0.9 copy-done.4
  79.7 0.9 copy-done.6
  80.6 0.9 copy-done.8
  81.5 0.9 copy-done.15
  82.4 1.9 %inner.1 = (f32[256,512]{1,0:T(8,128)S(1)}, f32[256,512]{1,0:T(8,128)S(1)}, bf16[256,384]{1,0:T(8,128)(2,1)S(1)}) custom-call(s32[1]{0:T(128)} %bitcast.3.me_ref, f32[8,128]{1,0:T(8,128)S(1)} %copy-done.11, f32[1,8]{1,0:T(1,128)S(1)} %bitcast.21, bf16[256,768]{1,0:T(8,128)(2,1)S(1)} %bitcast.19, bf16[2,32,640]{2,1,0:T(8,128)(2,1)S(1)} %copy-done.15, ...), custom_call_target="tpu_custom_call" | custom-call | flops 400000000 | bytes 1500000 | tf_op jit(solution)/shard_map/inner/pallas_call | solution.py:457
  84.3 13.3 %all-to-all-done.2 = bf16[64,8,768]{2,1,0:T(8,128)(2,1)S(1)} async-done(((bf16[64,8,768]{2,1,0:T(8,128)(2,1)}), bf16[64,8,768]{2,1,0:T(8,128)(2,1)S(1)}, u32[]{:S(2)}, u32[]{:S(2)}) %all-to-all-start.2) | async-done | bytes 786464 | tf_op jit(solution)/shard_map/combine/all_to_all | solution.py:375
  97.6 1.3 %outputs.1 = (bf16[256,512]{1,0:T(8,128)(2,1)}, f32[4,512,128]{2,1,0:T(8,128)}) custom-call(s32[1]{0:T(128)} %bitcast.missing_ref, f32[4,512,128]{2,1,0:T(8,128)S(1)} %bitcast.16, f32[1,512]{1,0:T(1,128)S(1)} %bitcast.20, f32[256,512]{1,0:T(8,128)S(1)} %get-tuple-element.25.base_ref, f32[256,512]{1,0:T(8,128)S(1)} %get-tuple-element.26.factor_ref, ...), custom_call_target="tpu_custom_call" | custom-call | flops 200000000 | bytes 4000000 | tf_op jit(solution)/shard_map/outputs/pallas_call | solution.py:477
  (21 shorter events, 0.1 us)
Async XLA Ops:
  0.6 74.7 %copy-start = (bf16[2,128]{1,0:T(2,128)(2,1)S(1)}, bf16[2,128]{1,0:T(2,128)(2,1)}, u32[]{:S(2)}) copy-start(bf16[2,128]{1,0:T(2,128)(2,1)} %param.30) | copy-start | bytes 1540
  0.6 6.3 %copy-start.1 = (f32[4,8,64,128]{3,2,1,0:T(8,128)S(1)}, f32[4,8,64,128]{3,2,1,0:T(8,128)}, u32[]{:S(2)}) copy-start(f32[4,8,64,128]{3,2,1,0:T(8,128)} %param.26) | copy-start | bytes 3145732
  2.6 13.3 %all-to-all-start = ((bf16[8,32,768]{2,1,0:T(8,128)(2,1)}), bf16[8,32,768]{2,1,0:T(8,128)(2,1)S(1)}, u32[]{:S(2)}, u32[]{:S(2)}) async-start(bf16[8,32,768]{2,1,0:T(8,128)(2,1)} %get-tuple-element.18), calls=%async_computation | async-start | bytes 786432 | tf_op jit(solution)/shard_map/tokens/all_to_all | solution.py:375
  6.9 8.9 %copy-start.11 = (f32[8,128]{1,0:T(8,128)S(1)}, f32[8,128]{1,0:T(8,128)}, u32[]{:S(2)}) copy-start(f32[8,128]{1,0:T(8,128)} %get-tuple-element.17.meta_ref) | copy-start | bytes 12292
  17.8 16.7 %copy-start.2 = (bf16[32,4096]{1,0:T(8,128)(2,1)S(1)}, bf16[32,4096]{1,0:T(8,128)(2,1)}, u32[]{:S(2)}) copy-start(bf16[32,4096]{1,0:T(8,128)(2,1)} %z_ref.1) | copy-start | bytes 786436
  17.8 16.7 %copy-start.9 = (bf16[32,1024]{1,0:T(8,128)(2,1)S(1)}, bf16[32,1024]{1,0:T(8,128)(2,1)}, u32[]{:S(2)}) copy-start(bf16[32,1024]{1,0:T(8,128)(2,1)} %c_ref.1) | copy-start | bytes 196612
  17.8 46.9 %all-to-all-start.1 = ((bf16[64,8,1024]{2,1,0:T(8,128)(2,1)}), bf16[64,8,1024]{2,1,0:T(8,128)(2,1)S(1)}, u32[]{:S(2)}, u32[]{:S(2)}) async-start(bf16[64,8,1024]{2,1,0:T(8,128)(2,1)} %bitcast.7), calls=%async_computation.1 | async-start | bytes 2097152 | tf_op jit(solution)/shard_map/local/all_to_all | solution.py:375
  34.5 1.9 %copy-start.18 = (s32[192]{0:T(256)S(1)}, s32[192]{0:T(256)}, u32[]{:S(2)}) copy-start(s32[192]{0:T(256)} %param.25) | copy-start | bytes 2308
  34.5 3.3 %collective-permute-start = (bf16[4,32,640]{2,1,0:T(8,128)(2,1)S(1)}, bf16[4,32,640]{2,1,0:T(8,128)(2,1)S(1)}, u32[]{:S(2)}, u32[]{:S(2)}) collective-permute-start(bf16[4,32,640]{2,1,0:T(8,128)(2,1)S(1)} %get-tuple-element.20), channel_id=1, source_target_pairs={{0,1},{1,0},{2,3},{3,2},{4,5},{5,4},{6,7},{7,6},{8,9},{9,8},{10,11... | collective-permute-start | bytes 491528 | tf_op jit(solution)/shard_map/gates/ppermute | solution.py:120
  37.9 0.6 copy-start.14
  38.5 10.5 %collective-permute-start.1 = (bf16[2,32,640]{2,1,0:T(8,128)(2,1)S(1)}, bf16[2,32,640]{2,1,0:T(8,128)(2,1)S(1)}, u32[]{:S(2)}, u32[]{:S(2)}) collective-permute-start(bf16[2,32,640]{2,1,0:T(8,128)(2,1)S(1)} %get-tuple-element.22), channel_id=1, source_target_pairs={{0,2},{1,3},{2,0},{3,1},{4,6},{5,7},{6,4},{7,5},{8,10},{9,11},{10,... | collective-permute-start | bytes 245768 | tf_op jit(solution)/shard_map/gates/ppermute | solution.py:130
  41.0 8.0 %collective-permute-start.2 = (bf16[2,32,640]{2,1,0:T(8,128)(2,1)S(1)}, bf16[2,32,640]{2,1,0:T(8,128)(2,1)S(1)}, u32[]{:S(2)}, u32[]{:S(2)}) collective-permute-start(bf16[2,32,640]{2,1,0:T(8,128)(2,1)S(1)} %get-tuple-element.23), channel_id=1, source_target_pairs={{0,4},{1,5},{2,6},{3,7},{4,0},{5,1},{6,2},{7,3},{8,12},{9,13},{10,... | collective-permute-start | bytes 245768 | tf_op jit(solution)/shard_map/gates/ppermute | solution.py:130
  45.0 19.8 %copy-start.12 = (s32[192]{0:T(256)S(1)}, s32[192]{0:T(256)}, u32[]{:S(2)}) copy-start(s32[192]{0:T(256)} %hit_ref.1) | copy-start | bytes 2308
  45.0 7.5 %collective-permute-start.3 = (bf16[2,32,640]{2,1,0:T(8,128)(2,1)S(1)}, bf16[2,32,640]{2,1,0:T(8,128)(2,1)S(1)}, u32[]{:S(2)}, u32[]{:S(2)}) collective-permute-start(bf16[2,32,640]{2,1,0:T(8,128)(2,1)S(1)} %get-tuple-element.24), channel_id=1, source_target_pairs={{0,6},{1,7},{2,4},{3,5},{4,2},{5,3},{6,0},{7,1},{8,14},{9,15},{10,... | collective-permute-start | bytes 245768 | tf_op jit(solution)/shard_map/gates/ppermute | solution.py:130
  49.0 18.2 %copy-start.3 = (bf16[2,32,640]{2,1,0:T(8,128)(2,1)}, bf16[2,32,640]{2,1,0:T(8,128)(2,1)S(1)}, u32[]{:S(2)}) copy-start(bf16[2,32,640]{2,1,0:T(8,128)(2,1)S(1)} %collective-permute-done.1.refs_1_.refs_0_) | copy-start | bytes 245764
  49.0 18.2 %copy-start.5 = (bf16[2,32,640]{2,1,0:T(8,128)(2,1)}, bf16[2,32,640]{2,1,0:T(8,128)(2,1)S(1)}, u32[]{:S(2)}) copy-start(bf16[2,32,640]{2,1,0:T(8,128)(2,1)S(1)} %collective-permute-done.2.refs_2_.refs_1_) | copy-start | bytes 245764
  52.5 14.7 %copy-start.7 = (bf16[2,32,640]{2,1,0:T(8,128)(2,1)}, bf16[2,32,640]{2,1,0:T(8,128)(2,1)S(1)}, u32[]{:S(2)}) copy-start(bf16[2,32,640]{2,1,0:T(8,128)(2,1)S(1)} %collective-permute-done.3.refs_3_.refs_2_) | copy-start | bytes 245764
  67.2 5.7 %copy-start.19 = (f32[8]{0:T(128)S(1)}, f32[8]{0:T(128)}, u32[]{:S(2)}) copy-start(f32[8]{0:T(128)} %param.33) | copy-start | bytes 100
  67.2 5.7 %copy-start.22 = (bf16[2,8]{1,0:T(2,128)(2,1)S(1)}, bf16[2,8]{1,0:T(2,128)(2,1)}, u32[]{:S(2)}) copy-start(bf16[2,8]{1,0:T(2,128)(2,1)} %param.31) | copy-start | bytes 100
  67.2 7.1 %copy-start.21 = (bf16[2,512]{1,0:T(2,128)(2,1)S(1)}, bf16[2,512]{1,0:T(2,128)(2,1)}, u32[]{:S(2)}) copy-start(bf16[2,512]{1,0:T(2,128)(2,1)} %param.28) | copy-start | bytes 6148
  67.2 7.9 %copy-start.17 = (f32[2,8,64,128]{3,2,1,0:T(8,128)S(1)}, f32[2,8,64,128]{3,2,1,0:T(8,128)}, u32[]{:S(2)}) copy-start(f32[2,8,64,128]{3,2,1,0:T(8,128)} %param.32) | copy-start | bytes 1572868
  67.2 30.4 %all-to-all-start.2 = ((bf16[64,8,768]{2,1,0:T(8,128)(2,1)}), bf16[64,8,768]{2,1,0:T(8,128)(2,1)S(1)}, u32[]{:S(2)}, u32[]{:S(2)}) async-start(bf16[64,8,768]{2,1,0:T(8,128)(2,1)} %combine.1), calls=%async_computation.2 | async-start | bytes 1572864 | tf_op jit(solution)/shard_map/combine/all_to_all | solution.py:375
  72.9 0.7 copy-start.20
  73.6 0.7 copy-start.23
  74.3 0.7 copy-start.10
  75.4 3.5 %copy-start.16 = (f32[2,8,64,128]{3,2,1,0:T(8,128)}, f32[2,8,64,128]{3,2,1,0:T(8,128)S(1)}, u32[]{:S(2)}) copy-start(f32[2,8,64,128]{3,2,1,0:T(8,128)S(1)} %multiply_add_fusion) | copy-start | bytes 1572868
  76.1 0.7 copy-start.13
  78.9 0.9 copy-start.4
  79.7 0.9 copy-start.6
  80.6 0.9 copy-start.8
  81.5 0.9 copy-start.15

commit v7 on v6

--- a/solution.py
+++ b/solution.py
@@ -67,7 +67,8 @@
 
 
 def pack_first(
-    x_ref, b_ref, dt_ref, rate_ref, len_ref, out_ref, meta_ref, xs, bs, steps, rates, lens, sems
+    x_ref, b_ref, dt_ref, rate_ref, len_ref, out_ref, meta_ref,
+    xs, bs, steps, rates, lens, made, sems, out_sems,
 ):
     count = out_ref.shape[0]
     heads_dev = dt_ref.shape[1] // count
@@ -75,24 +76,34 @@
     copies = [
         pltpu.make_async_copy(src, dst, sems.at[i])
         for i, (src, dst) in enumerate(
-            ((x_ref, xs), (b_ref, bs), (dt_ref, steps), (rate_ref, rates), (len_ref, lens))
+            ((dt_ref, steps), (b_ref, bs), (x_ref, xs), (rate_ref, rates), (len_ref, lens))
         )
     ]
     for copy in copies:
         copy.start()
-    for copy in copies:
-        copy.wait()
+    copies[0].wait()
     raw = steps[...].astype(f32)
     raw = jnp.concatenate([raw, jnp.zeros((raw.shape[0], STATE - raw.shape[1]), f32)], axis=1)
     for d in range(count):
-        out_ref[d, :, 0:width] = xs[:, d * width : (d + 1) * width]
-        out_ref[d, :, width : width + STATE] = bs[:, d * STATE : (d + 1) * STATE]
         mine = raw if d == 0 else pltpu.roll(raw, STATE - d * heads_dev, 1)
-        out_ref[d, :, width + STATE : width + 2 * STATE] = mine.astype(bf16)
+        made[d, :, width + STATE : width + 2 * STATE] = mine.astype(bf16)
+    copies[1].wait()
+    for d in range(count):
+        made[d, :, width : width + STATE] = bs[:, d * STATE : (d + 1) * STATE]
+    copies[2].wait()
+    leaving = []
+    for d in range(count):
+        made[d, :, 0:width] = xs[:, d * width : (d + 1) * width]
+        leaving.append(pltpu.make_async_copy(made.at[d], out_ref.at[d], out_sems.at[d]))
+        leaving[-1].start()
+    copies[3].wait()
+    copies[4].wait()
     meta_ref[...] = jnp.zeros_like(meta_ref)
     meta_ref[0:1, 0 : rates.shape[1]] = rates[...]
     meta_ref[1:2, 0:1] = lens[:, 0:1].astype(f32)
     meta_ref[2:3, 0:1] = (lens[:, 0:1] + lens[:, 1:2]).astype(f32)
+    for copy in leaving:
+        copy.wait()
 
 
 def pack_gates(me_ref, after_ref, z_ref, c_ref, keep_ref, give_ref):
@@ -218,21 +229,32 @@
 
 
 def combine(hit_ref, place_ref, recv_ref, *refs):
-    out_ref = refs[-1]
-    first = SLOTS * STATE
+    out_ref, held, picked, made, sems = refs[-5:]
+    first, half = SLOTS * STATE, REQS * STATE
     for s in range(recv_ref.shape[0]):
-        kept = recv_ref[s, :, first + REQS * STATE :].astype(f32)
+        block = recv_ref[s, :, 0:first].astype(f32)
+        for k in range(SLOTS):
+            held[s * SLOTS + k] = block[:, k * STATE : (k + 1) * STATE]
+    for s in range(recv_ref.shape[0]):
         for j in range(REQS):
-            hit = hit_ref[s * REQS + j]
-            start = pl.multiple_of((hit & (SLOTS - 1)) * STATE, STATE)
-            prefix = recv_ref[hit >> 2, :, pl.ds(start, STATE)]
-            out_ref[s, :, j * STATE : (j + 1) * STATE] = prefix
+            picked[s, :, j * STATE : (j + 1) * STATE] = held[hit_ref[s * REQS + j]].astype(bf16)
+    early = pltpu.make_async_copy(picked, out_ref.at[:, :, 0:half], sems.at[0])
+    early.start()
+    for s in range(recv_ref.shape[0]):
+        block = recv_ref[s, :, first:].astype(f32)
+        prefix = picked[s].astype(f32)
+        kept = block[:, half:]
+        for j in range(REQS):
+            columns = slice(j * STATE, (j + 1) * STATE)
             factor = kept[j : j + 1, :] + kept[REQS + j : REQS + j + 1, :]
-            own = recv_ref[s, :, first + j * STATE : first + (j + 1) * STATE].astype(f32)
-            new = factor * prefix.astype(f32) + own
+            new = factor * prefix[:, columns] + block[:, columns]
             place = place_ref[s * REQS + j]
-            start = pl.multiple_of((REQS + (place & 3)) * STATE, STATE)
-            out_ref[place >> 2, :, pl.ds(start, STATE)] = new.astype(bf16)
+            start = pl.multiple_of((place & 3) * STATE, STATE)
+            made[place >> 2, :, pl.ds(start, STATE)] = new.astype(bf16)
+    last = pltpu.make_async_copy(made, out_ref.at[:, :, half:], sems.at[1])
+    last.start()
+    early.wait()
+    last.wait()
 
 
 def token_inner(me_ref, meta_ref, skip_ref, tok_ref, *refs):
@@ -383,14 +405,16 @@
                 shape((8, STATE), f32),
             ),
             in_specs=[HBM] * 5,
-            out_specs=(VMEM, VMEM),
+            out_specs=(HBM, VMEM),
             scratch_shapes=[
                 pltpu.VMEM(pre_x.shape, bf16),
                 pltpu.VMEM(pre_b.shape, bf16),
                 pltpu.VMEM(pre_dt.shape, bf16),
                 pltpu.VMEM((1, heads), f32),
                 pltpu.VMEM(suffix_lengths.shape, jnp.int32),
+                pltpu.VMEM((n_head, rows, width + 2 * STATE), bf16),
                 pltpu.SemaphoreType.DMA((5,)),
+                pltpu.SemaphoreType.DMA((n_head,)),
             ],
             compiler_params=params(56),
             cost_estimate=cost(0, 800_000),
@@ -448,7 +472,13 @@
             combine,
             out_shape=shape((n_serve, ROWS, 2 * REQS * STATE), bf16),
             in_specs=[SMEM, SMEM, VMEM] + [ANY] * (chips - 1),
-            out_specs=VMEM,
+            out_specs=HBM,
+            scratch_shapes=[
+                pltpu.VMEM((n_serve * SLOTS, ROWS, STATE), f32),
+                pltpu.VMEM((n_serve, ROWS, REQS * STATE), bf16),
+                pltpu.VMEM((n_serve, ROWS, REQS * STATE), bf16),
+                pltpu.SemaphoreType.DMA((2,)),
+            ],
             compiler_params=params(),
             cost_estimate=cost(0, 4_000_000),
         )(prefix_hits, place, pieces, *gates[1:])

time: 99.6 us -> 99.9 us (level)
  no operation moved by 1% of the time
where the time goes in v7:
time: 99.9 us; the launch traced here: 99.1 us
  starting transfers between devices  38.9 us (39%)
  waiting for transfers between devices  38.3 us (38%)
  Pallas kernels  10.6 us (11%)
  local copies, waits for them, and re-layouts  7.7 us (8%)
  between operations  1.55 us (2%)
  other arithmetic  1.38 us (1%)
    all_to_all x3, waiting for transfers between devices, swap(): return lax.all_to_all(value, axis, split_axis=0, concat_axis=0, tiled=True)  33.6 us
    all_to_all x3, starting transfers between devices, swap(): return lax.all_to_all(value, axis, split_axis=0, concat_axis=0, tiled=True)  26.6 us
    ppermute x3, starting transfers between devices, exchange(): lax.ppermute(pairs[k], 'head', [(i, i ^ 2 * k) for i in range(n_head)])  10.4 us
    unnamed x48, local copies, waits for them, and re-layouts  6.8 us
    ppermute x3, waiting for transfers between devices, exchange(): lax.ppermute(pairs[k], 'head', [(i, i ^ 2 * k) for i in range(n_head)])  3.5 us
    pallas_call x1, Pallas kernels, local(): pl.pallas_call(pack_first, out_shape=(shape((n_head, rows, width + 2 * ST...  2.53 us
  transfers between devices with their start and end apart: 7, of which 5 were waited for; matrix products, arithmetic and copies ran while one was open for 3% of the time, Pallas kernels for 3%

profile of v7, /device:TPU:16, one launch (start us, length us, event | category | flops | bytes accessed | tf_op | source)
XLA Modules:
  0.0 99.1 jit_solution(7797609814380291140)
XLA Ops:
  0.6 0.0 copy-start
  0.6 0.0 copy-start.1
  0.7 2.5 %tokens.1 = (bf16[8,32,768]{2,1,0:T(8,128)(2,1)}, f32[8,128]{1,0:T(8,128)}) custom-call(bf16[32,4096]{1,0:T(8,128)(2,1)} %x_ref.1, bf16[32,1024]{1,0:T(8,128)(2,1)} %b_ref.1, bf16[32,64]{1,0:T(8,128)(2,1)} %dt_ref.1, f32[1,8]{1,0:T(1,128)} %bitcast.23, s32[1,3]{1,0:T(1,128)} %len_ref.1), custom_call_target="tpu_custom_call" | custom-call | bytes 800000 | tf_op jit(solution)/shard_map/tokens/pallas_call | solution.py:401
  3.2 4.3 %all-to-all-start = ((bf16[8,32,768]{2,1,0:T(8,128)(2,1)}), bf16[8,32,768]{2,1,0:T(8,128)(2,1)S(1)}, u32[]{:S(2)}, u32[]{:S(2)}) async-start(bf16[8,32,768]{2,1,0:T(8,128)(2,1)} %get-tuple-element.18), calls=%async_computation | async-start | bytes 786432 | tf_op jit(solution)/shard_map/tokens/all_to_all | solution.py:397
  7.5 0.0 copy-done.1
  7.5 0.0 copy-start.11
  7.5 0.9 cache.1.send_ref
  8.4 8.1 %all-to-all-done = bf16[8,32,768]{2,1,0:T(8,128)(2,1)S(1)} async-done(((bf16[8,32,768]{2,1,0:T(8,128)(2,1)}), bf16[8,32,768]{2,1,0:T(8,128)(2,1)S(1)}, u32[]{:S(2)}, u32[]{:S(2)}) %all-to-all-start) | async-done | bytes 393248 | tf_op jit(solution)/shard_map/tokens/all_to_all | solution.py:397
  16.4 0.0 copy-done.11
  16.5 2.0 %local.1.after_ref = bf16[512,1024]{1,0:T(8,128)(2,1)} custom-call(f32[8,128]{1,0:T(8,128)S(1)} %copy-done.11, bf16[256,768]{1,0:T(8,128)(2,1)S(1)} %bitcast.18, bf16[512,1024]{1,0:T(8,128)(2,1)} %cache.1.send_ref), custom_call_target="tpu_custom_call", output_to_operand_aliasing={{}: (2, {})} | custom-call | flops 300000000 | bytes 800000 | tf_op jit(solution)/shard_map/local/pallas_call | solution.py:446
  18.4 0.0 copy-start.2
  18.4 0.0 copy-start.9
  18.4 16.6 %all-to-all-start.1 = ((bf16[64,8,1024]{2,1,0:T(8,128)(2,1)}), bf16[64,8,1024]{2,1,0:T(8,128)(2,1)S(1)}, u32[]{:S(2)}, u32[]{:S(2)}) async-start(bf16[64,8,1024]{2,1,0:T(8,128)(2,1)} %bitcast.7), calls=%async_computation.1 | async-start | bytes 2097152 | tf_op jit(solution)/shard_map/local/all_to_all | solution.py:397
  35.1 0.0 copy-done.2
  35.1 0.0 copy-done.9
  35.1 0.0 copy-start.18
  35.2 1.9 %collective-permute-start = (bf16[4,32,640]{2,1,0:T(8,128)(2,1)S(1)}, bf16[4,32,640]{2,1,0:T(8,128)(2,1)S(1)}, u32[]{:S(2)}, u32[]{:S(2)}) collective-permute-start(bf16[4,32,640]{2,1,0:T(8,128)(2,1)S(1)} %get-tuple-element.20), channel_id=1, source_target_pairs={{0,1},{1,0},{2,3},{3,2},{4,5},{5,4},{6,7},{7,6},{8,9},{9,8},{10,11... | collective-permute-start | bytes 491528 | tf_op jit(solution)/shard_map/gates/ppermute | solution.py:131
  37.1 0.0 copy-done.18
  37.1 0.2 convert_reduce_fusion
  37.3 1.2 %collective-permute-done.got_ref = bf16[4,32,640]{2,1,0:T(8,128)(2,1)S(1)} collective-permute-done((bf16[4,32,640]{2,1,0:T(8,128)(2,1)S(1)}, bf16[4,32,640]{2,1,0:T(8,128)(2,1)S(1)}, u32[]{:S(2)}, u32[]{:S(2)}) %collective-permute-start) | collective-permute-done | bytes 163872 | tf_op jit(solution)/shard_map/gates/ppermute | solution.py:131
  38.5 0.0 copy-start.14
  38.5 0.6 copy-done.14
  39.1 2.5 %collective-permute-start.1 = (bf16[2,32,640]{2,1,0:T(8,128)(2,1)S(1)}, bf16[2,32,640]{2,1,0:T(8,128)(2,1)S(1)}, u32[]{:S(2)}, u32[]{:S(2)}) collective-permute-start(bf16[2,32,640]{2,1,0:T(8,128)(2,1)S(1)} %get-tuple-element.22), channel_id=1, source_target_pairs={{0,2},{1,3},{2,0},{3,1},{4,6},{5,7},{6,4},{7,5},{8,10},{9,11},{10,... | collective-permute-start | bytes 245768 | tf_op jit(solution)/shard_map/gates/ppermute | solution.py:141
  41.6 4.0 %collective-permute-start.2 = (bf16[2,32,640]{2,1,0:T(8,128)(2,1)S(1)}, bf16[2,32,640]{2,1,0:T(8,128)(2,1)S(1)}, u32[]{:S(2)}, u32[]{:S(2)}) collective-permute-start(bf16[2,32,640]{2,1,0:T(8,128)(2,1)S(1)} %get-tuple-element.23), channel_id=1, source_target_pairs={{0,4},{1,5},{2,6},{3,7},{4,0},{5,1},{6,2},{7,3},{8,12},{9,13},{10,... | collective-permute-start | bytes 245768 | tf_op jit(solution)/shard_map/gates/ppermute | solution.py:141
  45.6 0.0 copy-start.12
  45.6 4.0 %collective-permute-start.3 = (bf16[2,32,640]{2,1,0:T(8,128)(2,1)S(1)}, bf16[2,32,640]{2,1,0:T(8,128)(2,1)S(1)}, u32[]{:S(2)}, u32[]{:S(2)}) collective-permute-start(bf16[2,32,640]{2,1,0:T(8,128)(2,1)S(1)} %get-tuple-element.24), channel_id=1, source_target_pairs={{0,6},{1,7},{2,4},{3,5},{4,2},{5,3},{6,0},{7,1},{8,14},{9,15},{10,... | collective-permute-start | bytes 245768 | tf_op jit(solution)/shard_map/gates/ppermute | solution.py:141
  49.6 0.0 collective-permute-done.1.refs_1_.refs_0_
  49.6 0.0 copy-start.3
  49.6 0.0 collective-permute-done.2.refs_2_.refs_1_
  49.6 0.0 copy-start.5
  49.6 3.5 %collective-permute-done.3.refs_3_.refs_2_ = bf16[2,32,640]{2,1,0:T(8,128)(2,1)S(1)} collective-permute-done((bf16[2,32,640]{2,1,0:T(8,128)(2,1)S(1)}, bf16[2,32,640]{2,1,0:T(8,128)(2,1)S(1)}, u32[]{:S(2)}, u32[]{:S(2)}) %collective-permute-start.3) | collective-permute-done | bytes 81952 | tf_op jit(solution)/shard_map/gates/ppermute | solution.py:141
  53.1 12.2 %all-to-all-done.1.recv_ref = bf16[64,8,1024]{2,1,0:T(8,128)(2,1)S(1)} async-done(((bf16[64,8,1024]{2,1,0:T(8,128)(2,1)}), bf16[64,8,1024]{2,1,0:T(8,128)(2,1)S(1)}, u32[]{:S(2)}, u32[]{:S(2)}) %all-to-all-start.1) | async-done | bytes 1048608 | tf_op jit(solution)/shard_map/local/all_to_all | solution.py:397
  65.4 2.0 %combine.1 = bf16[64,8,768]{2,1,0:T(8,128)(2,1)} custom-call(s32[192]{0:T(256)S(1)} %copy-done.12, s32[192]{0:T(256)S(1)} %fusion.4.place_ref, bf16[64,8,1024]{2,1,0:T(8,128)(2,1)S(1)} %all-to-all-done.1.recv_ref, bf16[2,32,640]{2,1,0:T(8,128)(2,1)S(1)} %collective-permute-done.1.refs_1_.refs_0_, ...), custom_call_target="tpu_custom_call" | custom-call | bytes 4000000 | tf_op jit(solution)/shard_map/combine/pallas_call | solution.py:471
  67.4 0.0 copy-start.19
  67.4 0.0 copy-start.22
  67.4 0.0 copy-start.21
  67.4 0.0 copy-start.17
  67.4 5.7 %all-to-all-start.2 = ((bf16[64,8,768]{2,1,0:T(8,128)(2,1)}), bf16[64,8,768]{2,1,0:T(8,128)(2,1)S(1)}, u32[]{:S(2)}, u32[]{:S(2)}) async-start(bf16[64,8,768]{2,1,0:T(8,128)(2,1)} %combine.1), calls=%async_computation.2 | async-start | bytes 1572864 | tf_op jit(solution)/shard_map/combine/all_to_all | solution.py:397
  73.1 0.0 copy-done.19
  73.1 0.0 copy-done.22
  73.1 0.0 copy-start.20
  73.2 0.7 copy-done.20
  73.8 0.1 reshape.137
  73.9 0.6 copy-done.23
  74.5 0.0 copy-done.21
  74.5 0.1 reshape.139
  74.6 0.6 copy-done.10
  75.2 0.1 mul.108
  75.3 0.1 broadcast_multiply_fusion
  75.3 0.2 multiply_add_fusion
  75.6 0.0 copy-start.16
  75.6 0.7 fusion.5
  76.3 0.7 copy-done.13
  77.0 0.2 multiply_reduce_fusion
  77.1 0.1 multiply_convert_fusion
  77.2 0.7 convert_element_type.22
  77.9 0.6 fusion.7
  79.1 0.9 copy-done.4
  80.0 0.9 copy-done.6
  80.8 0.9 copy-done.8
  81.7 0.9 copy-done.15
  82.6 1.9 %inner.1 = (f32[256,512]{1,0:T(8,128)S(1)}, f32[256,512]{1,0:T(8,128)S(1)}, bf16[256,384]{1,0:T(8,128)(2,1)S(1)}) custom-call(s32[1]{0:T(128)} %bitcast.3.me_ref, f32[8,128]{1,0:T(8,128)S(1)} %copy-done.11, f32[1,8]{1,0:T(1,128)S(1)} %bitcast.21, bf16[256,768]{1,0:T(8,128)(2,1)S(1)} %bitcast.19, bf16[2,32,640]{2,1,0:T(8,128)(2,1)S(1)} %copy-done.15, ...), custom_call_target="tpu_custom_call" | custom-call | flops 400000000 | bytes 1500000 | tf_op jit(solution)/shard_map/inner/pallas_call | solution.py:487
  84.5 13.3 %all-to-all-done.2 = bf16[64,8,768]{2,1,0:T(8,128)(2,1)S(1)} async-done(((bf16[64,8,768]{2,1,0:T(8,128)(2,1)}), bf16[64,8,768]{2,1,0:T(8,128)(2,1)S(1)}, u32[]{:S(2)}, u32[]{:S(2)}) %all-to-all-start.2) | async-done | bytes 786464 | tf_op jit(solution)/shard_map/combine/all_to_all | solution.py:397
  97.8 1.3 %outputs.1 = (bf16[256,512]{1,0:T(8,128)(2,1)}, f32[4,512,128]{2,1,0:T(8,128)}) custom-call(s32[1]{0:T(128)} %bitcast.missing_ref, f32[4,512,128]{2,1,0:T(8,128)S(1)} %bitcast.16, f32[1,512]{1,0:T(1,128)S(1)} %bitcast.20, f32[256,512]{1,0:T(8,128)S(1)} %get-tuple-element.25.base_ref, f32[256,512]{1,0:T(8,128)S(1)} %get-tuple-element.26.factor_ref, ...), custom_call_target="tpu_custom_call" | custom-call | flops 200000000 | bytes 4000000 | tf_op jit(solution)/shard_map/outputs/pallas_call | solution.py:507
  (21 shorter events, 0.1 us)
Async XLA Ops:
  0.6 74.9 %copy-start = (bf16[2,128]{1,0:T(2,128)(2,1)S(1)}, bf16[2,128]{1,0:T(2,128)(2,1)}, u32[]{:S(2)}) copy-start(bf16[2,128]{1,0:T(2,128)(2,1)} %param.30) | copy-start | bytes 1540
  0.6 6.9 %copy-start.1 = (f32[4,8,64,128]{3,2,1,0:T(8,128)S(1)}, f32[4,8,64,128]{3,2,1,0:T(8,128)}, u32[]{:S(2)}) copy-start(f32[4,8,64,128]{3,2,1,0:T(8,128)} %param.26) | copy-start | bytes 3145732
  3.2 13.3 %all-to-all-start = ((bf16[8,32,768]{2,1,0:T(8,128)(2,1)}), bf16[8,32,768]{2,1,0:T(8,128)(2,1)S(1)}, u32[]{:S(2)}, u32[]{:S(2)}) async-start(bf16[8,32,768]{2,1,0:T(8,128)(2,1)} %get-tuple-element.18), calls=%async_computation | async-start | bytes 786432 | tf_op jit(solution)/shard_map/tokens/all_to_all | solution.py:397
  7.5 8.9 %copy-start.11 = (f32[8,128]{1,0:T(8,128)S(1)}, f32[8,128]{1,0:T(8,128)}, u32[]{:S(2)}) copy-start(f32[8,128]{1,0:T(8,128)} %get-tuple-element.17.meta_ref) | copy-start | bytes 12292
  18.4 16.7 %copy-start.2 = (bf16[32,4096]{1,0:T(8,128)(2,1)S(1)}, bf16[32,4096]{1,0:T(8,128)(2,1)}, u32[]{:S(2)}) copy-start(bf16[32,4096]{1,0:T(8,128)(2,1)} %z_ref.1) | copy-start | bytes 786436
  18.4 16.7 %copy-start.9 = (bf16[32,1024]{1,0:T(8,128)(2,1)S(1)}, bf16[32,1024]{1,0:T(8,128)(2,1)}, u32[]{:S(2)}) copy-start(bf16[32,1024]{1,0:T(8,128)(2,1)} %c_ref.1) | copy-start | bytes 196612
  18.4 46.9 %all-to-all-start.1 = ((bf16[64,8,1024]{2,1,0:T(8,128)(2,1)}), bf16[64,8,1024]{2,1,0:T(8,128)(2,1)S(1)}, u32[]{:S(2)}, u32[]{:S(2)}) async-start(bf16[64,8,1024]{2,1,0:T(8,128)(2,1)} %bitcast.7), calls=%async_computation.1 | async-start | bytes 2097152 | tf_op jit(solution)/shard_map/local/all_to_all | solution.py:397
  35.1 1.9 %copy-start.18 = (s32[192]{0:T(256)S(1)}, s32[192]{0:T(256)}, u32[]{:S(2)}) copy-start(s32[192]{0:T(256)} %param.25) | copy-start | bytes 2308
  35.2 3.3 %collective-permute-start = (bf16[4,32,640]{2,1,0:T(8,128)(2,1)S(1)}, bf16[4,32,640]{2,1,0:T(8,128)(2,1)S(1)}, u32[]{:S(2)}, u32[]{:S(2)}) collective-permute-start(bf16[4,32,640]{2,1,0:T(8,128)(2,1)S(1)} %get-tuple-element.20), channel_id=1, source_target_pairs={{0,1},{1,0},{2,3},{3,2},{4,5},{5,4},{6,7},{7,6},{8,9},{9,8},{10,11... | collective-permute-start | bytes 491528 | tf_op jit(solution)/shard_map/gates/ppermute | solution.py:131
  38.5 0.6 copy-start.14
  39.1 10.5 %collective-permute-start.1 = (bf16[2,32,640]{2,1,0:T(8,128)(2,1)S(1)}, bf16[2,32,640]{2,1,0:T(8,128)(2,1)S(1)}, u32[]{:S(2)}, u32[]{:S(2)}) collective-permute-start(bf16[2,32,640]{2,1,0:T(8,128)(2,1)S(1)} %get-tuple-element.22), channel_id=1, source_target_pairs={{0,2},{1,3},{2,0},{3,1},{4,6},{5,7},{6,4},{7,5},{8,10},{9,11},{10,... | collective-permute-start | bytes 245768 | tf_op jit(solution)/shard_map/gates/ppermute | solution.py:141
  41.6 8.0 %collective-permute-start.2 = (bf16[2,32,640]{2,1,0:T(8,128)(2,1)S(1)}, bf16[2,32,640]{2,1,0:T(8,128)(2,1)S(1)}, u32[]{:S(2)}, u32[]{:S(2)}) collective-permute-start(bf16[2,32,640]{2,1,0:T(8,128)(2,1)S(1)} %get-tuple-element.23), channel_id=1, source_target_pairs={{0,4},{1,5},{2,6},{3,7},{4,0},{5,1},{6,2},{7,3},{8,12},{9,13},{10,... | collective-permute-start | bytes 245768 | tf_op jit(solution)/shard_map/gates/ppermute | solution.py:141
  45.6 19.8 %copy-start.12 = (s32[192]{0:T(256)S(1)}, s32[192]{0:T(256)}, u32[]{:S(2)}) copy-start(s32[192]{0:T(256)} %hit_ref.1) | copy-start | bytes 2308
  45.6 7.5 %collective-permute-start.3 = (bf16[2,32,640]{2,1,0:T(8,128)(2,1)S(1)}, bf16[2,32,640]{2,1,0:T(8,128)(2,1)S(1)}, u32[]{:S(2)}, u32[]{:S(2)}) collective-permute-start(bf16[2,32,640]{2,1,0:T(8,128)(2,1)S(1)} %get-tuple-element.24), channel_id=1, source_target_pairs={{0,6},{1,7},{2,4},{3,5},{4,2},{5,3},{6,0},{7,1},{8,14},{9,15},{10,... | collective-permute-start | bytes 245768 | tf_op jit(solution)/shard_map/gates/ppermute | solution.py:141
  49.6 17.8 %copy-start.3 = (bf16[2,32,640]{2,1,0:T(8,128)(2,1)}, bf16[2,32,640]{2,1,0:T(8,128)(2,1)S(1)}, u32[]{:S(2)}) copy-start(bf16[2,32,640]{2,1,0:T(8,128)(2,1)S(1)} %collective-permute-done.1.refs_1_.refs_0_) | copy-start | bytes 245764
  49.6 17.8 %copy-start.5 = (bf16[2,32,640]{2,1,0:T(8,128)(2,1)}, bf16[2,32,640]{2,1,0:T(8,128)(2,1)S(1)}, u32[]{:S(2)}) copy-start(bf16[2,32,640]{2,1,0:T(8,128)(2,1)S(1)} %collective-permute-done.2.refs_2_.refs_1_) | copy-start | bytes 245764
  53.1 14.3 %copy-start.7 = (bf16[2,32,640]{2,1,0:T(8,128)(2,1)}, bf16[2,32,640]{2,1,0:T(8,128)(2,1)S(1)}, u32[]{:S(2)}) copy-start(bf16[2,32,640]{2,1,0:T(8,128)(2,1)S(1)} %collective-permute-done.3.refs_3_.refs_2_) | copy-start | bytes 245764
  67.4 5.7 %copy-start.19 = (f32[8]{0:T(128)S(1)}, f32[8]{0:T(128)}, u32[]{:S(2)}) copy-start(f32[8]{0:T(128)} %param.33) | copy-start | bytes 100
  67.4 5.7 %copy-start.22 = (bf16[2,8]{1,0:T(2,128)(2,1)S(1)}, bf16[2,8]{1,0:T(2,128)(2,1)}, u32[]{:S(2)}) copy-start(bf16[2,8]{1,0:T(2,128)(2,1)} %param.31) | copy-start | bytes 100
  67.4 7.1 %copy-start.21 = (bf16[2,512]{1,0:T(2,128)(2,1)S(1)}, bf16[2,512]{1,0:T(2,128)(2,1)}, u32[]{:S(2)}) copy-start(bf16[2,512]{1,0:T(2,128)(2,1)} %param.28) | copy-start | bytes 6148
  67.4 7.9 %copy-start.17 = (f32[2,8,64,128]{3,2,1,0:T(8,128)S(1)}, f32[2,8,64,128]{3,2,1,0:T(8,128)}, u32[]{:S(2)}) copy-start(f32[2,8,64,128]{3,2,1,0:T(8,128)} %param.32) | copy-start | bytes 1572868
  67.4 30.4 %all-to-all-start.2 = ((bf16[64,8,768]{2,1,0:T(8,128)(2,1)}), bf16[64,8,768]{2,1,0:T(8,128)(2,1)S(1)}, u32[]{:S(2)}, u32[]{:S(2)}) async-start(bf16[64,8,768]{2,1,0:T(8,128)(2,1)} %combine.1), calls=%async_computation.2 | async-start | bytes 1572864 | tf_op jit(solution)/shard_map/combine/all_to_all | solution.py:397
  73.1 0.7 copy-start.20
  73.8 0.7 copy-start.23
  74.5 0.7 copy-start.10
  75.6 3.5 %copy-start.16 = (f32[2,8,64,128]{3,2,1,0:T(8,128)}, f32[2,8,64,128]{3,2,1,0:T(8,128)S(1)}, u32[]{:S(2)}) copy-start(f32[2,8,64,128]{3,2,1,0:T(8,128)S(1)} %multiply_add_fusion) | copy-start | bytes 1572868
  76.3 0.7 copy-start.13
  79.1 0.9 copy-start.4
  80.0 0.9 copy-start.6
  80.8 0.9 copy-start.8
  81.7 0.9 copy-start.15

commit v8 on v7

--- a/solution.py
+++ b/solution.py
@@ -67,8 +67,7 @@
 
 
 def pack_first(
-    x_ref, b_ref, dt_ref, rate_ref, len_ref, out_ref, meta_ref,
-    xs, bs, steps, rates, lens, made, sems, out_sems,
+    x_ref, b_ref, dt_ref, rate_ref, len_ref, out_ref, meta_ref, xs, bs, steps, rates, lens, sems
 ):
     count = out_ref.shape[0]
     heads_dev = dt_ref.shape[1] // count
@@ -76,34 +75,24 @@
     copies = [
         pltpu.make_async_copy(src, dst, sems.at[i])
         for i, (src, dst) in enumerate(
-            ((dt_ref, steps), (b_ref, bs), (x_ref, xs), (rate_ref, rates), (len_ref, lens))
+            ((x_ref, xs), (b_ref, bs), (dt_ref, steps), (rate_ref, rates), (len_ref, lens))
         )
     ]
     for copy in copies:
         copy.start()
-    copies[0].wait()
+    for copy in copies:
+        copy.wait()
     raw = steps[...].astype(f32)
     raw = jnp.concatenate([raw, jnp.zeros((raw.shape[0], STATE - raw.shape[1]), f32)], axis=1)
     for d in range(count):
+        out_ref[d, :, 0:width] = xs[:, d * width : (d + 1) * width]
+        out_ref[d, :, width : width + STATE] = bs[:, d * STATE : (d + 1) * STATE]
         mine = raw if d == 0 else pltpu.roll(raw, STATE - d * heads_dev, 1)
-        made[d, :, width + STATE : width + 2 * STATE] = mine.astype(bf16)
-    copies[1].wait()
-    for d in range(count):
-        made[d, :, width : width + STATE] = bs[:, d * STATE : (d + 1) * STATE]
-    copies[2].wait()
-    leaving = []
-    for d in range(count):
-        made[d, :, 0:width] = xs[:, d * width : (d + 1) * width]
-        leaving.append(pltpu.make_async_copy(made.at[d], out_ref.at[d], out_sems.at[d]))
-        leaving[-1].start()
-    copies[3].wait()
-    copies[4].wait()
+        out_ref[d, :, width + STATE : width + 2 * STATE] = mine.astype(bf16)
     meta_ref[...] = jnp.zeros_like(meta_ref)
     meta_ref[0:1, 0 : rates.shape[1]] = rates[...]
     meta_ref[1:2, 0:1] = lens[:, 0:1].astype(f32)
     meta_ref[2:3, 0:1] = (lens[:, 0:1] + lens[:, 1:2]).astype(f32)
-    for copy in leaving:
-        copy.wait()
 
 
 def pack_gates(me_ref, after_ref, z_ref, c_ref, keep_ref, give_ref):
@@ -405,16 +394,14 @@
                 shape((8, STATE), f32),
             ),
             in_specs=[HBM] * 5,
-            out_specs=(HBM, VMEM),
+            out_specs=(VMEM, VMEM),
             scratch_shapes=[
                 pltpu.VMEM(pre_x.shape, bf16),
                 pltpu.VMEM(pre_b.shape, bf16),
                 pltpu.VMEM(pre_dt.shape, bf16),
                 pltpu.VMEM((1, heads), f32),
                 pltpu.VMEM(suffix_lengths.shape, jnp.int32),
-                pltpu.VMEM((n_head, rows, width + 2 * STATE), bf16),
                 pltpu.SemaphoreType.DMA((5,)),
-                pltpu.SemaphoreType.DMA((n_head,)),
             ],
             compiler_params=params(56),
             cost_estimate=cost(0, 800_000),

time: 99.9 us -> 99.3 us (level)
  no operation moved by 1% of the time
where the time goes in v8:
time: 99.3 us; the launch traced here: 98.5 us
  starting transfers between devices  38.9 us (39%)
  waiting for transfers between devices  38.3 us (39%)
  Pallas kernels  9.97 us (10%)
  local copies, waits for them, and re-layouts  7.7 us (8%)
  between operations  1.55 us (2%)
  other arithmetic  1.38 us (1%)
    all_to_all x3, waiting for transfers between devices, swap(): return lax.all_to_all(value, axis, split_axis=0, concat_axis=0, tiled=True)  33.6 us
    all_to_all x3, starting transfers between devices, swap(): return lax.all_to_all(value, axis, split_axis=0, concat_axis=0, tiled=True)  26.6 us
    ppermute x3, starting transfers between devices, exchange(): lax.ppermute(pairs[k], 'head', [(i, i ^ 2 * k) for i in range(n_head)])  10.4 us
    unnamed x48, local copies, waits for them, and re-layouts  6.8 us
    ppermute x3, waiting for transfers between devices, exchange(): lax.ppermute(pairs[k], 'head', [(i, i ^ 2 * k) for i in range(n_head)])  3.51 us
    pallas_call x1, Pallas kernels, local(): pl.pallas_call(combine, out_shape=shape((n_serve, ROWS, 2 * REQS * STATE)...  1.99 us
  transfers between devices with their start and end apart: 7, of which 5 were waited for; matrix products, arithmetic and copies ran while one was open for 3% of the time, Pallas kernels for 3%

profile of v8, /device:TPU:16, one launch (start us, length us, event | category | flops | bytes accessed | tf_op | source)
XLA Modules:
  0.0 98.5 jit_solution(16894558124311617709)
XLA Ops:
  0.6 0.0 copy-start
  0.6 0.0 copy-start.1
  0.7 1.9 %tokens.1 = (bf16[8,32,768]{2,1,0:T(8,128)(2,1)}, f32[8,128]{1,0:T(8,128)}) custom-call(bf16[32,4096]{1,0:T(8,128)(2,1)} %x_ref.1, bf16[32,1024]{1,0:T(8,128)(2,1)} %b_ref.1, bf16[32,64]{1,0:T(8,128)(2,1)} %dt_ref.1, f32[1,8]{1,0:T(1,128)} %bitcast.23, s32[1,3]{1,0:T(1,128)} %len_ref.1), custom_call_target="tpu_custom_call" | custom-call | bytes 800000 | tf_op jit(solution)/shard_map/tokens/pallas_call | solution.py:390
  2.6 4.3 %all-to-all-start = ((bf16[8,32,768]{2,1,0:T(8,128)(2,1)}), bf16[8,32,768]{2,1,0:T(8,128)(2,1)S(1)}, u32[]{:S(2)}, u32[]{:S(2)}) async-start(bf16[8,32,768]{2,1,0:T(8,128)(2,1)} %get-tuple-element.18), calls=%async_computation | async-start | bytes 786432 | tf_op jit(solution)/shard_map/tokens/all_to_all | solution.py:386
  6.9 0.0 copy-done.1
  6.9 0.0 copy-start.11
  6.9 0.9 cache.1.send_ref
  7.8 8.1 %all-to-all-done = bf16[8,32,768]{2,1,0:T(8,128)(2,1)S(1)} async-done(((bf16[8,32,768]{2,1,0:T(8,128)(2,1)}), bf16[8,32,768]{2,1,0:T(8,128)(2,1)S(1)}, u32[]{:S(2)}, u32[]{:S(2)}) %all-to-all-start) | async-done | bytes 393248 | tf_op jit(solution)/shard_map/tokens/all_to_all | solution.py:386
  15.8 0.0 copy-done.11
  15.8 2.0 %local.1.after_ref = bf16[512,1024]{1,0:T(8,128)(2,1)} custom-call(f32[8,128]{1,0:T(8,128)S(1)} %copy-done.11, bf16[256,768]{1,0:T(8,128)(2,1)S(1)} %bitcast.18, bf16[512,1024]{1,0:T(8,128)(2,1)} %cache.1.send_ref), custom_call_target="tpu_custom_call", output_to_operand_aliasing={{}: (2, {})} | custom-call | flops 300000000 | bytes 800000 | tf_op jit(solution)/shard_map/local/pallas_call | solution.py:433
  17.8 0.0 copy-start.2
  17.8 0.0 copy-start.9
  17.8 16.6 %all-to-all-start.1 = ((bf16[64,8,1024]{2,1,0:T(8,128)(2,1)}), bf16[64,8,1024]{2,1,0:T(8,128)(2,1)S(1)}, u32[]{:S(2)}, u32[]{:S(2)}) async-start(bf16[64,8,1024]{2,1,0:T(8,128)(2,1)} %bitcast.7), calls=%async_computation.1 | async-start | bytes 2097152 | tf_op jit(solution)/shard_map/local/all_to_all | solution.py:386
  34.5 0.0 copy-done.2
  34.5 0.0 copy-done.9
  34.5 0.0 copy-start.18
  34.5 1.9 %collective-permute-start = (bf16[4,32,640]{2,1,0:T(8,128)(2,1)S(1)}, bf16[4,32,640]{2,1,0:T(8,128)(2,1)S(1)}, u32[]{:S(2)}, u32[]{:S(2)}) collective-permute-start(bf16[4,32,640]{2,1,0:T(8,128)(2,1)S(1)} %get-tuple-element.20), channel_id=1, source_target_pairs={{0,1},{1,0},{2,3},{3,2},{4,5},{5,4},{6,7},{7,6},{8,9},{9,8},{10,11... | collective-permute-start | bytes 491528 | tf_op jit(solution)/shard_map/gates/ppermute | solution.py:120
  36.5 0.0 copy-done.18
  36.5 0.2 convert_reduce_fusion
  36.7 1.2 %collective-permute-done.got_ref = bf16[4,32,640]{2,1,0:T(8,128)(2,1)S(1)} collective-permute-done((bf16[4,32,640]{2,1,0:T(8,128)(2,1)S(1)}, bf16[4,32,640]{2,1,0:T(8,128)(2,1)S(1)}, u32[]{:S(2)}, u32[]{:S(2)}) %collective-permute-start) | collective-permute-done | bytes 163872 | tf_op jit(solution)/shard_map/gates/ppermute | solution.py:120
  37.9 0.0 copy-start.14
  37.9 0.6 copy-done.14
  38.5 2.5 %collective-permute-start.1 = (bf16[2,32,640]{2,1,0:T(8,128)(2,1)S(1)}, bf16[2,32,640]{2,1,0:T(8,128)(2,1)S(1)}, u32[]{:S(2)}, u32[]{:S(2)}) collective-permute-start(bf16[2,32,640]{2,1,0:T(8,128)(2,1)S(1)} %get-tuple-element.22), channel_id=1, source_target_pairs={{0,2},{1,3},{2,0},{3,1},{4,6},{5,7},{6,4},{7,5},{8,10},{9,11},{10,... | collective-permute-start | bytes 245768 | tf_op jit(solution)/shard_map/gates/ppermute | solution.py:130
  41.0 4.0 %collective-permute-start.2 = (bf16[2,32,640]{2,1,0:T(8,128)(2,1)S(1)}, bf16[2,32,640]{2,1,0:T(8,128)(2,1)S(1)}, u32[]{:S(2)}, u32[]{:S(2)}) collective-permute-start(bf16[2,32,640]{2,1,0:T(8,128)(2,1)S(1)} %get-tuple-element.23), channel_id=1, source_target_pairs={{0,4},{1,5},{2,6},{3,7},{4,0},{5,1},{6,2},{7,3},{8,12},{9,13},{10,... | collective-permute-start | bytes 245768 | tf_op jit(solution)/shard_map/gates/ppermute | solution.py:130
  45.0 0.0 copy-start.12
  45.0 4.0 %collective-permute-start.3 = (bf16[2,32,640]{2,1,0:T(8,128)(2,1)S(1)}, bf16[2,32,640]{2,1,0:T(8,128)(2,1)S(1)}, u32[]{:S(2)}, u32[]{:S(2)}) collective-permute-start(bf16[2,32,640]{2,1,0:T(8,128)(2,1)S(1)} %get-tuple-element.24), channel_id=1, source_target_pairs={{0,6},{1,7},{2,4},{3,5},{4,2},{5,3},{6,0},{7,1},{8,14},{9,15},{10,... | collective-permute-start | bytes 245768 | tf_op jit(solution)/shard_map/gates/ppermute | solution.py:130
  49.0 0.0 collective-permute-done.1.refs_1_.refs_0_
  49.0 0.0 copy-start.3
  49.0 0.0 collective-permute-done.2.refs_2_.refs_1_
  49.0 0.0 copy-start.5
  49.0 3.5 %collective-permute-done.3.refs_3_.refs_2_ = bf16[2,32,640]{2,1,0:T(8,128)(2,1)S(1)} collective-permute-done((bf16[2,32,640]{2,1,0:T(8,128)(2,1)S(1)}, bf16[2,32,640]{2,1,0:T(8,128)(2,1)S(1)}, u32[]{:S(2)}, u32[]{:S(2)}) %collective-permute-start.3) | collective-permute-done | bytes 81952 | tf_op jit(solution)/shard_map/gates/ppermute | solution.py:130
  52.5 12.2 %all-to-all-done.1.recv_ref = bf16[64,8,1024]{2,1,0:T(8,128)(2,1)S(1)} async-done(((bf16[64,8,1024]{2,1,0:T(8,128)(2,1)}), bf16[64,8,1024]{2,1,0:T(8,128)(2,1)S(1)}, u32[]{:S(2)}, u32[]{:S(2)}) %all-to-all-start.1) | async-done | bytes 1048608 | tf_op jit(solution)/shard_map/local/all_to_all | solution.py:386
  64.8 2.0 %combine.1 = bf16[64,8,768]{2,1,0:T(8,128)(2,1)} custom-call(s32[192]{0:T(256)S(1)} %copy-done.12, s32[192]{0:T(256)S(1)} %fusion.4.place_ref, bf16[64,8,1024]{2,1,0:T(8,128)(2,1)S(1)} %all-to-all-done.1.recv_ref, bf16[2,32,640]{2,1,0:T(8,128)(2,1)S(1)} %collective-permute-done.1.refs_1_.refs_0_, ...), custom_call_target="tpu_custom_call" | custom-call | bytes 4000000 | tf_op jit(solution)/shard_map/combine/pallas_call | solution.py:458
  66.8 0.0 copy-start.19
  66.8 0.0 copy-start.22
  66.8 0.0 copy-start.21
  66.8 0.0 copy-start.17
  66.8 5.7 %all-to-all-start.2 = ((bf16[64,8,768]{2,1,0:T(8,128)(2,1)}), bf16[64,8,768]{2,1,0:T(8,128)(2,1)S(1)}, u32[]{:S(2)}, u32[]{:S(2)}) async-start(bf16[64,8,768]{2,1,0:T(8,128)(2,1)} %combine.1), calls=%async_computation.2 | async-start | bytes 1572864 | tf_op jit(solution)/shard_map/combine/all_to_all | solution.py:386
  72.5 0.0 copy-done.19
  72.5 0.0 copy-done.22
  72.5 0.0 copy-start.20
  72.5 0.7 copy-done.20
  73.2 0.1 reshape.137
  73.3 0.6 copy-done.23
  73.9 0.1 reshape.139
  74.0 0.6 copy-done.10
  74.6 0.1 mul.108
  74.6 0.1 broadcast_multiply_fusion
  74.7 0.0 copy-done.17
  74.7 0.2 multiply_add_fusion
  75.0 0.0 copy-start.16
  75.0 0.7 fusion.5
  75.7 0.7 copy-done.13
  76.4 0.2 multiply_reduce_fusion
  76.5 0.1 multiply_convert_fusion
  76.6 0.7 convert_element_type.22
  77.3 0.6 fusion.7
  78.5 0.9 copy-done.4
  79.4 0.9 copy-done.6
  80.2 0.9 copy-done.8
  81.1 0.9 copy-done.15
  82.0 1.9 %inner.1 = (f32[256,512]{1,0:T(8,128)S(1)}, f32[256,512]{1,0:T(8,128)S(1)}, bf16[256,384]{1,0:T(8,128)(2,1)S(1)}) custom-call(s32[1]{0:T(128)} %bitcast.3.me_ref, f32[8,128]{1,0:T(8,128)S(1)} %copy-done.11, f32[1,8]{1,0:T(1,128)S(1)} %bitcast.21, bf16[256,768]{1,0:T(8,128)(2,1)S(1)} %bitcast.19, bf16[2,32,640]{2,1,0:T(8,128)(2,1)S(1)} %copy-done.15, ...), custom_call_target="tpu_custom_call" | custom-call | flops 400000000 | bytes 1500000 | tf_op jit(solution)/shard_map/inner/pallas_call | solution.py:474
  83.9 13.3 %all-to-all-done.2 = bf16[64,8,768]{2,1,0:T(8,128)(2,1)S(1)} async-done(((bf16[64,8,768]{2,1,0:T(8,128)(2,1)}), bf16[64,8,768]{2,1,0:T(8,128)(2,1)S(1)}, u32[]{:S(2)}, u32[]{:S(2)}) %all-to-all-start.2) | async-done | bytes 786464 | tf_op jit(solution)/shard_map/combine/all_to_all | solution.py:386
  97.2 1.3 %outputs.1 = (bf16[256,512]{1,0:T(8,128)(2,1)}, f32[4,512,128]{2,1,0:T(8,128)}) custom-call(s32[1]{0:T(128)} %bitcast.missing_ref, f32[4,512,128]{2,1,0:T(8,128)S(1)} %bitcast.16, f32[1,512]{1,0:T(1,128)S(1)} %bitcast.20, f32[256,512]{1,0:T(8,128)S(1)} %get-tuple-element.25.base_ref, f32[256,512]{1,0:T(8,128)S(1)} %get-tuple-element.26.factor_ref, ...), custom_call_target="tpu_custom_call" | custom-call | flops 200000000 | bytes 4000000 | tf_op jit(solution)/shard_map/outputs/pallas_call | solution.py:494
  (21 shorter events, 0.1 us)
Async XLA Ops:
  0.6 74.3 %copy-start = (bf16[2,128]{1,0:T(2,128)(2,1)S(1)}, bf16[2,128]{1,0:T(2,128)(2,1)}, u32[]{:S(2)}) copy-start(bf16[2,128]{1,0:T(2,128)(2,1)} %param.30) | copy-start | bytes 1540
  0.6 6.3 %copy-start.1 = (f32[4,8,64,128]{3,2,1,0:T(8,128)S(1)}, f32[4,8,64,128]{3,2,1,0:T(8,128)}, u32[]{:S(2)}) copy-start(f32[4,8,64,128]{3,2,1,0:T(8,128)} %param.26) | copy-start | bytes 3145732
  2.6 13.3 %all-to-all-start = ((bf16[8,32,768]{2,1,0:T(8,128)(2,1)}), bf16[8,32,768]{2,1,0:T(8,128)(2,1)S(1)}, u32[]{:S(2)}, u32[]{:S(2)}) async-start(bf16[8,32,768]{2,1,0:T(8,128)(2,1)} %get-tuple-element.18), calls=%async_computation | async-start | bytes 786432 | tf_op jit(solution)/shard_map/tokens/all_to_all | solution.py:386
  6.9 8.9 %copy-start.11 = (f32[8,128]{1,0:T(8,128)S(1)}, f32[8,128]{1,0:T(8,128)}, u32[]{:S(2)}) copy-start(f32[8,128]{1,0:T(8,128)} %get-tuple-element.17.meta_ref) | copy-start | bytes 12292
  17.8 16.7 %copy-start.2 = (bf16[32,4096]{1,0:T(8,128)(2,1)S(1)}, bf16[32,4096]{1,0:T(8,128)(2,1)}, u32[]{:S(2)}) copy-start(bf16[32,4096]{1,0:T(8,128)(2,1)} %z_ref.1) | copy-start | bytes 786436
  17.8 16.7 %copy-start.9 = (bf16[32,1024]{1,0:T(8,128)(2,1)S(1)}, bf16[32,1024]{1,0:T(8,128)(2,1)}, u32[]{:S(2)}) copy-start(bf16[32,1024]{1,0:T(8,128)(2,1)} %c_ref.1) | copy-start | bytes 196612
  17.8 46.9 %all-to-all-start.1 = ((bf16[64,8,1024]{2,1,0:T(8,128)(2,1)}), bf16[64,8,1024]{2,1,0:T(8,128)(2,1)S(1)}, u32[]{:S(2)}, u32[]{:S(2)}) async-start(bf16[64,8,1024]{2,1,0:T(8,128)(2,1)} %bitcast.7), calls=%async_computation.1 | async-start | bytes 2097152 | tf_op jit(solution)/shard_map/local/all_to_all | solution.py:386
  34.5 1.9 %copy-start.18 = (s32[192]{0:T(256)S(1)}, s32[192]{0:T(256)}, u32[]{:S(2)}) copy-start(s32[192]{0:T(256)} %param.25) | copy-start | bytes 2308
  34.5 3.3 %collective-permute-start = (bf16[4,32,640]{2,1,0:T(8,128)(2,1)S(1)}, bf16[4,32,640]{2,1,0:T(8,128)(2,1)S(1)}, u32[]{:S(2)}, u32[]{:S(2)}) collective-permute-start(bf16[4,32,640]{2,1,0:T(8,128)(2,1)S(1)} %get-tuple-element.20), channel_id=1, source_target_pairs={{0,1},{1,0},{2,3},{3,2},{4,5},{5,4},{6,7},{7,6},{8,9},{9,8},{10,11... | collective-permute-start | bytes 491528 | tf_op jit(solution)/shard_map/gates/ppermute | solution.py:120
  37.9 0.6 copy-start.14
  38.5 10.5 %collective-permute-start.1 = (bf16[2,32,640]{2,1,0:T(8,128)(2,1)S(1)}, bf16[2,32,640]{2,1,0:T(8,128)(2,1)S(1)}, u32[]{:S(2)}, u32[]{:S(2)}) collective-permute-start(bf16[2,32,640]{2,1,0:T(8,128)(2,1)S(1)} %get-tuple-element.22), channel_id=1, source_target_pairs={{0,2},{1,3},{2,0},{3,1},{4,6},{5,7},{6,4},{7,5},{8,10},{9,11},{10,... | collective-permute-start | bytes 245768 | tf_op jit(solution)/shard_map/gates/ppermute | solution.py:130
  41.0 8.0 %collective-permute-start.2 = (bf16[2,32,640]{2,1,0:T(8,128)(2,1)S(1)}, bf16[2,32,640]{2,1,0:T(8,128)(2,1)S(1)}, u32[]{:S(2)}, u32[]{:S(2)}) collective-permute-start(bf16[2,32,640]{2,1,0:T(8,128)(2,1)S(1)} %get-tuple-element.23), channel_id=1, source_target_pairs={{0,4},{1,5},{2,6},{3,7},{4,0},{5,1},{6,2},{7,3},{8,12},{9,13},{10,... | collective-permute-start | bytes 245768 | tf_op jit(solution)/shard_map/gates/ppermute | solution.py:130
  45.0 19.8 %copy-start.12 = (s32[192]{0:T(256)S(1)}, s32[192]{0:T(256)}, u32[]{:S(2)}) copy-start(s32[192]{0:T(256)} %hit_ref.1) | copy-start | bytes 2308
  45.0 7.5 %collective-permute-start.3 = (bf16[2,32,640]{2,1,0:T(8,128)(2,1)S(1)}, bf16[2,32,640]{2,1,0:T(8,128)(2,1)S(1)}, u32[]{:S(2)}, u32[]{:S(2)}) collective-permute-start(bf16[2,32,640]{2,1,0:T(8,128)(2,1)S(1)} %get-tuple-element.24), channel_id=1, source_target_pairs={{0,6},{1,7},{2,4},{3,5},{4,2},{5,3},{6,0},{7,1},{8,14},{9,15},{10,... | collective-permute-start | bytes 245768 | tf_op jit(solution)/shard_map/gates/ppermute | solution.py:130
  49.0 17.8 %copy-start.3 = (bf16[2,32,640]{2,1,0:T(8,128)(2,1)}, bf16[2,32,640]{2,1,0:T(8,128)(2,1)S(1)}, u32[]{:S(2)}) copy-start(bf16[2,32,640]{2,1,0:T(8,128)(2,1)S(1)} %collective-permute-done.1.refs_1_.refs_0_) | copy-start | bytes 245764
  49.0 17.8 %copy-start.5 = (bf16[2,32,640]{2,1,0:T(8,128)(2,1)}, bf16[2,32,640]{2,1,0:T(8,128)(2,1)S(1)}, u32[]{:S(2)}) copy-start(bf16[2,32,640]{2,1,0:T(8,128)(2,1)S(1)} %collective-permute-done.2.refs_2_.refs_1_) | copy-start | bytes 245764
  52.5 14.3 %copy-start.7 = (bf16[2,32,640]{2,1,0:T(8,128)(2,1)}, bf16[2,32,640]{2,1,0:T(8,128)(2,1)S(1)}, u32[]{:S(2)}) copy-start(bf16[2,32,640]{2,1,0:T(8,128)(2,1)S(1)} %collective-permute-done.3.refs_3_.refs_2_) | copy-start | bytes 245764
  66.8 5.7 %copy-start.19 = (f32[8]{0:T(128)S(1)}, f32[8]{0:T(128)}, u32[]{:S(2)}) copy-start(f32[8]{0:T(128)} %param.33) | copy-start | bytes 100
  66.8 5.7 %copy-start.22 = (bf16[2,8]{1,0:T(2,128)(2,1)S(1)}, bf16[2,8]{1,0:T(2,128)(2,1)}, u32[]{:S(2)}) copy-start(bf16[2,8]{1,0:T(2,128)(2,1)} %param.31) | copy-start | bytes 100
  66.8 7.1 %copy-start.21 = (bf16[2,512]{1,0:T(2,128)(2,1)S(1)}, bf16[2,512]{1,0:T(2,128)(2,1)}, u32[]{:S(2)}) copy-start(bf16[2,512]{1,0:T(2,128)(2,1)} %param.28) | copy-start | bytes 6148
  66.8 7.9 %copy-start.17 = (f32[2,8,64,128]{3,2,1,0:T(8,128)S(1)}, f32[2,8,64,128]{3,2,1,0:T(8,128)}, u32[]{:S(2)}) copy-start(f32[2,8,64,128]{3,2,1,0:T(8,128)} %param.32) | copy-start | bytes 1572868
  66.8 30.4 %all-to-all-start.2 = ((bf16[64,8,768]{2,1,0:T(8,128)(2,1)}), bf16[64,8,768]{2,1,0:T(8,128)(2,1)S(1)}, u32[]{:S(2)}, u32[]{:S(2)}) async-start(bf16[64,8,768]{2,1,0:T(8,128)(2,1)} %combine.1), calls=%async_computation.2 | async-start | bytes 1572864 | tf_op jit(solution)/shard_map/combine/all_to_all | solution.py:386
  72.5 0.7 copy-start.20
  73.2 0.7 copy-start.23
  73.9 0.7 copy-start.10
  75.0 3.5 %copy-start.16 = (f32[2,8,64,128]{3,2,1,0:T(8,128)}, f32[2,8,64,128]{3,2,1,0:T(8,128)S(1)}, u32[]{:S(2)}) copy-start(f32[2,8,64,128]{3,2,1,0:T(8,128)S(1)} %multiply_add_fusion) | copy-start | bytes 1572868
  75.7 0.7 copy-start.13
  78.5 0.9 copy-start.4
  79.4 0.9 copy-start.6
  80.2 0.9 copy-start.8
  81.1 0.9 copy-start.15
